TPU v7x, 32 devices: a whole 2x2x4 slice. The times are simulated.
32 devices in a mesh: wide: 4 (over y, x), narrow: 8 (over z, core).
Axes of the slice: x: 2, y: 2, z: 4, core: 2. Of those that a mesh axis runs over, the one named last changes fastest.
Arguments:
- coeff: bfloat16 [4096, 2048], P('wide', 'narrow'), may hold values from -6 to 6
- groupb_row_energy: float32 [4096], P('wide'), may hold values from 0.2 to 2
- groupa_energy: float32 [2048], P('narrow'), may hold values from 0.2 to 2
- groupb_basis_values: bfloat16 [4, 1024, 64], replicated, may hold values from -0.1875 to 0.1875
- basis_a: bfloat16 [2048, 2048], replicated, may hold values from -0.125 to 0.125
- potential: float32 [1024, 2048], P(('wide', 'narrow')), may hold values from 0.1 to 3
- slot_sparse_level: int32 [64], P('wide'), may hold values from 0 to 3
- block_pad: int32 [64], P('wide'), may hold values from 0 to 64, as said below
- slot_grid_offset: int32 [64], P('wide'), may hold values from 0 to 1023
Outputs:
- product: float32 [4096, 2048], P('wide', 'narrow')
Inputs may be any that keep to these rules, and one draw needn't show every extreme that they name: `block_pad`: A value of 64 marks an empty slot; one index of wide has all 16 slots filled and another only its first.
All inputs are finite; a program needn't handle non-finite values.
Results may differ from a plain program's by a relative error of at most 0.0023.
Values may be sent and summed in bfloat16 or wider, within the bound.
No kernel may reach another device: no remote copies, remote signals or barrier semaphores. Data moves between devices by JAX's collectives and lax.ppermute only.
A program may use at most 128 MiB of HBM per device.

v0:
```python
import functools

import jax
import jax.numpy as jnp
from jax import lax
from jax.experimental import pallas as pl
from jax.experimental.pallas import tpu as pltpu
from jax.sharding import PartitionSpec as P

MIB = 1024 * 1024
HBM = pl.BlockSpec(memory_space=pltpu.HBM)
VMEM = pl.BlockSpec(memory_space=pltpu.VMEM)
BF16 = jnp.bfloat16
F32 = jnp.float32
LONG = 8


def call(kernel, name, out_shape, in_specs, out_specs, scratch=(), flops=0, moved=0, mib=16):
    return pl.pallas_call(
        kernel,
        out_shape=out_shape,
        in_specs=in_specs,
        out_specs=out_specs,
        scratch_shapes=scratch,
        compiler_params=pltpu.CompilerParams(vmem_limit_bytes=mib * MIB),
        cost_estimate=pl.CostEstimate(flops=flops, bytes_accessed=moved, transcendentals=0),
        name=name,
    )


def in_hbm(value):
    return pltpu.with_memory_space_constraint(value, pltpu.HBM)


def array(shape, dtype):
    return jax.ShapeDtypeStruct(shape, dtype)


def dot(left, right):
    return jnp.dot(left, right, preferred_element_type=F32)


def dot_turned(left, right):
    return lax.dot_general(left, right, (((1,), (1,)), ((), ())), preferred_element_type=F32)


def chunk_of(turned_ref, rolled_ref, wide, k):
    own = rolled_ref.shape[1] // wide
    start = pl.multiple_of((lax.axis_index("wide") ^ k) * own, own)
    return dot(turned_ref[...], rolled_ref[:, pl.ds(start, own)])


def store_halves(chips, total, far_ref, near_ref):
    upper = lax.axis_index("narrow") // 2 >= chips // 2
    rows = far_ref.shape[0]
    turned = total.astype(BF16).T.astype(F32)
    low, high = turned[:rows], turned[rows:]
    far_ref[...] = jnp.where(upper, low, high).astype(BF16)
    near_ref[...] = jnp.where(upper, high, low).astype(BF16)


def start_pieces(source, target, rows, sem):
    for r in range(0, source.shape[0], rows):
        span = pl.ds(r, rows)
        pltpu.make_async_copy(source.at[span], target.at[span], sem).start()


def wait_all(source, target, sem):
    pltpu.make_async_copy(source, target, sem).wait()


def basis_pieces(basis_hbm, basis_ref):
    chips, columns, _ = basis_ref.shape
    place = lax.axis_index("narrow")
    core, chip = place % 2, place // 2
    pairs = []
    for j in range(chips):
        start = pl.multiple_of(((chip ^ j) * 2 + core) * columns, columns)
        pairs.append((basis_hbm.at[pl.ds(start, columns)], basis_ref.at[j]))
    return pairs


def halves(rows, columns):
    return (array((rows // 2, columns), BF16),) * 2


def first_kernel(
    wide,
    chips,
    level_hbm,
    pad_hbm,
    shift_hbm,
    coeff_hbm,
    table_hbm,
    basis_hbm,
    potential_hbm,
    out_ref,
    turned_ref,
    rolled_ref,
    basis_ref,
    potential_ref,
    level_ref,
    pad_ref,
    shift_ref,
    coeff_ref,
    table_ref,
    sems,
):
    slots = pad_ref.shape[0]
    levels, width, points = table_ref.shape
    small = [
        pltpu.make_async_copy(source, target, sems.at[i])
        for i, (source, target) in enumerate(
            ((level_hbm, level_ref), (shift_hbm, shift_ref), (pad_hbm, pad_ref))
        )
    ]
    for copy in small:
        copy.start()
    for n in range(levels):
        start_pieces(table_hbm.at[n], table_ref.at[n], 32, sems.at[3])
    start_pieces(coeff_hbm, coeff_ref, 128, sems.at[4])
    pairs = basis_pieces(basis_hbm, basis_ref)
    for j, (source, target) in enumerate(pairs):
        start_pieces(source, target, 64, sems.at[6 + j])
    start_pieces(potential_hbm, potential_ref, 8, sems.at[5])
    for copy in small:
        copy.wait()
    wait_all(table_hbm, table_ref, sems.at[3])
    row = lax.broadcasted_iota(jnp.int32, (width, 128), 0)
    for s in range(slots):
        rows = slice(s * width, (s + 1) * width)
        live = jnp.where(row < width - pad_ref[s], 1.0, 0.0).astype(BF16)
        rolled = pltpu.roll(table_ref[level_ref[s]], shift_ref[s], 1)
        for p in range(0, points, 128):
            rolled_ref[rows, p : p + 128] = rolled[:, p : p + 128] * live
    wait_all(coeff_hbm, coeff_ref, sems.at[4])
    turned_ref[...] = coeff_ref[...].T
    out_ref[...] = chunk_of(turned_ref, rolled_ref, wide, wide - 1).astype(BF16).T
    for j, (source, target) in enumerate(pairs):
        wait_all(source, target, sems.at[6 + j])
    wait_all(potential_hbm, potential_ref, sems.at[5])


def first(wide, chips, level, pad, shift, coeff, tables, basis, potential):
    rows, columns = coeff.shape
    points = tables.shape[2]
    slots = pad.shape[0]
    inputs = (level, pad, shift, coeff, tables, basis, potential)
    return call(
        functools.partial(first_kernel, wide, chips),
        "forward_first",
        (
            array((points // wide, columns), BF16),
            array((columns, rows), BF16),
            array((rows, points), BF16),
            array((chips, columns, basis.shape[1]), BF16),
            array(potential.shape, F32),
        ),
        [HBM] * 7,
        (VMEM,) * 5,
        [
            pltpu.SMEM((slots,), jnp.int32),
            pltpu.SMEM((slots,), jnp.int32),
            pltpu.SMEM((slots,), jnp.int32),
            pltpu.VMEM(coeff.shape, coeff.dtype),
            pltpu.VMEM(tables.shape, tables.dtype),
            pltpu.SemaphoreType.DMA((6 + chips,)),
        ],
        flops=2 * rows * points // wide * columns,
        moved=4 * MIB,
    )(*(in_hbm(value) for value in inputs))


def chunk_kernel(wide, chips, k, turned_ref, rolled_ref, far_ref, near_ref):
    store_halves(chips, chunk_of(turned_ref, rolled_ref, wide, k), far_ref, near_ref)


def chunk(wide, chips, k, turned, rolled):
    columns, rows = turned.shape
    own = rolled.shape[1] // wide
    return call(
        functools.partial(chunk_kernel, wide, chips, k),
        "forward_chunk",
        halves(own, columns),
        [VMEM] * 2,
        (VMEM,) * 2,
        flops=2 * rows * own * columns * LONG,
        moved=MIB * LONG,
    )(turned, rolled)


def last_kernel(wide, turned_ref, rolled_ref, out_ref):
    out_ref[...] = chunk_of(turned_ref, rolled_ref, wide, 0).T


def last(wide, turned, rolled):
    columns, rows = turned.shape
    own = rolled.shape[1] // wide
    return call(
        functools.partial(last_kernel, wide),
        "forward_own",
        array((own, columns), F32),
        [VMEM] * 2,
        VMEM,
        flops=2 * rows * own * columns,
        moved=MIB,
    )(turned, rolled)


def combine_kernel(chips, first, mine_ref, whole_ref, *refs):
    count = chips // 2
    parts, outs = refs[:-count], refs[-count:]
    chip = lax.axis_index("narrow") // 2
    rows = outs[0].shape[0]
    for i in range(count):
        target = chip ^ (first + i)
        span = pl.ds(pl.multiple_of(target * rows, rows), rows)
        total = mine_ref[span, :] + whole_ref[span, :].astype(F32)
        start = pl.multiple_of((target % count) * rows, rows)
        for part in parts:
            total = total + part[pl.ds(start, rows), :].astype(F32)
        outs[i][...] = total.astype(BF16)


def combine(chips, first, mine, whole, parts):
    rows, columns = mine.shape
    count = chips // 2
    return call(
        functools.partial(combine_kernel, chips, first),
        "wide_sum",
        (array((rows // chips, columns), BF16),) * count,
        [VMEM] * (len(parts) + 2),
        (VMEM,) * count,
        moved=MIB,
    )(mine, whole, *parts)


def own_points_kernel(x_ref, basis_ref, out_ref):
    out_ref[...] = dot(x_ref[...], basis_ref[0])


def own_points(x, where):
    basis, _ = where
    rows = x.shape[0]
    points = basis.shape[2]
    return call(
        own_points_kernel,
        "points_own",
        array((rows, points), F32),
        [VMEM] * 2,
        VMEM,
        flops=2 * rows * points * x.shape[1],
        moved=2 * MIB,
    )(x, basis)


def more_points_kernel(j, total_ref, x_ref, basis_ref, out_ref):
    out_ref[...] = total_ref[...] + dot(x_ref[...], basis_ref[j])


def more_points(total, x, where):
    basis, j = where
    rows, points = total.shape
    return call(
        functools.partial(more_points_kernel, j),
        "points_more",
        array((rows, points), F32),
        [VMEM] * 3,
        VMEM,
        flops=2 * rows * points * x.shape[1],
        moved=2 * MIB,
    )(total, x, basis)


def last_points_kernel(j, total_ref, x_ref, basis_ref, mine_ref, theirs_ref):
    core = lax.axis_index("narrow") % 2
    rows = mine_ref.shape[0]
    total = total_ref[...] + dot(x_ref[...], basis_ref[j])
    low, high = total[:rows], total[rows:]
    mine_ref[...] = jnp.where(core == 0, low, high)
    theirs_ref[...] = jnp.where(core == 0, high, low)


def last_points(total, x, where):
    basis, j = where
    rows, points = total.shape
    half = array((rows // 2, points), F32)
    return call(
        functools.partial(last_points_kernel, j),
        "points_last",
        (half, half),
        [VMEM] * 3,
        (VMEM, VMEM),
        flops=2 * rows * points * x.shape[1],
        moved=2 * MIB,
    )(total, x, basis)


def act_kernel(mine_ref, other_ref, potential_ref, out_ref):
    on_grid = mine_ref[...] + other_ref[...]
    out_ref[...] = (potential_ref[...] * on_grid).astype(BF16)


def act(mine, other, potential):
    return call(
        act_kernel, "act", array(mine.shape, BF16), [VMEM] * 3, VMEM, moved=MIB
    )(mine, other, potential)


def first_functions_kernel(j, mine_ref, other_ref, basis_ref, out_ref, both_ref):
    core = lax.axis_index("narrow") % 2
    rows = mine_ref.shape[0]
    mine, other = mine_ref[...].astype(F32), other_ref[...].astype(F32)
    both_ref[:rows] = jnp.where(core == 0, mine, other).astype(BF16)
    both_ref[rows:] = jnp.where(core == 0, other, mine).astype(BF16)
    out_ref[...] = dot_turned(both_ref[...], basis_ref[j]).astype(BF16)


def first_functions(mine, other, where):
    basis, j = where
    rows, points = mine.shape
    columns = basis.shape[1]
    return call(
        functools.partial(first_functions_kernel, j),
        "functions_first",
        (array((2 * rows, columns), BF16), array((2 * rows, points), BF16)),
        [VMEM] * 3,
        (VMEM, VMEM),
        flops=4 * rows * points * columns,
        moved=2 * MIB,
    )(mine, other, basis)


def functions_kernel(j, both_ref, basis_ref, out_ref):
    out_ref[...] = dot_turned(both_ref[...], basis_ref[j]).astype(BF16)


def functions(both, where):
    basis, j = where
    rows, points = both.shape
    columns = basis.shape[1]
    return call(
        functools.partial(functions_kernel, j),
        "functions_more",
        array((rows, columns), BF16),
        [VMEM] * 2,
        VMEM,
        flops=2 * rows * points * columns,
        moved=2 * MIB,
    )(both, basis)


def assemble_kernel(*refs):
    parts, out_ref = refs[:-1], refs[-1]
    chip = lax.axis_index("narrow") // 2
    rows = parts[0].shape[0]
    for j, part in enumerate(parts):
        start = pl.multiple_of((chip ^ j) * rows, rows)
        out_ref[pl.ds(start, rows), :] = part[...]


def assemble(parts):
    rows, columns = parts[0].shape
    chips = len(parts)
    return call(
        assemble_kernel,
        "assemble",
        array((rows * chips, columns), BF16),
        [VMEM] * chips,
        VMEM,
        moved=MIB // 4,
    )(*parts)


def own_kernel(wide, pad_ref, rolled_ref, grid_ref, coeff_ref, row_ref, column_ref, out_ref):
    slots = pad_ref.shape[0]
    width = rolled_ref.shape[0] // slots
    me = lax.axis_index("wide")
    own = rolled_ref.shape[1] // wide
    start = pl.multiple_of(me * own, own)
    out_ref[...] = dot(rolled_ref[:, pl.ds(start, own)], grid_ref[...])
    row = lax.broadcasted_iota(jnp.int32, (width, out_ref.shape[1]), 0)
    for s in range(slots):
        rows = slice(s * width, (s + 1) * width)
        energy = row_ref[rows, :] + column_ref[...]
        diagonal = energy * coeff_ref[rows, :].astype(F32)
        out_ref[rows, :] += jnp.where(row < width - pad_ref[s], diagonal, 0.0)


def backward_own(wide, pad, rolled, grid, coeff, row_energy, column_energy):
    smem = pl.BlockSpec(memory_space=pltpu.SMEM)
    rows, columns = coeff.shape
    return call(
        functools.partial(own_kernel, wide),
        "backward_own",
        array(coeff.shape, F32),
        [smem] + [VMEM] * 5,
        VMEM,
        flops=2 * rows * columns * rolled.shape[1] // wide,
        moved=4 * MIB,
    )(pad, rolled, grid, coeff, row_energy[:, None], column_energy[None, :])


def more_kernel(wide, k, total_ref, rolled_ref, grid_ref, out_ref):
    own = rolled_ref.shape[1] // wide
    start = pl.multiple_of((lax.axis_index("wide") ^ k) * own, own)
    out_ref[...] = total_ref[...] + dot(rolled_ref[:, pl.ds(start, own)], grid_ref[...])


def backward_more(wide, k, total, rolled, grid):
    rows, columns = total.shape
    return call(
        functools.partial(more_kernel, wide, k),
        "backward_more",
        array(total.shape, F32),
        [VMEM] * 3,
        VMEM,
        flops=2 * rows * columns * rolled.shape[1] // wide,
        moved=3 * MIB,
    )(total, rolled, grid)


def end_kernel(wide, k, total_ref, rolled_ref, grid_ref, out_hbm, out_ref, sems):
    own = rolled_ref.shape[1] // wide
    start = pl.multiple_of((lax.axis_index("wide") ^ k) * own, own)
    steps = sems.shape[0]
    rows = rolled_ref.shape[0] // steps
    copies = []
    for i in range(steps):
        span = pl.ds(i * rows, rows)
        part = dot(rolled_ref[span, pl.ds(start, own)], grid_ref[...])
        out_ref[span, :] = total_ref[span, :] + part
        copies.append(pltpu.make_async_copy(out_ref.at[span, :], out_hbm.at[span, :], sems.at[i]))
        copies[-1].start()
    for copy in copies:
        copy.wait()


def backward_end(wide, k, total, rolled, grid):
    rows, columns = total.shape
    return call(
        functools.partial(end_kernel, wide, k),
        "backward_end",
        array(total.shape, F32),
        [VMEM] * 3,
        HBM,
        [pltpu.VMEM(total.shape, F32), pltpu.SemaphoreType.DMA((16,))],
        flops=2 * rows * columns * rolled.shape[1] // wide,
        moved=4 * MIB,
    )(total, rolled, grid)


def exchange(value, step, size, axis):
    return lax.ppermute(value, axis, [(i, i ^ step) for i in range(size)])


def body(
    wide,
    narrow,
    coeff,
    groupb_row_energy,
    groupa_energy,
    groupb_basis_values,
    basis_a,
    potential,
    slot_sparse_level,
    block_pad,
    slot_grid_offset,
):
    chips = narrow // 2
    tables = jnp.swapaxes(groupb_basis_values, 1, 2)
    half = chips // 2
    order = list(range(1, wide - 1))
    whole, turned, rolled, basis, pot = first(
        wide,
        chips,
        slot_sparse_level,
        block_pad,
        slot_grid_offset,
        coeff,
        tables,
        basis_a,
        potential,
    )
    whole = exchange(whole, wide - 1, wide, "wide")
    where = {j: (basis, j) for j in range(chips)}
    sent = {k: chunk(wide, chips, k, turned, rolled) for k in order}
    far_parts = [exchange(sent[k][0], k, wide, "wide") for k in order]
    near_parts = [exchange(sent[k][1], k, wide, "wide") for k in order]
    mine = last(wide, turned, rolled)
    pieces = combine(chips, half, mine, whole, far_parts)
    xs = {j: exchange(pieces[j - half], 2 * j, narrow, "narrow") for j in range(half, chips)}
    pieces = combine(chips, 0, mine, whole, near_parts)
    for j in range(1, half):
        xs[j] = exchange(pieces[j], 2 * j, narrow, "narrow")
    total = own_points(pieces[0], where[0])
    visits = list(range(half, chips)) + list(range(1, half))
    for j in visits[:-1]:
        total = more_points(total, xs[j], where[j])
    mine, theirs = last_points(total, xs[visits[-1]], where[visits[-1]])
    acted = act(mine, exchange(theirs, 1, narrow, "narrow"), pot)
    other = exchange(acted, 1, narrow, "narrow")
    leave = list(range(1, chips))
    block, both = first_functions(acted, other, where[leave[0]])
    blocks = {leave[0]: exchange(block, 2 * leave[0], narrow, "narrow")}
    for j in leave[1:]:
        blocks[j] = exchange(functions(both, where[j]), 2 * j, narrow, "narrow")
    grid = assemble([functions(both, where[0])] + [blocks[j] for j in range(1, chips)])
    steps = [wide - 1] + order
    grids = {k: exchange(grid, k, wide, "wide") for k in steps}
    total = backward_own(
        wide, block_pad, rolled, grid, coeff, groupb_row_energy, groupa_energy
    )
    for k in steps[:-1]:
        total = backward_more(wide, k, total, rolled, grids[k])
    return backward_end(wide, steps[-1], total, rolled, grids[steps[-1]])


def solution(mesh):
    return jax.shard_map(
        functools.partial(body, mesh.shape["wide"], mesh.shape["narrow"]),
        mesh=mesh,
        in_specs=(
            P("wide", "narrow"),
            P("wide"),
            P("narrow"),
            P(),
            P(),
            P(("wide", "narrow"), None),
            P("wide"),
            P("wide"),
            P("wide"),
        ),
        out_specs=P("wide", "narrow"),
        check_vma=False,
    )
```

profile of v0, /device:TPU:0, one launch (start us, length us, event | category | flops | bytes accessed | tf_op | source)
XLA Modules:
  0.0 43.5 jit_solution(1832680051568091377)
XLA Ops:
  0.0 2.7 %forward_first.1 = (bf16[256,256]{1,0:T(8,128)(2,1)S(1)}, bf16[256,1024]{1,0:T(8,128)(2,1)S(1)}, bf16[1024,1024]{1,0:T(8,128)(2,1)S(1)}, bf16[4,256,2048]{2,1,0:T(8,128)(2,1)S(1)}, f32[32,2048]{1,0:T(8,128)S(1)}) custom-call(s32[16]{0:T(128)} %level_hbm.1, s32[16]{0:T(128)} %pad_ref.1, s32[16]{0:T(128)} %shift_hbm.1, bf16[1024,256]{1,0:T(8,128)(2,1)} %coeff_ref.1, ...), custom_call_target="tpu_custom_call" | custom-call | flops 134217728 | bytes 4194304 | tf_op jit(solution)/shard_map/forward_first/pallas_call | solution.py:149
  2.7 4.0 %collective-permute-start = (bf16[256,256]{1,0:T(8,128)(2,1)S(1)}, bf16[256,256]{1,0:T(8,128)(2,1)S(1)}, u32[]{:S(2)}, u32[]{:S(2)}) collective-permute-start(bf16[256,256]{1,0:T(8,128)(2,1)S(1)} %get-tuple-element.24), channel_id=1, source_target_pairs={{0,24},{8,16},{16,8},{24,0},{1,25},{9,17},{17,9},{25,1},{2,26},{10... | collective-permute-start | bytes 393224 | tf_op jit(solution)/shard_map/ppermute | solution.py:454
  7.0 0.6 %collective-permute-start.4 = (bf16[128,256]{1,0:T(8,128)(2,1)S(1)}, bf16[128,256]{1,0:T(8,128)(2,1)S(1)}, u32[]{:S(2)}, u32[]{:S(2)}) collective-permute-start(bf16[128,256]{1,0:T(8,128)(2,1)S(1)} %get-tuple-element.30), channel_id=1, source_target_pairs={{0,16},{8,24},{16,0},{24,8},{1,17},{9,25},{17,1},{25,9},{2,18},{10... | collective-permute-start | bytes 196616 | tf_op jit(solution)/shard_map/ppermute | solution.py:454
  8.1 2.0 %collective-permute-start.2 = (bf16[128,256]{1,0:T(8,128)(2,1)S(1)}, bf16[128,256]{1,0:T(8,128)(2,1)S(1)}, u32[]{:S(2)}, u32[]{:S(2)}) collective-permute-start(bf16[128,256]{1,0:T(8,128)(2,1)S(1)} %get-tuple-element.26), channel_id=1, source_target_pairs={{0,16},{8,24},{16,0},{24,8},{1,17},{9,25},{17,1},{25,9},{2,18},{10... | collective-permute-start | bytes 196616 | tf_op jit(solution)/shard_map/ppermute | solution.py:454
  10.1 1.5 %collective-permute-start.1 = (bf16[128,256]{1,0:T(8,128)(2,1)S(1)}, bf16[128,256]{1,0:T(8,128)(2,1)S(1)}, u32[]{:S(2)}, u32[]{:S(2)}) collective-permute-start(bf16[128,256]{1,0:T(8,128)(2,1)S(1)} %get-tuple-element.25), channel_id=1, source_target_pairs={{0,8},{8,0},{16,24},{24,16},{1,9},{9,1},{17,25},{25,17},{2,10},{10... | collective-permute-start | bytes 196616 | tf_op jit(solution)/shard_map/ppermute | solution.py:454
  12.1 0.7 %collective-permute-done.3.refs_0_ = bf16[128,256]{1,0:T(8,128)(2,1)S(1)} collective-permute-done((bf16[128,256]{1,0:T(8,128)(2,1)S(1)}, bf16[128,256]{1,0:T(8,128)(2,1)S(1)}, u32[]{:S(2)}, u32[]{:S(2)}) %collective-permute-start.3) | collective-permute-done | bytes 65568 | tf_op jit(solution)/shard_map/ppermute | solution.py:454
  12.8 2.7 %collective-permute-start.5 = (bf16[64,256]{1,0:T(8,128)(2,1)S(1)}, bf16[64,256]{1,0:T(8,128)(2,1)S(1)}, u32[]{:S(2)}, u32[]{:S(2)}) collective-permute-start(bf16[64,256]{1,0:T(8,128)(2,1)S(1)} %get-tuple-element.31), channel_id=1, source_target_pairs={{0,4},{1,5},{2,6},{3,7},{4,0},{5,1},{6,2},{7,3},{8,12},{9,13},{10,... | collective-permute-start | bytes 98312 | tf_op jit(solution)/shard_map/ppermute | solution.py:454
  15.5 1.3 %collective-permute-start.6 = (bf16[64,256]{1,0:T(8,128)(2,1)S(1)}, bf16[64,256]{1,0:T(8,128)(2,1)S(1)}, u32[]{:S(2)}, u32[]{:S(2)}) collective-permute-start(bf16[64,256]{1,0:T(8,128)(2,1)S(1)} %get-tuple-element.32), channel_id=1, source_target_pairs={{0,6},{1,7},{2,4},{3,5},{4,2},{5,3},{6,0},{7,1},{8,14},{9,15},{10,... | collective-permute-start | bytes 98312 | tf_op jit(solution)/shard_map/ppermute | solution.py:454
  18.2 3.0 %collective-permute-done.6.x_ref = bf16[64,256]{1,0:T(8,128)(2,1)S(1)} collective-permute-done((bf16[64,256]{1,0:T(8,128)(2,1)S(1)}, bf16[64,256]{1,0:T(8,128)(2,1)S(1)}, u32[]{:S(2)}, u32[]{:S(2)}) %collective-permute-start.6) | collective-permute-done | bytes 32800 | tf_op jit(solution)/shard_map/ppermute | solution.py:454
  21.9 1.5 %collective-permute-done.8.other_ref = f32[32,2048]{1,0:T(8,128)S(1)} collective-permute-done((f32[32,2048]{1,0:T(8,128)S(1)}, f32[32,2048]{1,0:T(8,128)S(1)}, u32[]{:S(2)}, u32[]{:S(2)}) %collective-permute-start.8) | collective-permute-done | bytes 262176 | tf_op jit(solution)/shard_map/ppermute | solution.py:454
  23.7 1.2 %collective-permute-done.9.other_ref = bf16[32,2048]{1,0:T(8,128)(2,1)S(1)} collective-permute-done((bf16[32,2048]{1,0:T(8,128)(2,1)S(1)}, bf16[32,2048]{1,0:T(8,128)(2,1)S(1)}, u32[]{:S(2)}, u32[]{:S(2)}) %collective-permute-start.9) | collective-permute-done | bytes 131104 | tf_op jit(solution)/shard_map/ppermute | solution.py:454
  24.9 0.4 %functions_first.1 = (bf16[64,256]{1,0:T(8,128)(2,1)S(1)}, bf16[64,2048]{1,0:T(8,128)(2,1)S(1)}) custom-call(bf16[32,2048]{1,0:T(8,128)(2,1)S(1)} %act.1.mine_ref, bf16[32,2048]{1,0:T(8,128)(2,1)S(1)} %collective-permute-done.9.other_ref, bf16[4,256,2048]{2,1,0:T(8,128)(2,1)S(1)} %get-tuple-element.28.basis_ref), custom_call_target="tpu_custom_call" | custom-call | flops 67108864 | bytes 2097152 | tf_op jit(solution)/shard_map/functions_first/pallas_call | solution.py:323
  25.8 0.4 %functions_more.4 = bf16[64,256]{1,0:T(8,128)(2,1)S(1)} custom-call(bf16[64,2048]{1,0:T(8,128)(2,1)S(1)} %get-tuple-element.37.both_ref, bf16[4,256,2048]{2,1,0:T(8,128)(2,1)S(1)} %get-tuple-element.28.basis_ref), custom_call_target="tpu_custom_call" | custom-call | flops 67108864 | bytes 2097152 | tf_op jit(solution)/shard_map/functions_more/pallas_call | solution.py:342
  26.3 1.9 %collective-permute-start.12 = (bf16[64,256]{1,0:T(8,128)(2,1)S(1)}, bf16[64,256]{1,0:T(8,128)(2,1)S(1)}, u32[]{:S(2)}, u32[]{:S(2)}) collective-permute-start(bf16[64,256]{1,0:T(8,128)(2,1)S(1)} %functions_more.5), channel_id=1, source_target_pairs={{0,6},{1,7},{2,4},{3,5},{4,2},{5,3},{6,0},{7,1},{8,14},{9,15},{10,... | collective-permute-start | bytes 98312 | tf_op jit(solution)/shard_map/ppermute | solution.py:454
  28.2 2.6 %collective-permute-start.10 = (bf16[64,256]{1,0:T(8,128)(2,1)S(1)}, bf16[64,256]{1,0:T(8,128)(2,1)S(1)}, u32[]{:S(2)}, u32[]{:S(2)}) collective-permute-start(bf16[64,256]{1,0:T(8,128)(2,1)S(1)} %get-tuple-element.38), channel_id=1, source_target_pairs={{0,2},{1,3},{2,0},{3,1},{4,6},{5,7},{6,4},{7,5},{8,10},{9,11},{10,... | collective-permute-start | bytes 98312 | tf_op jit(solution)/shard_map/ppermute | solution.py:454
  31.2 0.9 %collective-permute-done.12.refs_3_ = bf16[64,256]{1,0:T(8,128)(2,1)S(1)} collective-permute-done((bf16[64,256]{1,0:T(8,128)(2,1)S(1)}, bf16[64,256]{1,0:T(8,128)(2,1)S(1)}, u32[]{:S(2)}, u32[]{:S(2)}) %collective-permute-start.12) | collective-permute-done | bytes 32800 | tf_op jit(solution)/shard_map/ppermute | solution.py:454
  32.0 1.0 %collective-permute-done.11.refs_2_ = bf16[64,256]{1,0:T(8,128)(2,1)S(1)} collective-permute-done((bf16[64,256]{1,0:T(8,128)(2,1)S(1)}, bf16[64,256]{1,0:T(8,128)(2,1)S(1)}, u32[]{:S(2)}, u32[]{:S(2)}) %collective-permute-start.11) | collective-permute-done | bytes 32800 | tf_op jit(solution)/shard_map/ppermute | solution.py:454
  33.2 1.6 %collective-permute-start.13 = (bf16[256,256]{1,0:T(8,128)(2,1)S(1)}, bf16[256,256]{1,0:T(8,128)(2,1)}, u32[]{:S(2)}, u32[]{:S(2)}) collective-permute-start(bf16[256,256]{1,0:T(8,128)(2,1)S(1)} %assemble.1.grid_ref), channel_id=1, source_target_pairs={{0,24},{8,16},{16,8},{24,0},{1,25},{9,17},{17,9},{25,1},{2,26},{10... | collective-permute-start | bytes 393224 | tf_op jit(solution)/shard_map/ppermute | solution.py:454
  34.8 1.0 %collective-permute-start.14 = (bf16[256,256]{1,0:T(8,128)(2,1)S(1)}, bf16[256,256]{1,0:T(8,128)(2,1)S(1)}, u32[]{:S(2)}, u32[]{:S(2)}) collective-permute-start(bf16[256,256]{1,0:T(8,128)(2,1)S(1)} %assemble.1.grid_ref), channel_id=1, source_target_pairs={{0,8},{8,0},{16,24},{24,16},{1,9},{9,1},{17,25},{25,17},{2,10},{10... | collective-permute-start | bytes 393224 | tf_op jit(solution)/shard_map/ppermute | solution.py:454
  35.8 1.0 %collective-permute-start.15 = (bf16[256,256]{1,0:T(8,128)(2,1)S(1)}, bf16[256,256]{1,0:T(8,128)(2,1)S(1)}, u32[]{:S(2)}, u32[]{:S(2)}) collective-permute-start(bf16[256,256]{1,0:T(8,128)(2,1)S(1)} %assemble.1.grid_ref), channel_id=1, source_target_pairs={{0,16},{8,24},{16,0},{24,8},{1,17},{9,25},{17,1},{25,9},{2,18},{10... | collective-permute-start | bytes 393224 | tf_op jit(solution)/shard_map/ppermute | solution.py:454
  37.0 0.9 %backward_own.1.total_ref = f32[1024,256]{1,0:T(8,128)S(1)} custom-call(s32[16]{0:T(128)S(1)} %copy-done.1, bf16[1024,1024]{1,0:T(8,128)(2,1)S(1)} %get-tuple-element.22.rolled_ref, bf16[256,256]{1,0:T(8,128)(2,1)S(1)} %assemble.1.grid_ref, bf16[1024,256]{1,0:T(8,128)(2,1)S(1)} %copy-done, f32[1024,1]{1,0:T(8,128)S(1)} %copy.10.row_ref, f32[1,256]{1,0:T(1,128)S(1)} %bitcast.3), custom_call_target="tpu_custom_call" | custom-call | flops 134217728 | bytes 4194304 | tf_op jit(solution)/shard_map/backward_own/pallas_call | solution.py:393
  38.0 2.7 %collective-permute-done.13.grid_ref = bf16[256,256]{1,0:T(8,128)(2,1)} collective-permute-done((bf16[256,256]{1,0:T(8,128)(2,1)S(1)}, bf16[256,256]{1,0:T(8,128)(2,1)}, u32[]{:S(2)}, u32[]{:S(2)}) %collective-permute-start.13) | collective-permute-done | bytes 131104 | tf_op jit(solution)/shard_map/ppermute | solution.py:454
  40.7 1.2 %backward_more.2.total_ref = f32[1024,256]{1,0:T(8,128)S(1)} custom-call(f32[1024,256]{1,0:T(8,128)S(1)} %backward_own.1.total_ref, bf16[1024,1024]{1,0:T(8,128)(2,1)S(1)} %get-tuple-element.22.rolled_ref, bf16[256,256]{1,0:T(8,128)(2,1)} %collective-permute-done.13.grid_ref), custom_call_target="tpu_custom_call" | custom-call | flops 134217728 | bytes 3145728 | tf_op jit(solution)/shard_map/backward_more/pallas_call | solution.py:412
  42.2 1.3 %backward_end.1 = f32[1024,256]{1,0:T(8,128)} custom-call(f32[1024,256]{1,0:T(8,128)S(1)} %backward_more.3.total_ref, bf16[1024,1024]{1,0:T(8,128)(2,1)S(1)} %get-tuple-element.22.rolled_ref, bf16[256,256]{1,0:T(8,128)(2,1)S(1)} %collective-permute-done.15.grid_ref), custom_call_target="tpu_custom_call" | custom-call | flops 134217728 | bytes 4194304 | tf_op jit(solution)/shard_map/backward_end/pallas_call | solution.py:441
  (37 shorter events, 5.3 us)
Async XLA Ops:
  2.7 10.1 %collective-permute-start = (bf16[256,256]{1,0:T(8,128)(2,1)S(1)}, bf16[256,256]{1,0:T(8,128)(2,1)S(1)}, u32[]{:S(2)}, u32[]{:S(2)}) collective-permute-start(bf16[256,256]{1,0:T(8,128)(2,1)S(1)} %get-tuple-element.24), channel_id=1, source_target_pairs={{0,24},{8,16},{16,8},{24,0},{1,25},{9,17},{17,9},{25,1},{2,26},{10... | collective-permute-start | bytes 393224 | tf_op jit(solution)/shard_map/ppermute | solution.py:454
  7.0 5.1 %collective-permute-start.4 = (bf16[128,256]{1,0:T(8,128)(2,1)S(1)}, bf16[128,256]{1,0:T(8,128)(2,1)S(1)}, u32[]{:S(2)}, u32[]{:S(2)}) collective-permute-start(bf16[128,256]{1,0:T(8,128)(2,1)S(1)} %get-tuple-element.30), channel_id=1, source_target_pairs={{0,16},{8,24},{16,0},{24,8},{1,17},{9,25},{17,1},{25,9},{2,18},{10... | collective-permute-start | bytes 196616 | tf_op jit(solution)/shard_map/ppermute | solution.py:454
  7.9 4.8 %collective-permute-start.3 = (bf16[128,256]{1,0:T(8,128)(2,1)S(1)}, bf16[128,256]{1,0:T(8,128)(2,1)S(1)}, u32[]{:S(2)}, u32[]{:S(2)}) collective-permute-start(bf16[128,256]{1,0:T(8,128)(2,1)S(1)} %get-tuple-element.29), channel_id=1, source_target_pairs={{0,8},{8,0},{16,24},{24,16},{1,9},{9,1},{17,25},{25,17},{2,10},{10... | collective-permute-start | bytes 196616 | tf_op jit(solution)/shard_map/ppermute | solution.py:454
  8.1 8.7 %collective-permute-start.2 = (bf16[128,256]{1,0:T(8,128)(2,1)S(1)}, bf16[128,256]{1,0:T(8,128)(2,1)S(1)}, u32[]{:S(2)}, u32[]{:S(2)}) collective-permute-start(bf16[128,256]{1,0:T(8,128)(2,1)S(1)} %get-tuple-element.26), channel_id=1, source_target_pairs={{0,16},{8,24},{16,0},{24,8},{1,17},{9,25},{17,1},{25,9},{2,18},{10... | collective-permute-start | bytes 196616 | tf_op jit(solution)/shard_map/ppermute | solution.py:454
  10.1 6.8 %collective-permute-start.1 = (bf16[128,256]{1,0:T(8,128)(2,1)S(1)}, bf16[128,256]{1,0:T(8,128)(2,1)S(1)}, u32[]{:S(2)}, u32[]{:S(2)}) collective-permute-start(bf16[128,256]{1,0:T(8,128)(2,1)S(1)} %get-tuple-element.25), channel_id=1, source_target_pairs={{0,8},{8,0},{16,24},{24,16},{1,9},{9,1},{17,25},{25,17},{2,10},{10... | collective-permute-start | bytes 196616 | tf_op jit(solution)/shard_map/ppermute | solution.py:454
  12.8 5.1 %collective-permute-start.5 = (bf16[64,256]{1,0:T(8,128)(2,1)S(1)}, bf16[64,256]{1,0:T(8,128)(2,1)S(1)}, u32[]{:S(2)}, u32[]{:S(2)}) collective-permute-start(bf16[64,256]{1,0:T(8,128)(2,1)S(1)} %get-tuple-element.31), channel_id=1, source_target_pairs={{0,4},{1,5},{2,6},{3,7},{4,0},{5,1},{6,2},{7,3},{8,12},{9,13},{10,... | collective-permute-start | bytes 98312 | tf_op jit(solution)/shard_map/ppermute | solution.py:454
  15.5 5.7 %collective-permute-start.6 = (bf16[64,256]{1,0:T(8,128)(2,1)S(1)}, bf16[64,256]{1,0:T(8,128)(2,1)S(1)}, u32[]{:S(2)}, u32[]{:S(2)}) collective-permute-start(bf16[64,256]{1,0:T(8,128)(2,1)S(1)} %get-tuple-element.32), channel_id=1, source_target_pairs={{0,6},{1,7},{2,4},{3,5},{4,2},{5,3},{6,0},{7,1},{8,14},{9,15},{10,... | collective-permute-start | bytes 98312 | tf_op jit(solution)/shard_map/ppermute | solution.py:454
  16.9 4.6 %collective-permute-start.7 = (bf16[64,256]{1,0:T(8,128)(2,1)S(1)}, bf16[64,256]{1,0:T(8,128)(2,1)S(1)}, u32[]{:S(2)}, u32[]{:S(2)}) collective-permute-start(bf16[64,256]{1,0:T(8,128)(2,1)S(1)} %get-tuple-element.33), channel_id=1, source_target_pairs={{0,2},{1,3},{2,0},{3,1},{4,6},{5,7},{6,4},{7,5},{8,10},{9,11},{10,... | collective-permute-start | bytes 98312 | tf_op jit(solution)/shard_map/ppermute | solution.py:454
  21.8 1.6 %collective-permute-start.8 = (f32[32,2048]{1,0:T(8,128)S(1)}, f32[32,2048]{1,0:T(8,128)S(1)}, u32[]{:S(2)}, u32[]{:S(2)}) collective-permute-start(f32[32,2048]{1,0:T(8,128)S(1)} %get-tuple-element.35), channel_id=1, source_target_pairs={{0,1},{1,0},{2,3},{3,2},{4,5},{5,4},{6,7},{7,6},{8,9},{9,8},{10,11... | collective-permute-start | bytes 786440 | tf_op jit(solution)/shard_map/ppermute | solution.py:454
  23.5 1.4 %collective-permute-start.9 = (bf16[32,2048]{1,0:T(8,128)(2,1)S(1)}, bf16[32,2048]{1,0:T(8,128)(2,1)S(1)}, u32[]{:S(2)}, u32[]{:S(2)}) collective-permute-start(bf16[32,2048]{1,0:T(8,128)(2,1)S(1)} %act.1.mine_ref), channel_id=1, source_target_pairs={{0,1},{1,0},{2,3},{3,2},{4,5},{5,4},{6,7},{7,6},{8,9},{9,8},{10,11... | collective-permute-start | bytes 393224 | tf_op jit(solution)/shard_map/ppermute | solution.py:454
  25.8 11.0 %copy-start.3 = (f32[1024]{0:T(1024)S(1)}, f32[1024]{0:T(1024)}, u32[]{:S(2)}) copy-start(f32[1024]{0:T(1024)} %param.10) | copy-start | bytes 12292
  25.8 11.2 %copy-start = (bf16[1024,256]{1,0:T(8,128)(2,1)S(1)}, bf16[1024,256]{1,0:T(8,128)(2,1)}, u32[]{:S(2)}) copy-start(bf16[1024,256]{1,0:T(8,128)(2,1)} %coeff_ref.1) | copy-start | bytes 1572868
  25.8 11.2 %copy-start.1 = (s32[16]{0:T(128)S(1)}, s32[16]{0:T(128)}, u32[]{:S(2)}) copy-start(s32[16]{0:T(128)} %pad_ref.1) | copy-start | bytes 196
  25.8 11.2 %copy-start.2 = (f32[256]{0:T(256)S(1)}, f32[256]{0:T(256)}, u32[]{:S(2)}) copy-start(f32[256]{0:T(256)} %param.11) | copy-start | bytes 3076
  26.3 5.8 %collective-permute-start.12 = (bf16[64,256]{1,0:T(8,128)(2,1)S(1)}, bf16[64,256]{1,0:T(8,128)(2,1)S(1)}, u32[]{:S(2)}, u32[]{:S(2)}) collective-permute-start(bf16[64,256]{1,0:T(8,128)(2,1)S(1)} %functions_more.5), channel_id=1, source_target_pairs={{0,6},{1,7},{2,4},{3,5},{4,2},{5,3},{6,0},{7,1},{8,14},{9,15},{10,... | collective-permute-start | bytes 98312 | tf_op jit(solution)/shard_map/ppermute | solution.py:454
  28.2 4.9 %collective-permute-start.11 = (bf16[64,256]{1,0:T(8,128)(2,1)S(1)}, bf16[64,256]{1,0:T(8,128)(2,1)S(1)}, u32[]{:S(2)}, u32[]{:S(2)}) collective-permute-start(bf16[64,256]{1,0:T(8,128)(2,1)S(1)} %functions_more.4), channel_id=1, source_target_pairs={{0,4},{1,5},{2,6},{3,7},{4,0},{5,1},{6,2},{7,3},{8,12},{9,13},{10,... | collective-permute-start | bytes 98312 | tf_op jit(solution)/shard_map/ppermute | solution.py:454
  28.2 5.0 %collective-permute-start.10 = (bf16[64,256]{1,0:T(8,128)(2,1)S(1)}, bf16[64,256]{1,0:T(8,128)(2,1)S(1)}, u32[]{:S(2)}, u32[]{:S(2)}) collective-permute-start(bf16[64,256]{1,0:T(8,128)(2,1)S(1)} %get-tuple-element.38), channel_id=1, source_target_pairs={{0,2},{1,3},{2,0},{3,1},{4,6},{5,7},{6,4},{7,5},{8,10},{9,11},{10,... | collective-permute-start | bytes 98312 | tf_op jit(solution)/shard_map/ppermute | solution.py:454
  33.2 7.5 %collective-permute-start.13 = (bf16[256,256]{1,0:T(8,128)(2,1)S(1)}, bf16[256,256]{1,0:T(8,128)(2,1)}, u32[]{:S(2)}, u32[]{:S(2)}) collective-permute-start(bf16[256,256]{1,0:T(8,128)(2,1)S(1)} %assemble.1.grid_ref), channel_id=1, source_target_pairs={{0,24},{8,16},{16,8},{24,0},{1,25},{9,17},{17,9},{25,1},{2,26},{10... | collective-permute-start | bytes 393224 | tf_op jit(solution)/shard_map/ppermute | solution.py:454
  34.8 7.1 %collective-permute-start.14 = (bf16[256,256]{1,0:T(8,128)(2,1)S(1)}, bf16[256,256]{1,0:T(8,128)(2,1)S(1)}, u32[]{:S(2)}, u32[]{:S(2)}) collective-permute-start(bf16[256,256]{1,0:T(8,128)(2,1)S(1)} %assemble.1.grid_ref), channel_id=1, source_target_pairs={{0,8},{8,0},{16,24},{24,16},{1,9},{9,1},{17,25},{25,17},{2,10},{10... | collective-permute-start | bytes 393224 | tf_op jit(solution)/shard_map/ppermute | solution.py:454
  35.8 6.4 %collective-permute-start.15 = (bf16[256,256]{1,0:T(8,128)(2,1)S(1)}, bf16[256,256]{1,0:T(8,128)(2,1)S(1)}, u32[]{:S(2)}, u32[]{:S(2)}) collective-permute-start(bf16[256,256]{1,0:T(8,128)(2,1)S(1)} %assemble.1.grid_ref), channel_id=1, source_target_pairs={{0,16},{8,24},{16,0},{24,8},{1,17},{9,25},{17,1},{25,9},{2,18},{10... | collective-permute-start | bytes 393224 | tf_op jit(solution)/shard_map/ppermute | solution.py:454
where the time goes:
time: 43.7 us; the launch traced here: 43.5 us
  starting transfers between devices  20.7 us (47%)
  waiting for transfers between devices  11.7 us (27%)
  Pallas kernels  10.6 us (24%)
    ppermute x16, starting transfers between devices, exchange(): return lax.ppermute(value, axis, [(i, i ^ step) for i in range(size)])  20.7 us
    ppermute x16, waiting for transfers between devices, exchange(): return lax.ppermute(value, axis, [(i, i ^ step) for i in range(size)])  11.7 us
    pallas_call x1, Pallas kernels, first(): call(functools.partial(first_kernel, wide, chips), 'forward_first', (arra...  2.66 us
    pallas_call x2, Pallas kernels, backward_more(): call(functools.partial(more_kernel, wide, k), 'backward_more', array(tota...  1.5 us
    pallas_call x3, Pallas kernels, functions(): call(functools.partial(functions_kernel, j), 'functions_more', array((row...  1.33 us
    pallas_call x1, Pallas kernels, backward_end(): call(functools.partial(end_kernel, wide, k), 'backward_end', array(total....  1.32 us
    pallas_call x1, Pallas kernels, backward_own(): call(functools.partial(own_kernel, wide), 'backward_own', array(coeff.sha...  0.91 us
  transfers between devices with their start and end apart: 16, of which 10 were waited for; matrix products, arithmetic and copies ran while one was open for 1% of the time, Pallas kernels for 11%

commit v1 on v0

--- a/solution.py
+++ b/solution.py
@@ -127,12 +127,16 @@
         copy.wait()
     wait_all(table_hbm, table_ref, sems.at[3])
     row = lax.broadcasted_iota(jnp.int32, (width, 128), 0)
-    for s in range(slots):
-        rows = slice(s * width, (s + 1) * width)
+
+    def roll_slot(s, _):
+        rows = pl.ds(pl.multiple_of(s * width, width), width)
         live = jnp.where(row < width - pad_ref[s], 1.0, 0.0).astype(BF16)
         rolled = pltpu.roll(table_ref[level_ref[s]], shift_ref[s], 1)
         for p in range(0, points, 128):
             rolled_ref[rows, p : p + 128] = rolled[:, p : p + 128] * live
+        return 0
+
+    lax.fori_loop(0, slots, roll_slot, 0, unroll=2)
     wait_all(coeff_hbm, coeff_ref, sems.at[4])
     turned_ref[...] = coeff_ref[...].T
     out_ref[...] = chunk_of(turned_ref, rolled_ref, wide, wide - 1).astype(BF16).T
@@ -307,27 +311,26 @@
     )(mine, other, potential)
 
 
-def first_functions_kernel(j, mine_ref, other_ref, basis_ref, out_ref, both_ref):
+def first_functions_kernel(leave, mine_ref, other_ref, basis_ref, *refs):
+    outs, both_ref = refs[:-1], refs[-1]
     core = lax.axis_index("narrow") % 2
     rows = mine_ref.shape[0]
     mine, other = mine_ref[...].astype(F32), other_ref[...].astype(F32)
     both_ref[:rows] = jnp.where(core == 0, mine, other).astype(BF16)
     both_ref[rows:] = jnp.where(core == 0, other, mine).astype(BF16)
-    out_ref[...] = dot_turned(both_ref[...], basis_ref[j]).astype(BF16)
-
-
-def first_functions(mine, other, where):
-    basis, j = where
+    for j, out in zip(leave, outs):
+        out[...] = dot_turned(both_ref[...], basis_ref[j]).astype(BF16)
+
+
+def first_functions(leave, mine, other, basis):
     rows, points = mine.shape
     columns = basis.shape[1]
     return call(
-        functools.partial(first_functions_kernel, j),
+        functools.partial(first_functions_kernel, leave),
         "functions_first",
-        (array((2 * rows, columns), BF16), array((2 * rows, points), BF16)),
+        (array((2 * rows, columns), BF16),) * len(leave) + (array((2 * rows, points), BF16),),
         [VMEM] * 3,
-        (VMEM, VMEM),
-        flops=4 * rows * points * columns,
-        moved=2 * MIB,
+        (VMEM,) * (len(leave) + 1),
     )(mine, other, basis)
 
 
@@ -378,13 +381,21 @@
     me = lax.axis_index("wide")
     own = rolled_ref.shape[1] // wide
     start = pl.multiple_of(me * own, own)
-    out_ref[...] = dot(rolled_ref[:, pl.ds(start, own)], grid_ref[...])
     row = lax.broadcasted_iota(jnp.int32, (width, out_ref.shape[1]), 0)
-    for s in range(slots):
-        rows = slice(s * width, (s + 1) * width)
-        energy = row_ref[rows, :] + column_ref[...]
-        diagonal = energy * coeff_ref[rows, :].astype(F32)
-        out_ref[rows, :] += jnp.where(row < width - pad_ref[s], diagonal, 0.0)
+    group = 4
+
+    def block(i, _):
+        base = pl.multiple_of(i * group * width, group * width)
+        part = dot(rolled_ref[pl.ds(base, group * width), pl.ds(start, own)], grid_ref[...])
+        for s in range(group):
+            rows = pl.ds(base + s * width, width)
+            energy = row_ref[rows, :] + column_ref[...]
+            diagonal = energy * coeff_ref[rows, :].astype(F32)
+            live = row < width - pad_ref[i * group + s]
+            out_ref[rows, :] = part[s * width : (s + 1) * width] + jnp.where(live, diagonal, 0.0)
+        return 0
+
+    lax.fori_loop(0, slots // group, block, 0)
 
 
 def backward_own(wide, pad, rolled, grid, coeff, row_energy, column_energy):
@@ -404,7 +415,15 @@
 def more_kernel(wide, k, total_ref, rolled_ref, grid_ref, out_ref):
     own = rolled_ref.shape[1] // wide
     start = pl.multiple_of((lax.axis_index("wide") ^ k) * own, own)
-    out_ref[...] = total_ref[...] + dot(rolled_ref[:, pl.ds(start, own)], grid_ref[...])
+    count = 256
+
+    def block(i, _):
+        rows = pl.ds(pl.multiple_of(i * count, count), count)
+        part = dot(rolled_ref[rows, pl.ds(start, own)], grid_ref[...])
+        out_ref[rows, :] = total_ref[rows, :] + part
+        return 0
+
+    lax.fori_loop(0, rolled_ref.shape[0] // count, block, 0)
 
 
 def backward_more(wide, k, total, rolled, grid):
@@ -425,15 +444,22 @@
     start = pl.multiple_of((lax.axis_index("wide") ^ k) * own, own)
     steps = sems.shape[0]
     rows = rolled_ref.shape[0] // steps
-    copies = []
-    for i in range(steps):
-        span = pl.ds(i * rows, rows)
+
+    def block(i, _):
+        span = pl.ds(pl.multiple_of(i * rows, rows), rows)
         part = dot(rolled_ref[span, pl.ds(start, own)], grid_ref[...])
         out_ref[span, :] = total_ref[span, :] + part
-        copies.append(pltpu.make_async_copy(out_ref.at[span, :], out_hbm.at[span, :], sems.at[i]))
-        copies[-1].start()
-    for copy in copies:
-        copy.wait()
+        pltpu.make_async_copy(out_ref.at[span, :], out_hbm.at[span, :], sems.at[i]).start()
+        return 0
+
+    lax.fori_loop(0, steps, block, 0)
+
+    def finish(i, _):
+        span = pl.ds(pl.multiple_of(i * rows, rows), rows)
+        pltpu.make_async_copy(out_ref.at[span, :], out_hbm.at[span, :], sems.at[i]).wait()
+        return 0
+
+    lax.fori_loop(0, steps, finish, 0)
 
 
 def backward_end(wide, k, total, rolled, grid):
@@ -444,7 +470,7 @@
         array(total.shape, F32),
         [VMEM] * 3,
         HBM,
-        [pltpu.VMEM(total.shape, F32), pltpu.SemaphoreType.DMA((16,))],
+        [pltpu.VMEM(total.shape, F32), pltpu.SemaphoreType.DMA((8,))],
         flops=2 * rows * columns * rolled.shape[1] // wide,
         moved=4 * MIB,
     )(total, rolled, grid)
@@ -500,11 +526,9 @@
     mine, theirs = last_points(total, xs[visits[-1]], where[visits[-1]])
     acted = act(mine, exchange(theirs, 1, narrow, "narrow"), pot)
     other = exchange(acted, 1, narrow, "narrow")
-    leave = list(range(1, chips))
-    block, both = first_functions(acted, other, where[leave[0]])
-    blocks = {leave[0]: exchange(block, 2 * leave[0], narrow, "narrow")}
-    for j in leave[1:]:
-        blocks[j] = exchange(functions(both, where[j]), 2 * j, narrow, "narrow")
+    leave = list(reversed(range(1, chips)))
+    *out, both = first_functions(leave, acted, other, basis)
+    blocks = {j: exchange(out[i], 2 * j, narrow, "narrow") for i, j in enumerate(leave)}
     grid = assemble([functions(both, where[0])] + [blocks[j] for j in range(1, chips)])
     steps = [wide - 1] + order
     grids = {k: exchange(grid, k, wide, "wide") for k in steps}

time: 43.7 us -> 45.5 us (1.041)
  Pallas kernels: 10.6 us -> 12.7 us
    pallas_call x2, Pallas kernels: 1.5 us -> 2.44 us  [backward_more(): call(functools.partial(more_kernel, wide, k), 'backward_more', array(tota...]
    pallas_call x3 -> x1, Pallas kernels: 1.33 us -> 0.44 us  [functions(): call(functools.partial(functions_kernel, j), 'functions_more', array((row...]
    pallas_call x1, Pallas kernels: 1.32 us -> 2.08 us  [backward_end(): call(functools.partial(end_kernel, wide, k), 'backward_end', array(total....]
    pallas_call x1, Pallas kernels: 0.45 us -> 1.07 us  [first_functions(): call(functools.partial(first_functions_kernel, leave), 'functions_first',...]
    pallas_call x1, Pallas kernels: 0.91 us -> 1.39 us  [backward_own(): call(functools.partial(own_kernel, wide), 'backward_own', array(coeff.sha...]
  transfers between devices with their start and end apart: 16 -> 16, of which waited for: 10 -> 9; matrix products, arithmetic and copies ran while one was open for 1% -> 0% of each run, Pallas kernels for 11% -> 14%
where the time goes in v1:
time: 45.5 us; the launch traced here: 45.3 us
  starting transfers between devices  20.7 us (45%)
  Pallas kernels  12.7 us (28%)
  waiting for transfers between devices  11.4 us (25%)
    ppermute x16, starting transfers between devices, exchange(): return lax.ppermute(value, axis, [(i, i ^ step) for i in range(size)])  20.7 us
    ppermute x16, waiting for transfers between devices, exchange(): return lax.ppermute(value, axis, [(i, i ^ step) for i in range(size)])  11.4 us
    pallas_call x1, Pallas kernels, first(): call(functools.partial(first_kernel, wide, chips), 'forward_first', (arra...  2.89 us
    pallas_call x2, Pallas kernels, backward_more(): call(functools.partial(more_kernel, wide, k), 'backward_more', array(tota...  2.44 us
    pallas_call x1, Pallas kernels, backward_end(): call(functools.partial(end_kernel, wide, k), 'backward_end', array(total....  2.08 us
    pallas_call x1, Pallas kernels, backward_own(): call(functools.partial(own_kernel, wide), 'backward_own', array(coeff.sha...  1.39 us
    pallas_call x1, Pallas kernels, first_functions(): call(functools.partial(first_functions_kernel, leave), 'functions_first',...  1.07 us
  transfers between devices with their start and end apart: 16, of which 9 were waited for; matrix products, arithmetic and copies ran while one was open for 0% of the time, Pallas kernels for 14%

profile of v1, /device:TPU:0, one launch (start us, length us, event | category | flops | bytes accessed | tf_op | source)
XLA Modules:
  0.0 45.3 jit_solution(6299545922969347725)
XLA Ops:
  0.0 2.9 %forward_first.1 = (bf16[256,256]{1,0:T(8,128)(2,1)S(1)}, bf16[256,1024]{1,0:T(8,128)(2,1)S(1)}, bf16[1024,1024]{1,0:T(8,128)(2,1)S(1)}, bf16[4,256,2048]{2,1,0:T(8,128)(2,1)S(1)}, f32[32,2048]{1,0:T(8,128)S(1)}) custom-call(s32[16]{0:T(128)} %level_hbm.1, s32[16]{0:T(128)} %pad_ref.1, s32[16]{0:T(128)} %shift_hbm.1, bf16[1024,256]{1,0:T(8,128)(2,1)} %coeff_ref.1, ...), custom_call_target="tpu_custom_call" | custom-call | flops 134217728 | bytes 4194304 | tf_op jit(solution)/shard_map/forward_first/pallas_call | solution.py:153
  2.9 4.0 %collective-permute-start = (bf16[256,256]{1,0:T(8,128)(2,1)S(1)}, bf16[256,256]{1,0:T(8,128)(2,1)S(1)}, u32[]{:S(2)}, u32[]{:S(2)}) collective-permute-start(bf16[256,256]{1,0:T(8,128)(2,1)S(1)} %get-tuple-element.26), channel_id=1, source_target_pairs={{0,24},{8,16},{16,8},{24,0},{1,25},{9,17},{17,9},{25,1},{2,26},{10... | collective-permute-start | bytes 393224 | tf_op jit(solution)/shard_map/ppermute | solution.py:480
  7.2 0.6 %collective-permute-start.4 = (bf16[128,256]{1,0:T(8,128)(2,1)S(1)}, bf16[128,256]{1,0:T(8,128)(2,1)S(1)}, u32[]{:S(2)}, u32[]{:S(2)}) collective-permute-start(bf16[128,256]{1,0:T(8,128)(2,1)S(1)} %get-tuple-element.32), channel_id=1, source_target_pairs={{0,16},{8,24},{16,0},{24,8},{1,17},{9,25},{17,1},{25,9},{2,18},{10... | collective-permute-start | bytes 196616 | tf_op jit(solution)/shard_map/ppermute | solution.py:480
  8.3 2.0 %collective-permute-start.2 = (bf16[128,256]{1,0:T(8,128)(2,1)S(1)}, bf16[128,256]{1,0:T(8,128)(2,1)S(1)}, u32[]{:S(2)}, u32[]{:S(2)}) collective-permute-start(bf16[128,256]{1,0:T(8,128)(2,1)S(1)} %get-tuple-element.28), channel_id=1, source_target_pairs={{0,16},{8,24},{16,0},{24,8},{1,17},{9,25},{17,1},{25,9},{2,18},{10... | collective-permute-start | bytes 196616 | tf_op jit(solution)/shard_map/ppermute | solution.py:480
  10.3 1.5 %collective-permute-start.1 = (bf16[128,256]{1,0:T(8,128)(2,1)S(1)}, bf16[128,256]{1,0:T(8,128)(2,1)S(1)}, u32[]{:S(2)}, u32[]{:S(2)}) collective-permute-start(bf16[128,256]{1,0:T(8,128)(2,1)S(1)} %get-tuple-element.27), channel_id=1, source_target_pairs={{0,8},{8,0},{16,24},{24,16},{1,9},{9,1},{17,25},{25,17},{2,10},{10... | collective-permute-start | bytes 196616 | tf_op jit(solution)/shard_map/ppermute | solution.py:480
  12.3 0.7 %collective-permute-done.3.refs_0_ = bf16[128,256]{1,0:T(8,128)(2,1)S(1)} collective-permute-done((bf16[128,256]{1,0:T(8,128)(2,1)S(1)}, bf16[128,256]{1,0:T(8,128)(2,1)S(1)}, u32[]{:S(2)}, u32[]{:S(2)}) %collective-permute-start.3) | collective-permute-done | bytes 65568 | tf_op jit(solution)/shard_map/ppermute | solution.py:480
  13.1 2.7 %collective-permute-start.5 = (bf16[64,256]{1,0:T(8,128)(2,1)S(1)}, bf16[64,256]{1,0:T(8,128)(2,1)S(1)}, u32[]{:S(2)}, u32[]{:S(2)}) collective-permute-start(bf16[64,256]{1,0:T(8,128)(2,1)S(1)} %get-tuple-element.33), channel_id=1, source_target_pairs={{0,4},{1,5},{2,6},{3,7},{4,0},{5,1},{6,2},{7,3},{8,12},{9,13},{10,... | collective-permute-start | bytes 98312 | tf_op jit(solution)/shard_map/ppermute | solution.py:480
  15.7 1.3 %collective-permute-start.6 = (bf16[64,256]{1,0:T(8,128)(2,1)S(1)}, bf16[64,256]{1,0:T(8,128)(2,1)S(1)}, u32[]{:S(2)}, u32[]{:S(2)}) collective-permute-start(bf16[64,256]{1,0:T(8,128)(2,1)S(1)} %get-tuple-element.34), channel_id=1, source_target_pairs={{0,6},{1,7},{2,4},{3,5},{4,2},{5,3},{6,0},{7,1},{8,14},{9,15},{10,... | collective-permute-start | bytes 98312 | tf_op jit(solution)/shard_map/ppermute | solution.py:480
  18.4 3.0 %collective-permute-done.6.x_ref = bf16[64,256]{1,0:T(8,128)(2,1)S(1)} collective-permute-done((bf16[64,256]{1,0:T(8,128)(2,1)S(1)}, bf16[64,256]{1,0:T(8,128)(2,1)S(1)}, u32[]{:S(2)}, u32[]{:S(2)}) %collective-permute-start.6) | collective-permute-done | bytes 32800 | tf_op jit(solution)/shard_map/ppermute | solution.py:480
  22.1 1.5 %collective-permute-done.8.other_ref = f32[32,2048]{1,0:T(8,128)S(1)} collective-permute-done((f32[32,2048]{1,0:T(8,128)S(1)}, f32[32,2048]{1,0:T(8,128)S(1)}, u32[]{:S(2)}, u32[]{:S(2)}) %collective-permute-start.8) | collective-permute-done | bytes 262176 | tf_op jit(solution)/shard_map/ppermute | solution.py:480
  24.0 1.2 %collective-permute-done.9.other_ref = bf16[32,2048]{1,0:T(8,128)(2,1)S(1)} collective-permute-done((bf16[32,2048]{1,0:T(8,128)(2,1)S(1)}, bf16[32,2048]{1,0:T(8,128)(2,1)S(1)}, u32[]{:S(2)}, u32[]{:S(2)}) %collective-permute-start.9) | collective-permute-done | bytes 131104 | tf_op jit(solution)/shard_map/ppermute | solution.py:480
  25.2 1.1 %functions_first.1 = (bf16[64,256]{1,0:T(8,128)(2,1)S(1)}, bf16[64,256]{1,0:T(8,128)(2,1)S(1)}, bf16[64,256]{1,0:T(8,128)(2,1)S(1)}, bf16[64,2048]{1,0:T(8,128)(2,1)S(1)}) custom-call(bf16[32,2048]{1,0:T(8,128)(2,1)S(1)} %act.1.mine_ref, bf16[32,2048]{1,0:T(8,128)(2,1)S(1)} %collective-permute-done.9.other_ref, ...), custom_call_target="tpu_custom_call" | custom-call | tf_op jit(solution)/shard_map/functions_first/pallas_call | solution.py:328
  26.3 2.4 %collective-permute-start.11 = (bf16[64,256]{1,0:T(8,128)(2,1)S(1)}, bf16[64,256]{1,0:T(8,128)(2,1)S(1)}, u32[]{:S(2)}, u32[]{:S(2)}) collective-permute-start(bf16[64,256]{1,0:T(8,128)(2,1)S(1)} %get-tuple-element.41), channel_id=1, source_target_pairs={{0,4},{1,5},{2,6},{3,7},{4,0},{5,1},{6,2},{7,3},{8,12},{9,13},{10,... | collective-permute-start | bytes 98312 | tf_op jit(solution)/shard_map/ppermute | solution.py:480
  28.7 2.0 %collective-permute-start.12 = (bf16[64,256]{1,0:T(8,128)(2,1)S(1)}, bf16[64,256]{1,0:T(8,128)(2,1)S(1)}, u32[]{:S(2)}, u32[]{:S(2)}) collective-permute-start(bf16[64,256]{1,0:T(8,128)(2,1)S(1)} %get-tuple-element.42), channel_id=1, source_target_pairs={{0,6},{1,7},{2,4},{3,5},{4,2},{5,3},{6,0},{7,1},{8,14},{9,15},{10,... | collective-permute-start | bytes 98312 | tf_op jit(solution)/shard_map/ppermute | solution.py:480
  31.1 0.6 %collective-permute-done.11.refs_2_ = bf16[64,256]{1,0:T(8,128)(2,1)S(1)} collective-permute-done((bf16[64,256]{1,0:T(8,128)(2,1)S(1)}, bf16[64,256]{1,0:T(8,128)(2,1)S(1)}, u32[]{:S(2)}, u32[]{:S(2)}) %collective-permute-start.11) | collective-permute-done | bytes 32800 | tf_op jit(solution)/shard_map/ppermute | solution.py:480
  31.8 2.6 %collective-permute-done.12.refs_3_ = bf16[64,256]{1,0:T(8,128)(2,1)S(1)} collective-permute-done((bf16[64,256]{1,0:T(8,128)(2,1)S(1)}, bf16[64,256]{1,0:T(8,128)(2,1)S(1)}, u32[]{:S(2)}, u32[]{:S(2)}) %collective-permute-start.12) | collective-permute-done | bytes 32800 | tf_op jit(solution)/shard_map/ppermute | solution.py:480
  34.4 1.6 %collective-permute-start.13 = (bf16[256,256]{1,0:T(8,128)(2,1)S(1)}, bf16[256,256]{1,0:T(8,128)(2,1)}, u32[]{:S(2)}, u32[]{:S(2)}) collective-permute-start(bf16[256,256]{1,0:T(8,128)(2,1)S(1)} %assemble.1.grid_ref), channel_id=1, source_target_pairs={{0,24},{8,16},{16,8},{24,0},{1,25},{9,17},{17,9},{25,1},{2,26},{10... | collective-permute-start | bytes 393224 | tf_op jit(solution)/shard_map/ppermute | solution.py:480
  36.0 1.0 %collective-permute-start.14 = (bf16[256,256]{1,0:T(8,128)(2,1)S(1)}, bf16[256,256]{1,0:T(8,128)(2,1)S(1)}, u32[]{:S(2)}, u32[]{:S(2)}) collective-permute-start(bf16[256,256]{1,0:T(8,128)(2,1)S(1)} %assemble.1.grid_ref), channel_id=1, source_target_pairs={{0,8},{8,0},{16,24},{24,16},{1,9},{9,1},{17,25},{25,17},{2,10},{10... | collective-permute-start | bytes 393224 | tf_op jit(solution)/shard_map/ppermute | solution.py:480
  37.0 1.0 %collective-permute-start.15 = (bf16[256,256]{1,0:T(8,128)(2,1)S(1)}, bf16[256,256]{1,0:T(8,128)(2,1)S(1)}, u32[]{:S(2)}, u32[]{:S(2)}) collective-permute-start(bf16[256,256]{1,0:T(8,128)(2,1)S(1)} %assemble.1.grid_ref), channel_id=1, source_target_pairs={{0,16},{8,24},{16,0},{24,8},{1,17},{9,25},{17,1},{25,9},{2,18},{10... | collective-permute-start | bytes 393224 | tf_op jit(solution)/shard_map/ppermute | solution.py:480
  38.2 1.4 %backward_own.1.total_ref = f32[1024,256]{1,0:T(8,128)S(1)} custom-call(s32[16]{0:T(128)S(1)} %copy-done.1, bf16[1024,1024]{1,0:T(8,128)(2,1)S(1)} %get-tuple-element.24.rolled_ref, bf16[256,256]{1,0:T(8,128)(2,1)S(1)} %assemble.1.grid_ref, bf16[1024,256]{1,0:T(8,128)(2,1)S(1)} %copy-done, f32[1024,1]{1,0:T(8,128)S(1)} %copy.10.row_ref, f32[1,256]{1,0:T(1,128)S(1)} %bitcast.3), custom_call_target="tpu_custom_call" | custom-call | flops 134217728 | bytes 4194304 | tf_op jit(solution)/shard_map/backward_own/pallas_call | solution.py:404
  39.6 1.2 %collective-permute-done.13.grid_ref = bf16[256,256]{1,0:T(8,128)(2,1)} collective-permute-done((bf16[256,256]{1,0:T(8,128)(2,1)S(1)}, bf16[256,256]{1,0:T(8,128)(2,1)}, u32[]{:S(2)}, u32[]{:S(2)}) %collective-permute-start.13) | collective-permute-done | bytes 131104 | tf_op jit(solution)/shard_map/ppermute | solution.py:480
  40.8 1.7 %backward_more.2.total_ref = f32[1024,256]{1,0:T(8,128)S(1)} custom-call(f32[1024,256]{1,0:T(8,128)S(1)} %backward_own.1.total_ref, bf16[1024,1024]{1,0:T(8,128)(2,1)S(1)} %get-tuple-element.24.rolled_ref, bf16[256,256]{1,0:T(8,128)(2,1)} %collective-permute-done.13.grid_ref), custom_call_target="tpu_custom_call" | custom-call | flops 134217728 | bytes 3145728 | tf_op jit(solution)/shard_map/backward_more/pallas_call | solution.py:431
  42.5 0.8 %backward_more.3.total_ref = f32[1024,256]{1,0:T(8,128)S(1)} custom-call(f32[1024,256]{1,0:T(8,128)S(1)} %backward_more.2.total_ref, bf16[1024,1024]{1,0:T(8,128)(2,1)S(1)} %get-tuple-element.24.rolled_ref, bf16[256,256]{1,0:T(8,128)(2,1)S(1)} %collective-permute-done.14.grid_ref), custom_call_target="tpu_custom_call" | custom-call | flops 134217728 | bytes 3145728 | tf_op jit(solution)/shard_map/backward_more/pallas_call | solution.py:431
  43.3 2.1 %backward_end.1 = f32[1024,256]{1,0:T(8,128)} custom-call(f32[1024,256]{1,0:T(8,128)S(1)} %backward_more.3.total_ref, bf16[1024,1024]{1,0:T(8,128)(2,1)S(1)} %get-tuple-element.24.rolled_ref, bf16[256,256]{1,0:T(8,128)(2,1)S(1)} %collective-permute-done.15.grid_ref), custom_call_target="tpu_custom_call" | custom-call | flops 134217728 | bytes 4194304 | tf_op jit(solution)/shard_map/backward_end/pallas_call | solution.py:467
  (35 shorter events, 4.5 us)
Async XLA Ops:
  2.9 10.1 %collective-permute-start = (bf16[256,256]{1,0:T(8,128)(2,1)S(1)}, bf16[256,256]{1,0:T(8,128)(2,1)S(1)}, u32[]{:S(2)}, u32[]{:S(2)}) collective-permute-start(bf16[256,256]{1,0:T(8,128)(2,1)S(1)} %get-tuple-element.26), channel_id=1, source_target_pairs={{0,24},{8,16},{16,8},{24,0},{1,25},{9,17},{17,9},{25,1},{2,26},{10... | collective-permute-start | bytes 393224 | tf_op jit(solution)/shard_map/ppermute | solution.py:480
  7.2 5.1 %collective-permute-start.4 = (bf16[128,256]{1,0:T(8,128)(2,1)S(1)}, bf16[128,256]{1,0:T(8,128)(2,1)S(1)}, u32[]{:S(2)}, u32[]{:S(2)}) collective-permute-start(bf16[128,256]{1,0:T(8,128)(2,1)S(1)} %get-tuple-element.32), channel_id=1, source_target_pairs={{0,16},{8,24},{16,0},{24,8},{1,17},{9,25},{17,1},{25,9},{2,18},{10... | collective-permute-start | bytes 196616 | tf_op jit(solution)/shard_map/ppermute | solution.py:480
  8.2 4.8 %collective-permute-start.3 = (bf16[128,256]{1,0:T(8,128)(2,1)S(1)}, bf16[128,256]{1,0:T(8,128)(2,1)S(1)}, u32[]{:S(2)}, u32[]{:S(2)}) collective-permute-start(bf16[128,256]{1,0:T(8,128)(2,1)S(1)} %get-tuple-element.31), channel_id=1, source_target_pairs={{0,8},{8,0},{16,24},{24,16},{1,9},{9,1},{17,25},{25,17},{2,10},{10... | collective-permute-start | bytes 196616 | tf_op jit(solution)/shard_map/ppermute | solution.py:480
  8.3 8.8 %collective-permute-start.2 = (bf16[128,256]{1,0:T(8,128)(2,1)S(1)}, bf16[128,256]{1,0:T(8,128)(2,1)S(1)}, u32[]{:S(2)}, u32[]{:S(2)}) collective-permute-start(bf16[128,256]{1,0:T(8,128)(2,1)S(1)} %get-tuple-element.28), channel_id=1, source_target_pairs={{0,16},{8,24},{16,0},{24,8},{1,17},{9,25},{17,1},{25,9},{2,18},{10... | collective-permute-start | bytes 196616 | tf_op jit(solution)/shard_map/ppermute | solution.py:480
  10.3 6.8 %collective-permute-start.1 = (bf16[128,256]{1,0:T(8,128)(2,1)S(1)}, bf16[128,256]{1,0:T(8,128)(2,1)S(1)}, u32[]{:S(2)}, u32[]{:S(2)}) collective-permute-start(bf16[128,256]{1,0:T(8,128)(2,1)S(1)} %get-tuple-element.27), channel_id=1, source_target_pairs={{0,8},{8,0},{16,24},{24,16},{1,9},{9,1},{17,25},{25,17},{2,10},{10... | collective-permute-start | bytes 196616 | tf_op jit(solution)/shard_map/ppermute | solution.py:480
  13.1 5.1 %collective-permute-start.5 = (bf16[64,256]{1,0:T(8,128)(2,1)S(1)}, bf16[64,256]{1,0:T(8,128)(2,1)S(1)}, u32[]{:S(2)}, u32[]{:S(2)}) collective-permute-start(bf16[64,256]{1,0:T(8,128)(2,1)S(1)} %get-tuple-element.33), channel_id=1, source_target_pairs={{0,4},{1,5},{2,6},{3,7},{4,0},{5,1},{6,2},{7,3},{8,12},{9,13},{10,... | collective-permute-start | bytes 98312 | tf_op jit(solution)/shard_map/ppermute | solution.py:480
  15.7 5.7 %collective-permute-start.6 = (bf16[64,256]{1,0:T(8,128)(2,1)S(1)}, bf16[64,256]{1,0:T(8,128)(2,1)S(1)}, u32[]{:S(2)}, u32[]{:S(2)}) collective-permute-start(bf16[64,256]{1,0:T(8,128)(2,1)S(1)} %get-tuple-element.34), channel_id=1, source_target_pairs={{0,6},{1,7},{2,4},{3,5},{4,2},{5,3},{6,0},{7,1},{8,14},{9,15},{10,... | collective-permute-start | bytes 98312 | tf_op jit(solution)/shard_map/ppermute | solution.py:480
  17.1 4.6 %collective-permute-start.7 = (bf16[64,256]{1,0:T(8,128)(2,1)S(1)}, bf16[64,256]{1,0:T(8,128)(2,1)S(1)}, u32[]{:S(2)}, u32[]{:S(2)}) collective-permute-start(bf16[64,256]{1,0:T(8,128)(2,1)S(1)} %get-tuple-element.35), channel_id=1, source_target_pairs={{0,2},{1,3},{2,0},{3,1},{4,6},{5,7},{6,4},{7,5},{8,10},{9,11},{10,... | collective-permute-start | bytes 98312 | tf_op jit(solution)/shard_map/ppermute | solution.py:480
  22.1 1.6 %collective-permute-start.8 = (f32[32,2048]{1,0:T(8,128)S(1)}, f32[32,2048]{1,0:T(8,128)S(1)}, u32[]{:S(2)}, u32[]{:S(2)}) collective-permute-start(f32[32,2048]{1,0:T(8,128)S(1)} %get-tuple-element.37), channel_id=1, source_target_pairs={{0,1},{1,0},{2,3},{3,2},{4,5},{5,4},{6,7},{7,6},{8,9},{9,8},{10,11... | collective-permute-start | bytes 786440 | tf_op jit(solution)/shard_map/ppermute | solution.py:480
  23.7 14.3 %copy-start.3 = (f32[1024]{0:T(1024)S(1)}, f32[1024]{0:T(1024)}, u32[]{:S(2)}) copy-start(f32[1024]{0:T(1024)} %param.10) | copy-start | bytes 12292
  23.7 14.5 %copy-start = (bf16[1024,256]{1,0:T(8,128)(2,1)S(1)}, bf16[1024,256]{1,0:T(8,128)(2,1)}, u32[]{:S(2)}) copy-start(bf16[1024,256]{1,0:T(8,128)(2,1)} %coeff_ref.1) | copy-start | bytes 1572868
  23.7 14.5 %copy-start.1 = (s32[16]{0:T(128)S(1)}, s32[16]{0:T(128)}, u32[]{:S(2)}) copy-start(s32[16]{0:T(128)} %pad_ref.1) | copy-start | bytes 196
  23.7 14.5 %copy-start.2 = (f32[256]{0:T(256)S(1)}, f32[256]{0:T(256)}, u32[]{:S(2)}) copy-start(f32[256]{0:T(256)} %param.11) | copy-start | bytes 3076
  23.8 1.4 %collective-permute-start.9 = (bf16[32,2048]{1,0:T(8,128)(2,1)S(1)}, bf16[32,2048]{1,0:T(8,128)(2,1)S(1)}, u32[]{:S(2)}, u32[]{:S(2)}) collective-permute-start(bf16[32,2048]{1,0:T(8,128)(2,1)S(1)} %act.1.mine_ref), channel_id=1, source_target_pairs={{0,1},{1,0},{2,3},{3,2},{4,5},{5,4},{6,7},{7,6},{8,9},{9,8},{10,11... | collective-permute-start | bytes 393224 | tf_op jit(solution)/shard_map/ppermute | solution.py:480
  26.2 4.9 %collective-permute-start.10 = (bf16[64,256]{1,0:T(8,128)(2,1)S(1)}, bf16[64,256]{1,0:T(8,128)(2,1)S(1)}, u32[]{:S(2)}, u32[]{:S(2)}) collective-permute-start(bf16[64,256]{1,0:T(8,128)(2,1)S(1)} %get-tuple-element.40), channel_id=1, source_target_pairs={{0,2},{1,3},{2,0},{3,1},{4,6},{5,7},{6,4},{7,5},{8,10},{9,11},{10,... | collective-permute-start | bytes 98312 | tf_op jit(solution)/shard_map/ppermute | solution.py:480
  26.3 5.4 %collective-permute-start.11 = (bf16[64,256]{1,0:T(8,128)(2,1)S(1)}, bf16[64,256]{1,0:T(8,128)(2,1)S(1)}, u32[]{:S(2)}, u32[]{:S(2)}) collective-permute-start(bf16[64,256]{1,0:T(8,128)(2,1)S(1)} %get-tuple-element.41), channel_id=1, source_target_pairs={{0,4},{1,5},{2,6},{3,7},{4,0},{5,1},{6,2},{7,3},{8,12},{9,13},{10,... | collective-permute-start | bytes 98312 | tf_op jit(solution)/shard_map/ppermute | solution.py:480
  28.7 5.7 %collective-permute-start.12 = (bf16[64,256]{1,0:T(8,128)(2,1)S(1)}, bf16[64,256]{1,0:T(8,128)(2,1)S(1)}, u32[]{:S(2)}, u32[]{:S(2)}) collective-permute-start(bf16[64,256]{1,0:T(8,128)(2,1)S(1)} %get-tuple-element.42), channel_id=1, source_target_pairs={{0,6},{1,7},{2,4},{3,5},{4,2},{5,3},{6,0},{7,1},{8,14},{9,15},{10,... | collective-permute-start | bytes 98312 | tf_op jit(solution)/shard_map/ppermute | solution.py:480
  34.4 6.4 %collective-permute-start.13 = (bf16[256,256]{1,0:T(8,128)(2,1)S(1)}, bf16[256,256]{1,0:T(8,128)(2,1)}, u32[]{:S(2)}, u32[]{:S(2)}) collective-permute-start(bf16[256,256]{1,0:T(8,128)(2,1)S(1)} %assemble.1.grid_ref), channel_id=1, source_target_pairs={{0,24},{8,16},{16,8},{24,0},{1,25},{9,17},{17,9},{25,1},{2,26},{10... | collective-permute-start | bytes 393224 | tf_op jit(solution)/shard_map/ppermute | solution.py:480
  36.0 6.5 %collective-permute-start.14 = (bf16[256,256]{1,0:T(8,128)(2,1)S(1)}, bf16[256,256]{1,0:T(8,128)(2,1)S(1)}, u32[]{:S(2)}, u32[]{:S(2)}) collective-permute-start(bf16[256,256]{1,0:T(8,128)(2,1)S(1)} %assemble.1.grid_ref), channel_id=1, source_target_pairs={{0,8},{8,0},{16,24},{24,16},{1,9},{9,1},{17,25},{25,17},{2,10},{10... | collective-permute-start | bytes 393224 | tf_op jit(solution)/shard_map/ppermute | solution.py:480
  37.0 6.3 %collective-permute-start.15 = (bf16[256,256]{1,0:T(8,128)(2,1)S(1)}, bf16[256,256]{1,0:T(8,128)(2,1)S(1)}, u32[]{:S(2)}, u32[]{:S(2)}) collective-permute-start(bf16[256,256]{1,0:T(8,128)(2,1)S(1)} %assemble.1.grid_ref), channel_id=1, source_target_pairs={{0,16},{8,24},{16,0},{24,8},{1,17},{9,25},{17,1},{25,9},{2,18},{10... | collective-permute-start | bytes 393224 | tf_op jit(solution)/shard_map/ppermute | solution.py:480

commit v2 on v0

--- a/solution.py
+++ b/solution.py
@@ -307,27 +307,26 @@
     )(mine, other, potential)
 
 
-def first_functions_kernel(j, mine_ref, other_ref, basis_ref, out_ref, both_ref):
+def first_functions_kernel(leave, mine_ref, other_ref, basis_ref, *refs):
+    outs, both_ref = refs[:-1], refs[-1]
     core = lax.axis_index("narrow") % 2
     rows = mine_ref.shape[0]
     mine, other = mine_ref[...].astype(F32), other_ref[...].astype(F32)
     both_ref[:rows] = jnp.where(core == 0, mine, other).astype(BF16)
     both_ref[rows:] = jnp.where(core == 0, other, mine).astype(BF16)
-    out_ref[...] = dot_turned(both_ref[...], basis_ref[j]).astype(BF16)
-
-
-def first_functions(mine, other, where):
-    basis, j = where
+    for j, out in zip(leave, outs):
+        out[...] = dot_turned(both_ref[...], basis_ref[j]).astype(BF16)
+
+
+def first_functions(leave, mine, other, basis):
     rows, points = mine.shape
     columns = basis.shape[1]
     return call(
-        functools.partial(first_functions_kernel, j),
+        functools.partial(first_functions_kernel, leave),
         "functions_first",
-        (array((2 * rows, columns), BF16), array((2 * rows, points), BF16)),
+        (array((2 * rows, columns), BF16),) * len(leave) + (array((2 * rows, points), BF16),),
         [VMEM] * 3,
-        (VMEM, VMEM),
-        flops=4 * rows * points * columns,
-        moved=2 * MIB,
+        (VMEM,) * (len(leave) + 1),
     )(mine, other, basis)
 
 
@@ -372,33 +371,26 @@
     )(*parts)
 
 
-def own_kernel(wide, pad_ref, rolled_ref, grid_ref, coeff_ref, row_ref, column_ref, out_ref):
+def diagonal_kernel(pad_ref, coeff_ref, row_ref, column_ref, out_ref):
     slots = pad_ref.shape[0]
-    width = rolled_ref.shape[0] // slots
-    me = lax.axis_index("wide")
-    own = rolled_ref.shape[1] // wide
-    start = pl.multiple_of(me * own, own)
-    out_ref[...] = dot(rolled_ref[:, pl.ds(start, own)], grid_ref[...])
+    width = coeff_ref.shape[0] // slots
     row = lax.broadcasted_iota(jnp.int32, (width, out_ref.shape[1]), 0)
     for s in range(slots):
         rows = slice(s * width, (s + 1) * width)
         energy = row_ref[rows, :] + column_ref[...]
         diagonal = energy * coeff_ref[rows, :].astype(F32)
-        out_ref[rows, :] += jnp.where(row < width - pad_ref[s], diagonal, 0.0)
-
-
-def backward_own(wide, pad, rolled, grid, coeff, row_energy, column_energy):
+        out_ref[rows, :] = jnp.where(row < width - pad_ref[s], diagonal, 0.0)
+
+
+def diagonal(pad, coeff, row_energy, column_energy):
     smem = pl.BlockSpec(memory_space=pltpu.SMEM)
-    rows, columns = coeff.shape
-    return call(
-        functools.partial(own_kernel, wide),
-        "backward_own",
+    return call(
+        diagonal_kernel,
+        "diagonal",
         array(coeff.shape, F32),
-        [smem] + [VMEM] * 5,
-        VMEM,
-        flops=2 * rows * columns * rolled.shape[1] // wide,
-        moved=4 * MIB,
-    )(pad, rolled, grid, coeff, row_energy[:, None], column_energy[None, :])
+        [smem] + [VMEM] * 3,
+        VMEM,
+    )(pad, coeff, row_energy[:, None], column_energy[None, :])
 
 
 def more_kernel(wide, k, total_ref, rolled_ref, grid_ref, out_ref):
@@ -500,17 +492,14 @@
     mine, theirs = last_points(total, xs[visits[-1]], where[visits[-1]])
     acted = act(mine, exchange(theirs, 1, narrow, "narrow"), pot)
     other = exchange(acted, 1, narrow, "narrow")
-    leave = list(range(1, chips))
-    block, both = first_functions(acted, other, where[leave[0]])
-    blocks = {leave[0]: exchange(block, 2 * leave[0], narrow, "narrow")}
-    for j in leave[1:]:
-        blocks[j] = exchange(functions(both, where[j]), 2 * j, narrow, "narrow")
+    leave = list(reversed(range(1, chips)))
+    *out, both = first_functions(leave, acted, other, basis)
+    blocks = {j: exchange(out[i], 2 * j, narrow, "narrow") for i, j in enumerate(leave)}
     grid = assemble([functions(both, where[0])] + [blocks[j] for j in range(1, chips)])
     steps = [wide - 1] + order
     grids = {k: exchange(grid, k, wide, "wide") for k in steps}
-    total = backward_own(
-        wide, block_pad, rolled, grid, coeff, groupb_row_energy, groupa_energy
-    )
+    total = diagonal(block_pad, coeff, groupb_row_energy, groupa_energy)
+    total = backward_more(wide, 0, total, rolled, grid)
     for k in steps[:-1]:
         total = backward_more(wide, k, total, rolled, grids[k])
     return backward_end(wide, steps[-1], total, rolled, grids[steps[-1]])

time: 43.7 us -> 43.6 us (level)
    pallas_call x3 -> x1, Pallas kernels: 1.33 us -> 0.44 us  [functions(): call(functools.partial(functions_kernel, j), 'functions_more', array((row...]
    pallas_call x2, Pallas kernels: 1.36 us -> 1.83 us  [the longest x1 1.07 us: first_functions(): call(functools.partial(first_functions_kernel, leave), 'functions_first',...]
    pallas_call x2 -> x3, Pallas kernels: 1.5 us -> 1.8 us  [backward_more(): call(functools.partial(more_kernel, wide, k), 'backward_more', array(tota...]
  transfers between devices with their start and end apart: 16 -> 16, of which waited for: 10 -> 9; matrix products, arithmetic and copies ran while one was open for 1% -> 1% of each run, Pallas kernels for 11% -> 12%
where the time goes in v2:
time: 43.6 us; the launch traced here: 43.4 us
  starting transfers between devices  20.7 us (47%)
  waiting for transfers between devices  11.7 us (27%)
  Pallas kernels  10.5 us (24%)
    ppermute x16, starting transfers between devices, exchange(): return lax.ppermute(value, axis, [(i, i ^ step) for i in range(size)])  20.7 us
    ppermute x16, waiting for transfers between devices, exchange(): return lax.ppermute(value, axis, [(i, i ^ step) for i in range(size)])  11.7 us
    pallas_call x1, Pallas kernels, first(): call(functools.partial(first_kernel, wide, chips), 'forward_first', (arra...  2.66 us
    pallas_call x3, Pallas kernels, backward_more(): call(functools.partial(more_kernel, wide, k), 'backward_more', array(tota...  1.8 us
    pallas_call x1, Pallas kernels, backward_end(): call(functools.partial(end_kernel, wide, k), 'backward_end', array(total....  1.32 us
    pallas_call x1, Pallas kernels, first_functions(): call(functools.partial(first_functions_kernel, leave), 'functions_first',...  1.07 us
  transfers between devices with their start and end apart: 16, of which 9 were waited for; matrix products, arithmetic and copies ran while one was open for 1% of the time, Pallas kernels for 12%

profile of v2, /device:TPU:0, one launch (start us, length us, event | category | flops | bytes accessed | tf_op | source)
XLA Modules:
  0.0 43.4 jit_solution(17471547193844329546)
XLA Ops:
  0.0 2.7 %forward_first.1 = (bf16[256,256]{1,0:T(8,128)(2,1)S(1)}, bf16[256,1024]{1,0:T(8,128)(2,1)S(1)}, bf16[1024,1024]{1,0:T(8,128)(2,1)S(1)}, bf16[4,256,2048]{2,1,0:T(8,128)(2,1)S(1)}, f32[32,2048]{1,0:T(8,128)S(1)}) custom-call(s32[16]{0:T(128)} %level_hbm.1, s32[16]{0:T(128)} %pad_hbm.1, s32[16]{0:T(128)} %shift_hbm.1, bf16[1024,256]{1,0:T(8,128)(2,1)} %coeff_hbm.1, ...), custom_call_target="tpu_custom_call" | custom-call | flops 134217728 | bytes 4194304 | tf_op jit(solution)/shard_map/forward_first/pallas_call | solution.py:149
  2.7 4.0 %collective-permute-start = (bf16[256,256]{1,0:T(8,128)(2,1)S(1)}, bf16[256,256]{1,0:T(8,128)(2,1)S(1)}, u32[]{:S(2)}, u32[]{:S(2)}) collective-permute-start(bf16[256,256]{1,0:T(8,128)(2,1)S(1)} %get-tuple-element.26), channel_id=1, source_target_pairs={{0,24},{8,16},{16,8},{24,0},{1,25},{9,17},{17,9},{25,1},{2,26},{10... | collective-permute-start | bytes 393224 | tf_op jit(solution)/shard_map/ppermute | solution.py:446
  7.0 0.6 %collective-permute-start.4 = (bf16[128,256]{1,0:T(8,128)(2,1)S(1)}, bf16[128,256]{1,0:T(8,128)(2,1)S(1)}, u32[]{:S(2)}, u32[]{:S(2)}) collective-permute-start(bf16[128,256]{1,0:T(8,128)(2,1)S(1)} %get-tuple-element.32), channel_id=1, source_target_pairs={{0,16},{8,24},{16,0},{24,8},{1,17},{9,25},{17,1},{25,9},{2,18},{10... | collective-permute-start | bytes 196616 | tf_op jit(solution)/shard_map/ppermute | solution.py:446
  8.1 2.0 %collective-permute-start.2 = (bf16[128,256]{1,0:T(8,128)(2,1)S(1)}, bf16[128,256]{1,0:T(8,128)(2,1)S(1)}, u32[]{:S(2)}, u32[]{:S(2)}) collective-permute-start(bf16[128,256]{1,0:T(8,128)(2,1)S(1)} %get-tuple-element.28), channel_id=1, source_target_pairs={{0,16},{8,24},{16,0},{24,8},{1,17},{9,25},{17,1},{25,9},{2,18},{10... | collective-permute-start | bytes 196616 | tf_op jit(solution)/shard_map/ppermute | solution.py:446
  10.1 1.5 %collective-permute-start.1 = (bf16[128,256]{1,0:T(8,128)(2,1)S(1)}, bf16[128,256]{1,0:T(8,128)(2,1)S(1)}, u32[]{:S(2)}, u32[]{:S(2)}) collective-permute-start(bf16[128,256]{1,0:T(8,128)(2,1)S(1)} %get-tuple-element.27), channel_id=1, source_target_pairs={{0,8},{8,0},{16,24},{24,16},{1,9},{9,1},{17,25},{25,17},{2,10},{10... | collective-permute-start | bytes 196616 | tf_op jit(solution)/shard_map/ppermute | solution.py:446
  12.1 0.7 %collective-permute-done.3.refs_0_ = bf16[128,256]{1,0:T(8,128)(2,1)S(1)} collective-permute-done((bf16[128,256]{1,0:T(8,128)(2,1)S(1)}, bf16[128,256]{1,0:T(8,128)(2,1)S(1)}, u32[]{:S(2)}, u32[]{:S(2)}) %collective-permute-start.3) | collective-permute-done | bytes 65568 | tf_op jit(solution)/shard_map/ppermute | solution.py:446
  12.8 2.7 %collective-permute-start.5 = (bf16[64,256]{1,0:T(8,128)(2,1)S(1)}, bf16[64,256]{1,0:T(8,128)(2,1)S(1)}, u32[]{:S(2)}, u32[]{:S(2)}) collective-permute-start(bf16[64,256]{1,0:T(8,128)(2,1)S(1)} %get-tuple-element.33), channel_id=1, source_target_pairs={{0,4},{1,5},{2,6},{3,7},{4,0},{5,1},{6,2},{7,3},{8,12},{9,13},{10,... | collective-permute-start | bytes 98312 | tf_op jit(solution)/shard_map/ppermute | solution.py:446
  15.5 1.3 %collective-permute-start.6 = (bf16[64,256]{1,0:T(8,128)(2,1)S(1)}, bf16[64,256]{1,0:T(8,128)(2,1)S(1)}, u32[]{:S(2)}, u32[]{:S(2)}) collective-permute-start(bf16[64,256]{1,0:T(8,128)(2,1)S(1)} %get-tuple-element.34), channel_id=1, source_target_pairs={{0,6},{1,7},{2,4},{3,5},{4,2},{5,3},{6,0},{7,1},{8,14},{9,15},{10,... | collective-permute-start | bytes 98312 | tf_op jit(solution)/shard_map/ppermute | solution.py:446
  18.2 3.0 %collective-permute-done.6.x_ref = bf16[64,256]{1,0:T(8,128)(2,1)S(1)} collective-permute-done((bf16[64,256]{1,0:T(8,128)(2,1)S(1)}, bf16[64,256]{1,0:T(8,128)(2,1)S(1)}, u32[]{:S(2)}, u32[]{:S(2)}) %collective-permute-start.6) | collective-permute-done | bytes 32800 | tf_op jit(solution)/shard_map/ppermute | solution.py:446
  21.9 1.5 %collective-permute-done.8.other_ref = f32[32,2048]{1,0:T(8,128)S(1)} collective-permute-done((f32[32,2048]{1,0:T(8,128)S(1)}, f32[32,2048]{1,0:T(8,128)S(1)}, u32[]{:S(2)}, u32[]{:S(2)}) %collective-permute-start.8) | collective-permute-done | bytes 262176 | tf_op jit(solution)/shard_map/ppermute | solution.py:446
  23.7 1.2 %collective-permute-done.9.other_ref = bf16[32,2048]{1,0:T(8,128)(2,1)S(1)} collective-permute-done((bf16[32,2048]{1,0:T(8,128)(2,1)S(1)}, bf16[32,2048]{1,0:T(8,128)(2,1)S(1)}, u32[]{:S(2)}, u32[]{:S(2)}) %collective-permute-start.9) | collective-permute-done | bytes 131104 | tf_op jit(solution)/shard_map/ppermute | solution.py:446
  24.9 1.1 %functions_first.1 = (bf16[64,256]{1,0:T(8,128)(2,1)S(1)}, bf16[64,256]{1,0:T(8,128)(2,1)S(1)}, bf16[64,256]{1,0:T(8,128)(2,1)S(1)}, bf16[64,2048]{1,0:T(8,128)(2,1)S(1)}) custom-call(bf16[32,2048]{1,0:T(8,128)(2,1)S(1)} %act.1.mine_ref, bf16[32,2048]{1,0:T(8,128)(2,1)S(1)} %collective-permute-done.9.other_ref, ...), custom_call_target="tpu_custom_call" | custom-call | tf_op jit(solution)/shard_map/functions_first/pallas_call | solution.py:324
  26.1 2.4 %collective-permute-start.11 = (bf16[64,256]{1,0:T(8,128)(2,1)S(1)}, bf16[64,256]{1,0:T(8,128)(2,1)S(1)}, u32[]{:S(2)}, u32[]{:S(2)}) collective-permute-start(bf16[64,256]{1,0:T(8,128)(2,1)S(1)} %get-tuple-element.41), channel_id=1, source_target_pairs={{0,4},{1,5},{2,6},{3,7},{4,0},{5,1},{6,2},{7,3},{8,12},{9,13},{10,... | collective-permute-start | bytes 98312 | tf_op jit(solution)/shard_map/ppermute | solution.py:446
  28.5 2.0 %collective-permute-start.12 = (bf16[64,256]{1,0:T(8,128)(2,1)S(1)}, bf16[64,256]{1,0:T(8,128)(2,1)S(1)}, u32[]{:S(2)}, u32[]{:S(2)}) collective-permute-start(bf16[64,256]{1,0:T(8,128)(2,1)S(1)} %get-tuple-element.42), channel_id=1, source_target_pairs={{0,6},{1,7},{2,4},{3,5},{4,2},{5,3},{6,0},{7,1},{8,14},{9,15},{10,... | collective-permute-start | bytes 98312 | tf_op jit(solution)/shard_map/ppermute | solution.py:446
  30.5 0.4 %functions_more.1.refs_0_ = bf16[64,256]{1,0:T(8,128)(2,1)S(1)} custom-call(bf16[64,2048]{1,0:T(8,128)(2,1)S(1)} %get-tuple-element.39.both_ref, bf16[4,256,2048]{2,1,0:T(8,128)(2,1)S(1)} %get-tuple-element.30.basis_ref), custom_call_target="tpu_custom_call" | custom-call | flops 67108864 | bytes 2097152 | tf_op jit(solution)/shard_map/functions_more/pallas_call | solution.py:341
  30.9 0.6 %collective-permute-done.11.refs_2_ = bf16[64,256]{1,0:T(8,128)(2,1)S(1)} collective-permute-done((bf16[64,256]{1,0:T(8,128)(2,1)S(1)}, bf16[64,256]{1,0:T(8,128)(2,1)S(1)}, u32[]{:S(2)}, u32[]{:S(2)}) %collective-permute-start.11) | collective-permute-done | bytes 32800 | tf_op jit(solution)/shard_map/ppermute | solution.py:446
  31.5 2.6 %collective-permute-done.12.refs_3_ = bf16[64,256]{1,0:T(8,128)(2,1)S(1)} collective-permute-done((bf16[64,256]{1,0:T(8,128)(2,1)S(1)}, bf16[64,256]{1,0:T(8,128)(2,1)S(1)}, u32[]{:S(2)}, u32[]{:S(2)}) %collective-permute-start.12) | collective-permute-done | bytes 32800 | tf_op jit(solution)/shard_map/ppermute | solution.py:446
  34.2 1.6 %collective-permute-start.13 = (bf16[256,256]{1,0:T(8,128)(2,1)S(1)}, bf16[256,256]{1,0:T(8,128)(2,1)}, u32[]{:S(2)}, u32[]{:S(2)}) collective-permute-start(bf16[256,256]{1,0:T(8,128)(2,1)S(1)} %assemble.1.grid_ref), channel_id=1, source_target_pairs={{0,24},{8,16},{16,8},{24,0},{1,25},{9,17},{17,9},{25,1},{2,26},{10... | collective-permute-start | bytes 393224 | tf_op jit(solution)/shard_map/ppermute | solution.py:446
  35.8 1.0 %collective-permute-start.14 = (bf16[256,256]{1,0:T(8,128)(2,1)S(1)}, bf16[256,256]{1,0:T(8,128)(2,1)S(1)}, u32[]{:S(2)}, u32[]{:S(2)}) collective-permute-start(bf16[256,256]{1,0:T(8,128)(2,1)S(1)} %assemble.1.grid_ref), channel_id=1, source_target_pairs={{0,8},{8,0},{16,24},{24,16},{1,9},{9,1},{17,25},{25,17},{2,10},{10... | collective-permute-start | bytes 393224 | tf_op jit(solution)/shard_map/ppermute | solution.py:446
  36.7 1.0 %collective-permute-start.15 = (bf16[256,256]{1,0:T(8,128)(2,1)S(1)}, bf16[256,256]{1,0:T(8,128)(2,1)S(1)}, u32[]{:S(2)}, u32[]{:S(2)}) collective-permute-start(bf16[256,256]{1,0:T(8,128)(2,1)S(1)} %assemble.1.grid_ref), channel_id=1, source_target_pairs={{0,16},{8,24},{16,0},{24,8},{1,17},{9,25},{17,1},{25,9},{2,18},{10... | collective-permute-start | bytes 393224 | tf_op jit(solution)/shard_map/ppermute | solution.py:446
  38.0 0.8 %diagonal.1.total_ref = f32[1024,256]{1,0:T(8,128)S(1)} custom-call(s32[16]{0:T(128)S(1)} %copy-done.1, bf16[1024,256]{1,0:T(8,128)(2,1)S(1)} %copy-done, f32[1024,1]{1,0:T(8,128)S(1)} %copy.10.row_ref, f32[1,256]{1,0:T(1,128)S(1)} %bitcast.3), custom_call_target="tpu_custom_call" | custom-call | tf_op jit(solution)/shard_map/diagonal/pallas_call | solution.py:387
  39.1 1.5 %collective-permute-done.13.grid_ref = bf16[256,256]{1,0:T(8,128)(2,1)} collective-permute-done((bf16[256,256]{1,0:T(8,128)(2,1)S(1)}, bf16[256,256]{1,0:T(8,128)(2,1)}, u32[]{:S(2)}, u32[]{:S(2)}) %collective-permute-start.13) | collective-permute-done | bytes 131104 | tf_op jit(solution)/shard_map/ppermute | solution.py:446
  40.6 1.2 %backward_more.4.total_ref = f32[1024,256]{1,0:T(8,128)S(1)} custom-call(f32[1024,256]{1,0:T(8,128)S(1)} %backward_more.3.total_ref, bf16[1024,1024]{1,0:T(8,128)(2,1)S(1)} %get-tuple-element.24.rolled_ref, bf16[256,256]{1,0:T(8,128)(2,1)} %collective-permute-done.13.grid_ref), custom_call_target="tpu_custom_call" | custom-call | flops 134217728 | bytes 3145728 | tf_op jit(solution)/shard_map/backward_more/pallas_call | solution.py:404
  42.1 1.3 %backward_end.1 = f32[1024,256]{1,0:T(8,128)} custom-call(f32[1024,256]{1,0:T(8,128)S(1)} %backward_more.5.total_ref, bf16[1024,1024]{1,0:T(8,128)(2,1)S(1)} %get-tuple-element.24.rolled_ref, bf16[256,256]{1,0:T(8,128)(2,1)S(1)} %collective-permute-done.15.grid_ref), custom_call_target="tpu_custom_call" | custom-call | flops 134217728 | bytes 4194304 | tf_op jit(solution)/shard_map/backward_end/pallas_call | solution.py:433
  (36 shorter events, 4.6 us)
Async XLA Ops:
  2.7 10.1 %collective-permute-start = (bf16[256,256]{1,0:T(8,128)(2,1)S(1)}, bf16[256,256]{1,0:T(8,128)(2,1)S(1)}, u32[]{:S(2)}, u32[]{:S(2)}) collective-permute-start(bf16[256,256]{1,0:T(8,128)(2,1)S(1)} %get-tuple-element.26), channel_id=1, source_target_pairs={{0,24},{8,16},{16,8},{24,0},{1,25},{9,17},{17,9},{25,1},{2,26},{10... | collective-permute-start | bytes 393224 | tf_op jit(solution)/shard_map/ppermute | solution.py:446
  7.0 5.1 %collective-permute-start.4 = (bf16[128,256]{1,0:T(8,128)(2,1)S(1)}, bf16[128,256]{1,0:T(8,128)(2,1)S(1)}, u32[]{:S(2)}, u32[]{:S(2)}) collective-permute-start(bf16[128,256]{1,0:T(8,128)(2,1)S(1)} %get-tuple-element.32), channel_id=1, source_target_pairs={{0,16},{8,24},{16,0},{24,8},{1,17},{9,25},{17,1},{25,9},{2,18},{10... | collective-permute-start | bytes 196616 | tf_op jit(solution)/shard_map/ppermute | solution.py:446
  7.9 4.8 %collective-permute-start.3 = (bf16[128,256]{1,0:T(8,128)(2,1)S(1)}, bf16[128,256]{1,0:T(8,128)(2,1)S(1)}, u32[]{:S(2)}, u32[]{:S(2)}) collective-permute-start(bf16[128,256]{1,0:T(8,128)(2,1)S(1)} %get-tuple-element.31), channel_id=1, source_target_pairs={{0,8},{8,0},{16,24},{24,16},{1,9},{9,1},{17,25},{25,17},{2,10},{10... | collective-permute-start | bytes 196616 | tf_op jit(solution)/shard_map/ppermute | solution.py:446
  8.1 8.7 %collective-permute-start.2 = (bf16[128,256]{1,0:T(8,128)(2,1)S(1)}, bf16[128,256]{1,0:T(8,128)(2,1)S(1)}, u32[]{:S(2)}, u32[]{:S(2)}) collective-permute-start(bf16[128,256]{1,0:T(8,128)(2,1)S(1)} %get-tuple-element.28), channel_id=1, source_target_pairs={{0,16},{8,24},{16,0},{24,8},{1,17},{9,25},{17,1},{25,9},{2,18},{10... | collective-permute-start | bytes 196616 | tf_op jit(solution)/shard_map/ppermute | solution.py:446
  10.1 6.8 %collective-permute-start.1 = (bf16[128,256]{1,0:T(8,128)(2,1)S(1)}, bf16[128,256]{1,0:T(8,128)(2,1)S(1)}, u32[]{:S(2)}, u32[]{:S(2)}) collective-permute-start(bf16[128,256]{1,0:T(8,128)(2,1)S(1)} %get-tuple-element.27), channel_id=1, source_target_pairs={{0,8},{8,0},{16,24},{24,16},{1,9},{9,1},{17,25},{25,17},{2,10},{10... | collective-permute-start | bytes 196616 | tf_op jit(solution)/shard_map/ppermute | solution.py:446
  12.8 5.1 %collective-permute-start.5 = (bf16[64,256]{1,0:T(8,128)(2,1)S(1)}, bf16[64,256]{1,0:T(8,128)(2,1)S(1)}, u32[]{:S(2)}, u32[]{:S(2)}) collective-permute-start(bf16[64,256]{1,0:T(8,128)(2,1)S(1)} %get-tuple-element.33), channel_id=1, source_target_pairs={{0,4},{1,5},{2,6},{3,7},{4,0},{5,1},{6,2},{7,3},{8,12},{9,13},{10,... | collective-permute-start | bytes 98312 | tf_op jit(solution)/shard_map/ppermute | solution.py:446
  15.5 5.7 %collective-permute-start.6 = (bf16[64,256]{1,0:T(8,128)(2,1)S(1)}, bf16[64,256]{1,0:T(8,128)(2,1)S(1)}, u32[]{:S(2)}, u32[]{:S(2)}) collective-permute-start(bf16[64,256]{1,0:T(8,128)(2,1)S(1)} %get-tuple-element.34), channel_id=1, source_target_pairs={{0,6},{1,7},{2,4},{3,5},{4,2},{5,3},{6,0},{7,1},{8,14},{9,15},{10,... | collective-permute-start | bytes 98312 | tf_op jit(solution)/shard_map/ppermute | solution.py:446
  16.9 4.6 %collective-permute-start.7 = (bf16[64,256]{1,0:T(8,128)(2,1)S(1)}, bf16[64,256]{1,0:T(8,128)(2,1)S(1)}, u32[]{:S(2)}, u32[]{:S(2)}) collective-permute-start(bf16[64,256]{1,0:T(8,128)(2,1)S(1)} %get-tuple-element.35), channel_id=1, source_target_pairs={{0,2},{1,3},{2,0},{3,1},{4,6},{5,7},{6,4},{7,5},{8,10},{9,11},{10,... | collective-permute-start | bytes 98312 | tf_op jit(solution)/shard_map/ppermute | solution.py:446
  21.8 1.6 %collective-permute-start.8 = (f32[32,2048]{1,0:T(8,128)S(1)}, f32[32,2048]{1,0:T(8,128)S(1)}, u32[]{:S(2)}, u32[]{:S(2)}) collective-permute-start(f32[32,2048]{1,0:T(8,128)S(1)} %get-tuple-element.37), channel_id=1, source_target_pairs={{0,1},{1,0},{2,3},{3,2},{4,5},{5,4},{6,7},{7,6},{8,9},{9,8},{10,11... | collective-permute-start | bytes 786440 | tf_op jit(solution)/shard_map/ppermute | solution.py:446
  23.5 14.3 %copy-start.3 = (f32[1024]{0:T(1024)S(1)}, f32[1024]{0:T(1024)}, u32[]{:S(2)}) copy-start(f32[1024]{0:T(1024)} %param.10) | copy-start | bytes 12292
  23.5 14.5 %copy-start = (bf16[1024,256]{1,0:T(8,128)(2,1)S(1)}, bf16[1024,256]{1,0:T(8,128)(2,1)}, u32[]{:S(2)}) copy-start(bf16[1024,256]{1,0:T(8,128)(2,1)} %coeff_hbm.1) | copy-start | bytes 1572868
  23.5 14.5 %copy-start.1 = (s32[16]{0:T(128)S(1)}, s32[16]{0:T(128)}, u32[]{:S(2)}) copy-start(s32[16]{0:T(128)} %pad_hbm.1) | copy-start | bytes 196
  23.5 14.5 %copy-start.2 = (f32[256]{0:T(256)S(1)}, f32[256]{0:T(256)}, u32[]{:S(2)}) copy-start(f32[256]{0:T(256)} %param.11) | copy-start | bytes 3076
  23.5 1.4 %collective-permute-start.9 = (bf16[32,2048]{1,0:T(8,128)(2,1)S(1)}, bf16[32,2048]{1,0:T(8,128)(2,1)S(1)}, u32[]{:S(2)}, u32[]{:S(2)}) collective-permute-start(bf16[32,2048]{1,0:T(8,128)(2,1)S(1)} %act.1.mine_ref), channel_id=1, source_target_pairs={{0,1},{1,0},{2,3},{3,2},{4,5},{5,4},{6,7},{7,6},{8,9},{9,8},{10,11... | collective-permute-start | bytes 393224 | tf_op jit(solution)/shard_map/ppermute | solution.py:446
  26.0 4.9 %collective-permute-start.10 = (bf16[64,256]{1,0:T(8,128)(2,1)S(1)}, bf16[64,256]{1,0:T(8,128)(2,1)S(1)}, u32[]{:S(2)}, u32[]{:S(2)}) collective-permute-start(bf16[64,256]{1,0:T(8,128)(2,1)S(1)} %get-tuple-element.40), channel_id=1, source_target_pairs={{0,2},{1,3},{2,0},{3,1},{4,6},{5,7},{6,4},{7,5},{8,10},{9,11},{10,... | collective-permute-start | bytes 98312 | tf_op jit(solution)/shard_map/ppermute | solution.py:446
  26.1 5.4 %collective-permute-start.11 = (bf16[64,256]{1,0:T(8,128)(2,1)S(1)}, bf16[64,256]{1,0:T(8,128)(2,1)S(1)}, u32[]{:S(2)}, u32[]{:S(2)}) collective-permute-start(bf16[64,256]{1,0:T(8,128)(2,1)S(1)} %get-tuple-element.41), channel_id=1, source_target_pairs={{0,4},{1,5},{2,6},{3,7},{4,0},{5,1},{6,2},{7,3},{8,12},{9,13},{10,... | collective-permute-start | bytes 98312 | tf_op jit(solution)/shard_map/ppermute | solution.py:446
  28.5 5.7 %collective-permute-start.12 = (bf16[64,256]{1,0:T(8,128)(2,1)S(1)}, bf16[64,256]{1,0:T(8,128)(2,1)S(1)}, u32[]{:S(2)}, u32[]{:S(2)}) collective-permute-start(bf16[64,256]{1,0:T(8,128)(2,1)S(1)} %get-tuple-element.42), channel_id=1, source_target_pairs={{0,6},{1,7},{2,4},{3,5},{4,2},{5,3},{6,0},{7,1},{8,14},{9,15},{10,... | collective-permute-start | bytes 98312 | tf_op jit(solution)/shard_map/ppermute | solution.py:446
  34.2 6.4 %collective-permute-start.13 = (bf16[256,256]{1,0:T(8,128)(2,1)S(1)}, bf16[256,256]{1,0:T(8,128)(2,1)}, u32[]{:S(2)}, u32[]{:S(2)}) collective-permute-start(bf16[256,256]{1,0:T(8,128)(2,1)S(1)} %assemble.1.grid_ref), channel_id=1, source_target_pairs={{0,24},{8,16},{16,8},{24,0},{1,25},{9,17},{17,9},{25,1},{2,26},{10... | collective-permute-start | bytes 393224 | tf_op jit(solution)/shard_map/ppermute | solution.py:446
  35.8 6.0 %collective-permute-start.14 = (bf16[256,256]{1,0:T(8,128)(2,1)S(1)}, bf16[256,256]{1,0:T(8,128)(2,1)S(1)}, u32[]{:S(2)}, u32[]{:S(2)}) collective-permute-start(bf16[256,256]{1,0:T(8,128)(2,1)S(1)} %assemble.1.grid_ref), channel_id=1, source_target_pairs={{0,8},{8,0},{16,24},{24,16},{1,9},{9,1},{17,25},{25,17},{2,10},{10... | collective-permute-start | bytes 393224 | tf_op jit(solution)/shard_map/ppermute | solution.py:446
  36.7 5.3 %collective-permute-start.15 = (bf16[256,256]{1,0:T(8,128)(2,1)S(1)}, bf16[256,256]{1,0:T(8,128)(2,1)S(1)}, u32[]{:S(2)}, u32[]{:S(2)}) collective-permute-start(bf16[256,256]{1,0:T(8,128)(2,1)S(1)} %assemble.1.grid_ref), channel_id=1, source_target_pairs={{0,16},{8,24},{16,0},{24,8},{1,17},{9,25},{17,1},{25,9},{2,18},{10... | collective-permute-start | bytes 393224 | tf_op jit(solution)/shard_map/ppermute | solution.py:446

commit v3 on v2

--- a/solution.py
+++ b/solution.py
@@ -69,13 +69,13 @@
     pltpu.make_async_copy(source, target, sem).wait()
 
 
-def basis_pieces(basis_hbm, basis_ref):
-    chips, columns, _ = basis_ref.shape
+def basis_pieces(first, basis_hbm, basis_ref):
+    count, columns, _ = basis_ref.shape
     place = lax.axis_index("narrow")
     core, chip = place % 2, place // 2
     pairs = []
-    for j in range(chips):
-        start = pl.multiple_of(((chip ^ j) * 2 + core) * columns, columns)
+    for j in range(count):
+        start = pl.multiple_of(((chip ^ (first + j)) * 2 + core) * columns, columns)
         pairs.append((basis_hbm.at[pl.ds(start, columns)], basis_ref.at[j]))
     return pairs
 
@@ -119,7 +119,7 @@
     for n in range(levels):
         start_pieces(table_hbm.at[n], table_ref.at[n], 32, sems.at[3])
     start_pieces(coeff_hbm, coeff_ref, 128, sems.at[4])
-    pairs = basis_pieces(basis_hbm, basis_ref)
+    pairs = basis_pieces(0, basis_hbm, basis_ref)
     for j, (source, target) in enumerate(pairs):
         start_pieces(source, target, 64, sems.at[6 + j])
     start_pieces(potential_hbm, potential_ref, 8, sems.at[5])
@@ -153,7 +153,7 @@
             array((points // wide, columns), BF16),
             array((columns, rows), BF16),
             array((rows, points), BF16),
-            array((chips, columns, basis.shape[1]), BF16),
+            array((chips // 2, columns, basis.shape[1]), BF16),
             array(potential.shape, F32),
         ),
         [HBM] * 7,
@@ -189,22 +189,28 @@
     )(turned, rolled)
 
 
-def last_kernel(wide, turned_ref, rolled_ref, out_ref):
+def last_kernel(wide, turned_ref, rolled_ref, basis_hbm, out_ref, basis_ref, sems):
+    count = basis_ref.shape[0]
+    pairs = basis_pieces(count, basis_hbm, basis_ref)
+    for j, (source, target) in enumerate(pairs):
+        start_pieces(source, target, 64, sems.at[j])
     out_ref[...] = chunk_of(turned_ref, rolled_ref, wide, 0).T
-
-
-def last(wide, turned, rolled):
+    for j, (source, target) in enumerate(pairs):
+        wait_all(source, target, sems.at[j])
+
+
+def last(wide, chips, turned, rolled, basis):
     columns, rows = turned.shape
     own = rolled.shape[1] // wide
+    count = chips - chips // 2
     return call(
         functools.partial(last_kernel, wide),
         "forward_own",
-        array((own, columns), F32),
-        [VMEM] * 2,
-        VMEM,
-        flops=2 * rows * own * columns,
-        moved=MIB,
-    )(turned, rolled)
+        (array((own, columns), F32), array((count, columns, basis.shape[1]), BF16)),
+        [VMEM, VMEM, HBM],
+        (VMEM,) * 2,
+        [pltpu.SemaphoreType.DMA((count,))],
+    )(turned, rolled, in_hbm(basis))
 
 
 def combine_kernel(chips, first, mine_ref, whole_ref, *refs):
@@ -307,7 +313,7 @@
     )(mine, other, potential)
 
 
-def first_functions_kernel(leave, mine_ref, other_ref, basis_ref, *refs):
+def first_functions_kernel(leave, mine_ref, other_ref, basis_ref, more_ref, *refs):
     outs, both_ref = refs[:-1], refs[-1]
     core = lax.axis_index("narrow") % 2
     rows = mine_ref.shape[0]
@@ -315,19 +321,21 @@
     both_ref[:rows] = jnp.where(core == 0, mine, other).astype(BF16)
     both_ref[rows:] = jnp.where(core == 0, other, mine).astype(BF16)
     for j, out in zip(leave, outs):
-        out[...] = dot_turned(both_ref[...], basis_ref[j]).astype(BF16)
-
-
-def first_functions(leave, mine, other, basis):
+        half = basis_ref.shape[0]
+        block = basis_ref[j] if j < half else more_ref[j - half]
+        out[...] = dot_turned(both_ref[...], block).astype(BF16)
+
+
+def first_functions(leave, mine, other, basis, more):
     rows, points = mine.shape
     columns = basis.shape[1]
     return call(
         functools.partial(first_functions_kernel, leave),
         "functions_first",
         (array((2 * rows, columns), BF16),) * len(leave) + (array((2 * rows, points), BF16),),
-        [VMEM] * 3,
+        [VMEM] * 4,
         (VMEM,) * (len(leave) + 1),
-    )(mine, other, basis)
+    )(mine, other, basis, more)
 
 
 def functions_kernel(j, both_ref, basis_ref, out_ref):
@@ -436,14 +444,15 @@
         array(total.shape, F32),
         [VMEM] * 3,
         HBM,
-        [pltpu.VMEM(total.shape, F32), pltpu.SemaphoreType.DMA((16,))],
+        [pltpu.VMEM(total.shape, F32), pltpu.SemaphoreType.DMA((8,))],
         flops=2 * rows * columns * rolled.shape[1] // wide,
         moved=4 * MIB,
     )(total, rolled, grid)
 
 
 def exchange(value, step, size, axis):
-    return lax.ppermute(value, axis, [(i, i ^ step) for i in range(size)])
+    moved = lax.ppermute(value, axis, [(i, i ^ step) for i in range(size)])
+    return pltpu.with_memory_space_constraint(moved, pltpu.VMEM)
 
 
 def body(
@@ -475,11 +484,11 @@
         potential,
     )
     whole = exchange(whole, wide - 1, wide, "wide")
-    where = {j: (basis, j) for j in range(chips)}
     sent = {k: chunk(wide, chips, k, turned, rolled) for k in order}
     far_parts = [exchange(sent[k][0], k, wide, "wide") for k in order]
     near_parts = [exchange(sent[k][1], k, wide, "wide") for k in order]
-    mine = last(wide, turned, rolled)
+    mine, more = last(wide, chips, turned, rolled, basis_a)
+    where = {j: (basis, j) if j < half else (more, j - half) for j in range(chips)}
     pieces = combine(chips, half, mine, whole, far_parts)
     xs = {j: exchange(pieces[j - half], 2 * j, narrow, "narrow") for j in range(half, chips)}
     pieces = combine(chips, 0, mine, whole, near_parts)
@@ -493,7 +502,7 @@
     acted = act(mine, exchange(theirs, 1, narrow, "narrow"), pot)
     other = exchange(acted, 1, narrow, "narrow")
     leave = list(reversed(range(1, chips)))
-    *out, both = first_functions(leave, acted, other, basis)
+    *out, both = first_functions(leave, acted, other, basis, more)
     blocks = {j: exchange(out[i], 2 * j, narrow, "narrow") for i, j in enumerate(leave)}
     grid = assemble([functions(both, where[0])] + [blocks[j] for j in range(1, chips)])
     steps = [wide - 1] + order

time: 43.6 us -> 43.7 us (level)
  Pallas kernels: 10.5 us -> 11.4 us
  waiting for transfers between devices: 11.7 us -> 11 us
    pallas_call x1, Pallas kernels: 0.37 us -> 1.66 us  [last(): call(functools.partial(last_kernel, wide), 'forward_own', (array((own, co...]
    ppermute x16, waiting for transfers between devices: 11.7 us -> 11 us  [exchange(): moved = lax.ppermute(value, axis, [(i, i ^ step) for i in range(size)])]
  transfers between devices with their start and end apart: 16 -> 16, of which waited for: 9 -> 7; matrix products, arithmetic and copies ran while one was open for 1% -> 1% of each run, Pallas kernels for 12% -> 15%
where the time goes in v3:
time: 43.7 us; the launch traced here: 43.5 us
  starting transfers between devices  20.7 us (47%)
  Pallas kernels  11.4 us (26%)
  waiting for transfers between devices  11 us (25%)
    ppermute x16, starting transfers between devices, exchange(): moved = lax.ppermute(value, axis, [(i, i ^ step) for i in range(size)])  20.7 us
    ppermute x16, waiting for transfers between devices, exchange(): moved = lax.ppermute(value, axis, [(i, i ^ step) for i in range(size)])  11 us
    pallas_call x1, Pallas kernels, first(): call(functools.partial(first_kernel, wide, chips), 'forward_first', (arra...  2.33 us
    pallas_call x3, Pallas kernels, backward_more(): call(functools.partial(more_kernel, wide, k), 'backward_more', array(tota...  1.79 us
    pallas_call x1, Pallas kernels, last(): call(functools.partial(last_kernel, wide), 'forward_own', (array((own, co...  1.66 us
    pallas_call x1, Pallas kernels, backward_end(): call(functools.partial(end_kernel, wide, k), 'backward_end', array(total....  1.24 us
    pallas_call x1, Pallas kernels, first_functions(): call(functools.partial(first_functions_kernel, leave), 'functions_first',...  1.07 us
  transfers between devices with their start and end apart: 16, of which 7 were waited for; matrix products, arithmetic and copies ran while one was open for 1% of the time, Pallas kernels for 15%

profile of v3, /device:TPU:0, one launch (start us, length us, event | category | flops | bytes accessed | tf_op | source)
XLA Modules:
  0.0 43.5 jit_solution(2248055313941460358)
XLA Ops:
  0.0 2.3 %forward_first.1 = (bf16[256,256]{1,0:T(8,128)(2,1)S(1)}, bf16[256,1024]{1,0:T(8,128)(2,1)S(1)}, bf16[1024,1024]{1,0:T(8,128)(2,1)S(1)}, bf16[2,256,2048]{2,1,0:T(8,128)(2,1)S(1)}, f32[32,2048]{1,0:T(8,128)S(1)}) custom-call(s32[16]{0:T(128)} %level_hbm.1, s32[16]{0:T(128)} %pad_hbm.1, s32[16]{0:T(128)} %shift_hbm.1, bf16[1024,256]{1,0:T(8,128)(2,1)} %coeff_hbm.1, ...), custom_call_target="tpu_custom_call" | custom-call | flops 134217728 | bytes 4194304 | tf_op jit(solution)/shard_map/forward_first/pallas_call | solution.py:149
  2.3 4.0 %collective-permute-start = (bf16[256,256]{1,0:T(8,128)(2,1)S(1)}, bf16[256,256]{1,0:T(8,128)(2,1)S(1)}, u32[]{:S(2)}, u32[]{:S(2)}) collective-permute-start(bf16[256,256]{1,0:T(8,128)(2,1)S(1)} %get-tuple-element.29), channel_id=1, source_target_pairs={{0,24},{8,16},{16,8},{24,0},{1,25},{9,17},{17,9},{25,1},{2,26},{10... | collective-permute-start | bytes 393224 | tf_op jit(solution)/shard_map/ppermute | solution.py:454
  6.7 0.6 %collective-permute-start.4 = (bf16[128,256]{1,0:T(8,128)(2,1)S(1)}, bf16[128,256]{1,0:T(8,128)(2,1)S(1)}, u32[]{:S(2)}, u32[]{:S(2)}) collective-permute-start(bf16[128,256]{1,0:T(8,128)(2,1)S(1)} %get-tuple-element.35), channel_id=1, source_target_pairs={{0,16},{8,24},{16,0},{24,8},{1,17},{9,25},{17,1},{25,9},{2,18},{10... | collective-permute-start | bytes 196616 | tf_op jit(solution)/shard_map/ppermute | solution.py:454
  7.8 2.0 %collective-permute-start.2 = (bf16[128,256]{1,0:T(8,128)(2,1)S(1)}, bf16[128,256]{1,0:T(8,128)(2,1)S(1)}, u32[]{:S(2)}, u32[]{:S(2)}) collective-permute-start(bf16[128,256]{1,0:T(8,128)(2,1)S(1)} %get-tuple-element.31), channel_id=1, source_target_pairs={{0,16},{8,24},{16,0},{24,8},{1,17},{9,25},{17,1},{25,9},{2,18},{10... | collective-permute-start | bytes 196616 | tf_op jit(solution)/shard_map/ppermute | solution.py:454
  9.7 1.5 %collective-permute-start.1 = (bf16[128,256]{1,0:T(8,128)(2,1)S(1)}, bf16[128,256]{1,0:T(8,128)(2,1)S(1)}, u32[]{:S(2)}, u32[]{:S(2)}) collective-permute-start(bf16[128,256]{1,0:T(8,128)(2,1)S(1)} %get-tuple-element.30), channel_id=1, source_target_pairs={{0,8},{8,0},{16,24},{24,16},{1,9},{9,1},{17,25},{25,17},{2,10},{10... | collective-permute-start | bytes 196616 | tf_op jit(solution)/shard_map/ppermute | solution.py:454
  11.2 1.7 %forward_own.1 = (f32[256,256]{1,0:T(8,128)S(1)}, bf16[2,256,2048]{2,1,0:T(8,128)(2,1)S(1)}) custom-call(bf16[256,1024]{1,0:T(8,128)(2,1)S(1)} %get-tuple-element.27.turned_ref, bf16[1024,1024]{1,0:T(8,128)(2,1)S(1)} %get-tuple-element.26.rolled_ref, bf16[2048,2048]{1,0:T(8,128)(2,1)} %basis_hbm.3), custom_call_target="tpu_custom_call" | custom-call | tf_op jit(solution)/shard_map/forward_own/pallas_call | solution.py:206
  13.0 2.7 %collective-permute-start.5 = (bf16[64,256]{1,0:T(8,128)(2,1)S(1)}, bf16[64,256]{1,0:T(8,128)(2,1)S(1)}, u32[]{:S(2)}, u32[]{:S(2)}) collective-permute-start(bf16[64,256]{1,0:T(8,128)(2,1)S(1)} %get-tuple-element.36), channel_id=1, source_target_pairs={{0,4},{1,5},{2,6},{3,7},{4,0},{5,1},{6,2},{7,3},{8,12},{9,13},{10,... | collective-permute-start | bytes 98312 | tf_op jit(solution)/shard_map/ppermute | solution.py:454
  15.6 1.4 %collective-permute-start.6 = (bf16[64,256]{1,0:T(8,128)(2,1)S(1)}, bf16[64,256]{1,0:T(8,128)(2,1)S(1)}, u32[]{:S(2)}, u32[]{:S(2)}) collective-permute-start(bf16[64,256]{1,0:T(8,128)(2,1)S(1)} %get-tuple-element.38), channel_id=1, source_target_pairs={{0,6},{1,7},{2,4},{3,5},{4,2},{5,3},{6,0},{7,1},{8,14},{9,15},{10,... | collective-permute-start | bytes 98312 | tf_op jit(solution)/shard_map/ppermute | solution.py:454
  17.7 0.6 %collective-permute-done.5.x_ref = bf16[64,256]{1,0:T(8,128)(2,1)S(1)} collective-permute-done((bf16[64,256]{1,0:T(8,128)(2,1)S(1)}, bf16[64,256]{1,0:T(8,128)(2,1)S(1)}, u32[]{:S(2)}, u32[]{:S(2)}) %collective-permute-start.5) | collective-permute-done | bytes 32800 | tf_op jit(solution)/shard_map/ppermute | solution.py:454
  18.5 2.9 %collective-permute-done.6.x_ref = bf16[64,256]{1,0:T(8,128)(2,1)S(1)} collective-permute-done((bf16[64,256]{1,0:T(8,128)(2,1)S(1)}, bf16[64,256]{1,0:T(8,128)(2,1)S(1)}, u32[]{:S(2)}, u32[]{:S(2)}) %collective-permute-start.6) | collective-permute-done | bytes 32800 | tf_op jit(solution)/shard_map/ppermute | solution.py:454
  22.1 1.5 %collective-permute-done.8.other_ref = f32[32,2048]{1,0:T(8,128)S(1)} collective-permute-done((f32[32,2048]{1,0:T(8,128)S(1)}, f32[32,2048]{1,0:T(8,128)S(1)}, u32[]{:S(2)}, u32[]{:S(2)}) %collective-permute-start.8) | collective-permute-done | bytes 262176 | tf_op jit(solution)/shard_map/ppermute | solution.py:454
  23.8 1.2 %collective-permute-done.9.other_ref = bf16[32,2048]{1,0:T(8,128)(2,1)S(1)} collective-permute-done((bf16[32,2048]{1,0:T(8,128)(2,1)S(1)}, bf16[32,2048]{1,0:T(8,128)(2,1)S(1)}, u32[]{:S(2)}, u32[]{:S(2)}) %collective-permute-start.9) | collective-permute-done | bytes 131104 | tf_op jit(solution)/shard_map/ppermute | solution.py:454
  25.0 1.1 %functions_first.1 = (bf16[64,256]{1,0:T(8,128)(2,1)S(1)}, bf16[64,256]{1,0:T(8,128)(2,1)S(1)}, bf16[64,256]{1,0:T(8,128)(2,1)S(1)}, bf16[64,2048]{1,0:T(8,128)(2,1)S(1)}) custom-call(bf16[32,2048]{1,0:T(8,128)(2,1)S(1)} %act.1.mine_ref, bf16[32,2048]{1,0:T(8,128)(2,1)S(1)} %collective-permute-done.9.other_ref, ...), custom_call_target="tpu_custom_call" | custom-call | tf_op jit(solution)/shard_map/functions_first/pallas_call | solution.py:332
  26.2 2.4 %collective-permute-start.11 = (bf16[64,256]{1,0:T(8,128)(2,1)S(1)}, bf16[64,256]{1,0:T(8,128)(2,1)S(1)}, u32[]{:S(2)}, u32[]{:S(2)}) collective-permute-start(bf16[64,256]{1,0:T(8,128)(2,1)S(1)} %get-tuple-element.45), channel_id=1, source_target_pairs={{0,4},{1,5},{2,6},{3,7},{4,0},{5,1},{6,2},{7,3},{8,12},{9,13},{10,... | collective-permute-start | bytes 98312 | tf_op jit(solution)/shard_map/ppermute | solution.py:454
  28.6 2.0 %collective-permute-start.12 = (bf16[64,256]{1,0:T(8,128)(2,1)S(1)}, bf16[64,256]{1,0:T(8,128)(2,1)S(1)}, u32[]{:S(2)}, u32[]{:S(2)}) collective-permute-start(bf16[64,256]{1,0:T(8,128)(2,1)S(1)} %get-tuple-element.46), channel_id=1, source_target_pairs={{0,6},{1,7},{2,4},{3,5},{4,2},{5,3},{6,0},{7,1},{8,14},{9,15},{10,... | collective-permute-start | bytes 98312 | tf_op jit(solution)/shard_map/ppermute | solution.py:454
  31.1 0.6 %collective-permute-done.11.refs_2_ = bf16[64,256]{1,0:T(8,128)(2,1)S(1)} collective-permute-done((bf16[64,256]{1,0:T(8,128)(2,1)S(1)}, bf16[64,256]{1,0:T(8,128)(2,1)S(1)}, u32[]{:S(2)}, u32[]{:S(2)}) %collective-permute-start.11) | collective-permute-done | bytes 32800 | tf_op jit(solution)/shard_map/ppermute | solution.py:454
  31.7 2.6 %collective-permute-done.12.refs_3_ = bf16[64,256]{1,0:T(8,128)(2,1)S(1)} collective-permute-done((bf16[64,256]{1,0:T(8,128)(2,1)S(1)}, bf16[64,256]{1,0:T(8,128)(2,1)S(1)}, u32[]{:S(2)}, u32[]{:S(2)}) %collective-permute-start.12) | collective-permute-done | bytes 32800 | tf_op jit(solution)/shard_map/ppermute | solution.py:454
  34.3 1.1 %collective-permute-start.13 = (bf16[256,256]{1,0:T(8,128)(2,1)S(1)}, bf16[256,256]{1,0:T(8,128)(2,1)}, u32[]{:S(2)}, u32[]{:S(2)}) collective-permute-start(bf16[256,256]{1,0:T(8,128)(2,1)S(1)} %assemble.1.grid_ref), channel_id=1, source_target_pairs={{0,24},{8,16},{16,8},{24,0},{1,25},{9,17},{17,9},{25,1},{2,26},{10... | collective-permute-start | bytes 393224 | tf_op jit(solution)/shard_map/ppermute | solution.py:454
  35.4 1.0 %collective-permute-start.14 = (bf16[256,256]{1,0:T(8,128)(2,1)S(1)}, bf16[256,256]{1,0:T(8,128)(2,1)S(1)}, u32[]{:S(2)}, u32[]{:S(2)}) collective-permute-start(bf16[256,256]{1,0:T(8,128)(2,1)S(1)} %assemble.1.grid_ref), channel_id=1, source_target_pairs={{0,8},{8,0},{16,24},{24,16},{1,9},{9,1},{17,25},{25,17},{2,10},{10... | collective-permute-start | bytes 393224 | tf_op jit(solution)/shard_map/ppermute | solution.py:454
  36.4 1.5 %collective-permute-start.15 = (bf16[256,256]{1,0:T(8,128)(2,1)S(1)}, bf16[256,256]{1,0:T(8,128)(2,1)S(1)}, u32[]{:S(2)}, u32[]{:S(2)}) collective-permute-start(bf16[256,256]{1,0:T(8,128)(2,1)S(1)} %assemble.1.grid_ref), channel_id=1, source_target_pairs={{0,16},{8,24},{16,0},{24,8},{1,17},{9,25},{17,1},{25,9},{2,18},{10... | collective-permute-start | bytes 393224 | tf_op jit(solution)/shard_map/ppermute | solution.py:454
  38.2 0.8 %diagonal.1.total_ref = f32[1024,256]{1,0:T(8,128)S(1)} custom-call(s32[16]{0:T(128)S(1)} %copy-done.1, bf16[1024,256]{1,0:T(8,128)(2,1)S(1)} %copy-done, f32[1024,1]{1,0:T(8,128)S(1)} %copy.10.row_ref, f32[1,256]{1,0:T(1,128)S(1)} %bitcast.3), custom_call_target="tpu_custom_call" | custom-call | tf_op jit(solution)/shard_map/diagonal/pallas_call | solution.py:395
  39.2 1.5 %collective-permute-done.13.grid_ref = bf16[256,256]{1,0:T(8,128)(2,1)} collective-permute-done((bf16[256,256]{1,0:T(8,128)(2,1)S(1)}, bf16[256,256]{1,0:T(8,128)(2,1)}, u32[]{:S(2)}, u32[]{:S(2)}) %collective-permute-start.13) | collective-permute-done | bytes 131104 | tf_op jit(solution)/shard_map/ppermute | solution.py:454
  40.8 1.2 %backward_more.4.total_ref = f32[1024,256]{1,0:T(8,128)S(1)} custom-call(f32[1024,256]{1,0:T(8,128)S(1)} %backward_more.3.total_ref, bf16[1024,1024]{1,0:T(8,128)(2,1)S(1)} %get-tuple-element.26.rolled_ref, bf16[256,256]{1,0:T(8,128)(2,1)} %collective-permute-done.13.grid_ref), custom_call_target="tpu_custom_call" | custom-call | flops 134217728 | bytes 3145728 | tf_op jit(solution)/shard_map/backward_more/pallas_call | solution.py:412
  42.3 1.2 %backward_end.1 = f32[1024,256]{1,0:T(8,128)} custom-call(f32[1024,256]{1,0:T(8,128)S(1)} %backward_more.5.total_ref, bf16[1024,1024]{1,0:T(8,128)(2,1)S(1)} %get-tuple-element.26.rolled_ref, bf16[256,256]{1,0:T(8,128)(2,1)S(1)} %collective-permute-done.15.grid_ref), custom_call_target="tpu_custom_call" | custom-call | flops 134217728 | bytes 4194304 | tf_op jit(solution)/shard_map/backward_end/pallas_call | solution.py:441
  (36 shorter events, 4.2 us)
Async XLA Ops:
  2.3 10.6 %collective-permute-start = (bf16[256,256]{1,0:T(8,128)(2,1)S(1)}, bf16[256,256]{1,0:T(8,128)(2,1)S(1)}, u32[]{:S(2)}, u32[]{:S(2)}) collective-permute-start(bf16[256,256]{1,0:T(8,128)(2,1)S(1)} %get-tuple-element.29), channel_id=1, source_target_pairs={{0,24},{8,16},{16,8},{24,0},{1,25},{9,17},{17,9},{25,1},{2,26},{10... | collective-permute-start | bytes 393224 | tf_op jit(solution)/shard_map/ppermute | solution.py:454
  6.7 6.2 %collective-permute-start.4 = (bf16[128,256]{1,0:T(8,128)(2,1)S(1)}, bf16[128,256]{1,0:T(8,128)(2,1)S(1)}, u32[]{:S(2)}, u32[]{:S(2)}) collective-permute-start(bf16[128,256]{1,0:T(8,128)(2,1)S(1)} %get-tuple-element.35), channel_id=1, source_target_pairs={{0,16},{8,24},{16,0},{24,8},{1,17},{9,25},{17,1},{25,9},{2,18},{10... | collective-permute-start | bytes 196616 | tf_op jit(solution)/shard_map/ppermute | solution.py:454
  7.6 5.3 %collective-permute-start.3 = (bf16[128,256]{1,0:T(8,128)(2,1)S(1)}, bf16[128,256]{1,0:T(8,128)(2,1)S(1)}, u32[]{:S(2)}, u32[]{:S(2)}) collective-permute-start(bf16[128,256]{1,0:T(8,128)(2,1)S(1)} %get-tuple-element.34), channel_id=1, source_target_pairs={{0,8},{8,0},{16,24},{24,16},{1,9},{9,1},{17,25},{25,17},{2,10},{10... | collective-permute-start | bytes 196616 | tf_op jit(solution)/shard_map/ppermute | solution.py:454
  7.8 9.2 %collective-permute-start.2 = (bf16[128,256]{1,0:T(8,128)(2,1)S(1)}, bf16[128,256]{1,0:T(8,128)(2,1)S(1)}, u32[]{:S(2)}, u32[]{:S(2)}) collective-permute-start(bf16[128,256]{1,0:T(8,128)(2,1)S(1)} %get-tuple-element.31), channel_id=1, source_target_pairs={{0,16},{8,24},{16,0},{24,8},{1,17},{9,25},{17,1},{25,9},{2,18},{10... | collective-permute-start | bytes 196616 | tf_op jit(solution)/shard_map/ppermute | solution.py:454
  9.7 7.3 %collective-permute-start.1 = (bf16[128,256]{1,0:T(8,128)(2,1)S(1)}, bf16[128,256]{1,0:T(8,128)(2,1)S(1)}, u32[]{:S(2)}, u32[]{:S(2)}) collective-permute-start(bf16[128,256]{1,0:T(8,128)(2,1)S(1)} %get-tuple-element.30), channel_id=1, source_target_pairs={{0,8},{8,0},{16,24},{24,16},{1,9},{9,1},{17,25},{25,17},{2,10},{10... | collective-permute-start | bytes 196616 | tf_op jit(solution)/shard_map/ppermute | solution.py:454
  13.0 5.2 %collective-permute-start.5 = (bf16[64,256]{1,0:T(8,128)(2,1)S(1)}, bf16[64,256]{1,0:T(8,128)(2,1)S(1)}, u32[]{:S(2)}, u32[]{:S(2)}) collective-permute-start(bf16[64,256]{1,0:T(8,128)(2,1)S(1)} %get-tuple-element.36), channel_id=1, source_target_pairs={{0,4},{1,5},{2,6},{3,7},{4,0},{5,1},{6,2},{7,3},{8,12},{9,13},{10,... | collective-permute-start | bytes 98312 | tf_op jit(solution)/shard_map/ppermute | solution.py:454
  15.6 5.7 %collective-permute-start.6 = (bf16[64,256]{1,0:T(8,128)(2,1)S(1)}, bf16[64,256]{1,0:T(8,128)(2,1)S(1)}, u32[]{:S(2)}, u32[]{:S(2)}) collective-permute-start(bf16[64,256]{1,0:T(8,128)(2,1)S(1)} %get-tuple-element.38), channel_id=1, source_target_pairs={{0,6},{1,7},{2,4},{3,5},{4,2},{5,3},{6,0},{7,1},{8,14},{9,15},{10,... | collective-permute-start | bytes 98312 | tf_op jit(solution)/shard_map/ppermute | solution.py:454
  17.0 4.6 %collective-permute-start.7 = (bf16[64,256]{1,0:T(8,128)(2,1)S(1)}, bf16[64,256]{1,0:T(8,128)(2,1)S(1)}, u32[]{:S(2)}, u32[]{:S(2)}) collective-permute-start(bf16[64,256]{1,0:T(8,128)(2,1)S(1)} %get-tuple-element.39), channel_id=1, source_target_pairs={{0,2},{1,3},{2,0},{3,1},{4,6},{5,7},{6,4},{7,5},{8,10},{9,11},{10,... | collective-permute-start | bytes 98312 | tf_op jit(solution)/shard_map/ppermute | solution.py:454
  22.0 1.6 %collective-permute-start.8 = (f32[32,2048]{1,0:T(8,128)S(1)}, f32[32,2048]{1,0:T(8,128)S(1)}, u32[]{:S(2)}, u32[]{:S(2)}) collective-permute-start(f32[32,2048]{1,0:T(8,128)S(1)} %get-tuple-element.41), channel_id=1, source_target_pairs={{0,1},{1,0},{2,3},{3,2},{4,5},{5,4},{6,7},{7,6},{8,9},{9,8},{10,11... | collective-permute-start | bytes 786440 | tf_op jit(solution)/shard_map/ppermute | solution.py:454
  23.6 1.4 %collective-permute-start.9 = (bf16[32,2048]{1,0:T(8,128)(2,1)S(1)}, bf16[32,2048]{1,0:T(8,128)(2,1)S(1)}, u32[]{:S(2)}, u32[]{:S(2)}) collective-permute-start(bf16[32,2048]{1,0:T(8,128)(2,1)S(1)} %act.1.mine_ref), channel_id=1, source_target_pairs={{0,1},{1,0},{2,3},{3,2},{4,5},{5,4},{6,7},{7,6},{8,9},{9,8},{10,11... | collective-permute-start | bytes 393224 | tf_op jit(solution)/shard_map/ppermute | solution.py:454
  26.1 11.8 %copy-start.3 = (f32[1024]{0:T(1024)S(1)}, f32[1024]{0:T(1024)}, u32[]{:S(2)}) copy-start(f32[1024]{0:T(1024)} %param.10) | copy-start | bytes 12292
  26.1 12.0 %copy-start = (bf16[1024,256]{1,0:T(8,128)(2,1)S(1)}, bf16[1024,256]{1,0:T(8,128)(2,1)}, u32[]{:S(2)}) copy-start(bf16[1024,256]{1,0:T(8,128)(2,1)} %coeff_hbm.1) | copy-start | bytes 1572868
  26.1 12.0 %copy-start.1 = (s32[16]{0:T(128)S(1)}, s32[16]{0:T(128)}, u32[]{:S(2)}) copy-start(s32[16]{0:T(128)} %pad_hbm.1) | copy-start | bytes 196
  26.2 12.0 %copy-start.2 = (f32[256]{0:T(256)S(1)}, f32[256]{0:T(256)}, u32[]{:S(2)}) copy-start(f32[256]{0:T(256)} %param.11) | copy-start | bytes 3076
  26.2 4.9 %collective-permute-start.10 = (bf16[64,256]{1,0:T(8,128)(2,1)S(1)}, bf16[64,256]{1,0:T(8,128)(2,1)S(1)}, u32[]{:S(2)}, u32[]{:S(2)}) collective-permute-start(bf16[64,256]{1,0:T(8,128)(2,1)S(1)} %get-tuple-element.44), channel_id=1, source_target_pairs={{0,2},{1,3},{2,0},{3,1},{4,6},{5,7},{6,4},{7,5},{8,10},{9,11},{10,... | collective-permute-start | bytes 98312 | tf_op jit(solution)/shard_map/ppermute | solution.py:454
  26.2 5.4 %collective-permute-start.11 = (bf16[64,256]{1,0:T(8,128)(2,1)S(1)}, bf16[64,256]{1,0:T(8,128)(2,1)S(1)}, u32[]{:S(2)}, u32[]{:S(2)}) collective-permute-start(bf16[64,256]{1,0:T(8,128)(2,1)S(1)} %get-tuple-element.45), channel_id=1, source_target_pairs={{0,4},{1,5},{2,6},{3,7},{4,0},{5,1},{6,2},{7,3},{8,12},{9,13},{10,... | collective-permute-start | bytes 98312 | tf_op jit(solution)/shard_map/ppermute | solution.py:454
  28.6 5.7 %collective-permute-start.12 = (bf16[64,256]{1,0:T(8,128)(2,1)S(1)}, bf16[64,256]{1,0:T(8,128)(2,1)S(1)}, u32[]{:S(2)}, u32[]{:S(2)}) collective-permute-start(bf16[64,256]{1,0:T(8,128)(2,1)S(1)} %get-tuple-element.46), channel_id=1, source_target_pairs={{0,6},{1,7},{2,4},{3,5},{4,2},{5,3},{6,0},{7,1},{8,14},{9,15},{10,... | collective-permute-start | bytes 98312 | tf_op jit(solution)/shard_map/ppermute | solution.py:454
  34.3 6.4 %collective-permute-start.13 = (bf16[256,256]{1,0:T(8,128)(2,1)S(1)}, bf16[256,256]{1,0:T(8,128)(2,1)}, u32[]{:S(2)}, u32[]{:S(2)}) collective-permute-start(bf16[256,256]{1,0:T(8,128)(2,1)S(1)} %assemble.1.grid_ref), channel_id=1, source_target_pairs={{0,24},{8,16},{16,8},{24,0},{1,25},{9,17},{17,9},{25,1},{2,26},{10... | collective-permute-start | bytes 393224 | tf_op jit(solution)/shard_map/ppermute | solution.py:454
  35.4 6.5 %collective-permute-start.14 = (bf16[256,256]{1,0:T(8,128)(2,1)S(1)}, bf16[256,256]{1,0:T(8,128)(2,1)S(1)}, u32[]{:S(2)}, u32[]{:S(2)}) collective-permute-start(bf16[256,256]{1,0:T(8,128)(2,1)S(1)} %assemble.1.grid_ref), channel_id=1, source_target_pairs={{0,8},{8,0},{16,24},{24,16},{1,9},{9,1},{17,25},{25,17},{2,10},{10... | collective-permute-start | bytes 393224 | tf_op jit(solution)/shard_map/ppermute | solution.py:454
  36.4 5.9 %collective-permute-start.15 = (bf16[256,256]{1,0:T(8,128)(2,1)S(1)}, bf16[256,256]{1,0:T(8,128)(2,1)S(1)}, u32[]{:S(2)}, u32[]{:S(2)}) collective-permute-start(bf16[256,256]{1,0:T(8,128)(2,1)S(1)} %assemble.1.grid_ref), channel_id=1, source_target_pairs={{0,16},{8,24},{16,0},{24,8},{1,17},{9,25},{17,1},{25,9},{2,18},{10... | collective-permute-start | bytes 393224 | tf_op jit(solution)/shard_map/ppermute | solution.py:454

commit v4 on v3

--- a/solution.py
+++ b/solution.py
@@ -357,25 +357,25 @@
     )(both, basis)
 
 
-def assemble_kernel(*refs):
-    parts, out_ref = refs[:-1], refs[-1]
+def assemble_kernel(count, *refs):
+    parts, outs = refs[:count], refs[count:]
     chip = lax.axis_index("narrow") // 2
     rows = parts[0].shape[0]
     for j, part in enumerate(parts):
-        start = pl.multiple_of((chip ^ j) * rows, rows)
-        out_ref[pl.ds(start, rows), :] = part[...]
-
-
-def assemble(parts):
+        span = pl.ds(pl.multiple_of((chip ^ j) * rows, rows), rows)
+        for out in outs:
+            out[span, :] = part[...]
+
+
+def assemble(copies, parts):
     rows, columns = parts[0].shape
     chips = len(parts)
     return call(
-        assemble_kernel,
+        functools.partial(assemble_kernel, chips),
         "assemble",
-        array((rows * chips, columns), BF16),
+        (array((rows * chips, columns), BF16),) * copies,
         [VMEM] * chips,
-        VMEM,
-        moved=MIB // 4,
+        (VMEM,) * copies,
     )(*parts)
 
 
@@ -451,8 +451,7 @@
 
 
 def exchange(value, step, size, axis):
-    moved = lax.ppermute(value, axis, [(i, i ^ step) for i in range(size)])
-    return pltpu.with_memory_space_constraint(moved, pltpu.VMEM)
+    return lax.ppermute(value, axis, [(i, i ^ step) for i in range(size)])
 
 
 def body(
@@ -504,9 +503,11 @@
     leave = list(reversed(range(1, chips)))
     *out, both = first_functions(leave, acted, other, basis, more)
     blocks = {j: exchange(out[i], 2 * j, narrow, "narrow") for i, j in enumerate(leave)}
-    grid = assemble([functions(both, where[0])] + [blocks[j] for j in range(1, chips)])
+    grid, *sources = assemble(
+        wide, [functions(both, where[0])] + [blocks[j] for j in range(1, chips)]
+    )
     steps = [wide - 1] + order
-    grids = {k: exchange(grid, k, wide, "wide") for k in steps}
+    grids = {k: exchange(source, k, wide, "wide") for k, source in zip(steps, sources)}
     total = diagonal(block_pad, coeff, groupb_row_energy, groupa_energy)
     total = backward_more(wide, 0, total, rolled, grid)
     for k in steps[:-1]:

time: 43.7 us -> 44.6 us (1.021)
  Pallas kernels: 11.4 us -> 12.1 us
    pallas_call x1, Pallas kernels: 0.01 us -> 0.77 us  [assemble(): call(functools.partial(assemble_kernel, chips), 'assemble', (array((rows...]
  transfers between devices with their start and end apart: 16 -> 16, of which waited for: 7 -> 7; matrix products, arithmetic and copies ran while one was open for 1% -> 0% of each run, Pallas kernels for 15% -> 14%
where the time goes in v4:
time: 44.6 us; the launch traced here: 44.4 us
  starting transfers between devices  20.7 us (46%)
  Pallas kernels  12.1 us (27%)
  waiting for transfers between devices  11.2 us (25%)
    ppermute x16, starting transfers between devices, exchange(): return lax.ppermute(value, axis, [(i, i ^ step) for i in range(size)])  20.7 us
    ppermute x16, waiting for transfers between devices, exchange(): return lax.ppermute(value, axis, [(i, i ^ step) for i in range(size)])  11.2 us
    pallas_call x1, Pallas kernels, first(): call(functools.partial(first_kernel, wide, chips), 'forward_first', (arra...  2.33 us
    pallas_call x3, Pallas kernels, backward_more(): call(functools.partial(more_kernel, wide, k), 'backward_more', array(tota...  1.79 us
    pallas_call x1, Pallas kernels, last(): call(functools.partial(last_kernel, wide), 'forward_own', (array((own, co...  1.66 us
    pallas_call x1, Pallas kernels, backward_end(): call(functools.partial(end_kernel, wide, k), 'backward_end', array(total....  1.23 us
    pallas_call x1, Pallas kernels, first_functions(): call(functools.partial(first_functions_kernel, leave), 'functions_first',...  1.07 us
  transfers between devices with their start and end apart: 16, of which 7 were waited for; matrix products, arithmetic and copies ran while one was open for 0% of the time, Pallas kernels for 14%

profile of v4, /device:TPU:0, one launch (start us, length us, event | category | flops | bytes accessed | tf_op | source)
XLA Modules:
  0.0 44.4 jit_solution(14881015143333781254)
XLA Ops:
  0.0 2.3 %forward_first.1 = (bf16[256,256]{1,0:T(8,128)(2,1)S(1)}, bf16[256,1024]{1,0:T(8,128)(2,1)S(1)}, bf16[1024,1024]{1,0:T(8,128)(2,1)S(1)}, bf16[2,256,2048]{2,1,0:T(8,128)(2,1)S(1)}, f32[32,2048]{1,0:T(8,128)S(1)}) custom-call(s32[16]{0:T(128)} %level_hbm.1, s32[16]{0:T(128)} %pad_hbm.1, s32[16]{0:T(128)} %shift_hbm.1, bf16[1024,256]{1,0:T(8,128)(2,1)} %coeff_hbm.1, ...), custom_call_target="tpu_custom_call" | custom-call | flops 134217728 | bytes 4194304 | tf_op jit(solution)/shard_map/forward_first/pallas_call | solution.py:149
  2.3 4.0 %collective-permute-start = (bf16[256,256]{1,0:T(8,128)(2,1)S(1)}, bf16[256,256]{1,0:T(8,128)(2,1)S(1)}, u32[]{:S(2)}, u32[]{:S(2)}) collective-permute-start(bf16[256,256]{1,0:T(8,128)(2,1)S(1)} %get-tuple-element.33), channel_id=1, source_target_pairs={{0,24},{8,16},{16,8},{24,0},{1,25},{9,17},{17,9},{25,1},{2,26},{10... | collective-permute-start | bytes 393224 | tf_op jit(solution)/shard_map/ppermute | solution.py:454
  6.7 0.6 %collective-permute-start.4 = (bf16[128,256]{1,0:T(8,128)(2,1)S(1)}, bf16[128,256]{1,0:T(8,128)(2,1)S(1)}, u32[]{:S(2)}, u32[]{:S(2)}) collective-permute-start(bf16[128,256]{1,0:T(8,128)(2,1)S(1)} %get-tuple-element.39), channel_id=1, source_target_pairs={{0,16},{8,24},{16,0},{24,8},{1,17},{9,25},{17,1},{25,9},{2,18},{10... | collective-permute-start | bytes 196616 | tf_op jit(solution)/shard_map/ppermute | solution.py:454
  7.8 2.0 %collective-permute-start.2 = (bf16[128,256]{1,0:T(8,128)(2,1)S(1)}, bf16[128,256]{1,0:T(8,128)(2,1)S(1)}, u32[]{:S(2)}, u32[]{:S(2)}) collective-permute-start(bf16[128,256]{1,0:T(8,128)(2,1)S(1)} %get-tuple-element.35), channel_id=1, source_target_pairs={{0,16},{8,24},{16,0},{24,8},{1,17},{9,25},{17,1},{25,9},{2,18},{10... | collective-permute-start | bytes 196616 | tf_op jit(solution)/shard_map/ppermute | solution.py:454
  9.7 1.5 %collective-permute-start.1 = (bf16[128,256]{1,0:T(8,128)(2,1)S(1)}, bf16[128,256]{1,0:T(8,128)(2,1)S(1)}, u32[]{:S(2)}, u32[]{:S(2)}) collective-permute-start(bf16[128,256]{1,0:T(8,128)(2,1)S(1)} %get-tuple-element.34), channel_id=1, source_target_pairs={{0,8},{8,0},{16,24},{24,16},{1,9},{9,1},{17,25},{25,17},{2,10},{10... | collective-permute-start | bytes 196616 | tf_op jit(solution)/shard_map/ppermute | solution.py:454
  11.2 1.7 %forward_own.1 = (f32[256,256]{1,0:T(8,128)S(1)}, bf16[2,256,2048]{2,1,0:T(8,128)(2,1)S(1)}) custom-call(bf16[256,1024]{1,0:T(8,128)(2,1)S(1)} %get-tuple-element.31.turned_ref, bf16[1024,1024]{1,0:T(8,128)(2,1)S(1)} %get-tuple-element.30.rolled_ref, bf16[2048,2048]{1,0:T(8,128)(2,1)} %basis_hbm.3), custom_call_target="tpu_custom_call" | custom-call | tf_op jit(solution)/shard_map/forward_own/pallas_call | solution.py:206
  13.0 2.7 %collective-permute-start.5 = (bf16[64,256]{1,0:T(8,128)(2,1)S(1)}, bf16[64,256]{1,0:T(8,128)(2,1)S(1)}, u32[]{:S(2)}, u32[]{:S(2)}) collective-permute-start(bf16[64,256]{1,0:T(8,128)(2,1)S(1)} %get-tuple-element.40), channel_id=1, source_target_pairs={{0,4},{1,5},{2,6},{3,7},{4,0},{5,1},{6,2},{7,3},{8,12},{9,13},{10,... | collective-permute-start | bytes 98312 | tf_op jit(solution)/shard_map/ppermute | solution.py:454
  15.6 1.4 %collective-permute-start.6 = (bf16[64,256]{1,0:T(8,128)(2,1)S(1)}, bf16[64,256]{1,0:T(8,128)(2,1)S(1)}, u32[]{:S(2)}, u32[]{:S(2)}) collective-permute-start(bf16[64,256]{1,0:T(8,128)(2,1)S(1)} %get-tuple-element.42), channel_id=1, source_target_pairs={{0,6},{1,7},{2,4},{3,5},{4,2},{5,3},{6,0},{7,1},{8,14},{9,15},{10,... | collective-permute-start | bytes 98312 | tf_op jit(solution)/shard_map/ppermute | solution.py:454
  18.5 2.9 %collective-permute-done.6.x_ref = bf16[64,256]{1,0:T(8,128)(2,1)S(1)} collective-permute-done((bf16[64,256]{1,0:T(8,128)(2,1)S(1)}, bf16[64,256]{1,0:T(8,128)(2,1)S(1)}, u32[]{:S(2)}, u32[]{:S(2)}) %collective-permute-start.6) | collective-permute-done | bytes 32800 | tf_op jit(solution)/shard_map/ppermute | solution.py:454
  22.1 1.5 %collective-permute-done.8.other_ref = f32[32,2048]{1,0:T(8,128)S(1)} collective-permute-done((f32[32,2048]{1,0:T(8,128)S(1)}, f32[32,2048]{1,0:T(8,128)S(1)}, u32[]{:S(2)}, u32[]{:S(2)}) %collective-permute-start.8) | collective-permute-done | bytes 262176 | tf_op jit(solution)/shard_map/ppermute | solution.py:454
  23.8 1.2 %collective-permute-done.9.other_ref = bf16[32,2048]{1,0:T(8,128)(2,1)S(1)} collective-permute-done((bf16[32,2048]{1,0:T(8,128)(2,1)S(1)}, bf16[32,2048]{1,0:T(8,128)(2,1)S(1)}, u32[]{:S(2)}, u32[]{:S(2)}) %collective-permute-start.9) | collective-permute-done | bytes 131104 | tf_op jit(solution)/shard_map/ppermute | solution.py:454
  25.0 1.1 %functions_first.1 = (bf16[64,256]{1,0:T(8,128)(2,1)S(1)}, bf16[64,256]{1,0:T(8,128)(2,1)S(1)}, bf16[64,256]{1,0:T(8,128)(2,1)S(1)}, bf16[64,2048]{1,0:T(8,128)(2,1)S(1)}) custom-call(bf16[32,2048]{1,0:T(8,128)(2,1)S(1)} %act.1.mine_ref, bf16[32,2048]{1,0:T(8,128)(2,1)S(1)} %collective-permute-done.9.other_ref, ...), custom_call_target="tpu_custom_call" | custom-call | tf_op jit(solution)/shard_map/functions_first/pallas_call | solution.py:332
  26.2 2.4 %collective-permute-start.11 = (bf16[64,256]{1,0:T(8,128)(2,1)S(1)}, bf16[64,256]{1,0:T(8,128)(2,1)S(1)}, u32[]{:S(2)}, u32[]{:S(2)}) collective-permute-start(bf16[64,256]{1,0:T(8,128)(2,1)S(1)} %get-tuple-element.49), channel_id=1, source_target_pairs={{0,4},{1,5},{2,6},{3,7},{4,0},{5,1},{6,2},{7,3},{8,12},{9,13},{10,... | collective-permute-start | bytes 98312 | tf_op jit(solution)/shard_map/ppermute | solution.py:454
  28.6 2.0 %collective-permute-start.12 = (bf16[64,256]{1,0:T(8,128)(2,1)S(1)}, bf16[64,256]{1,0:T(8,128)(2,1)S(1)}, u32[]{:S(2)}, u32[]{:S(2)}) collective-permute-start(bf16[64,256]{1,0:T(8,128)(2,1)S(1)} %get-tuple-element.50), channel_id=1, source_target_pairs={{0,6},{1,7},{2,4},{3,5},{4,2},{5,3},{6,0},{7,1},{8,14},{9,15},{10,... | collective-permute-start | bytes 98312 | tf_op jit(solution)/shard_map/ppermute | solution.py:454
  31.1 0.6 %collective-permute-done.11.refs_2_ = bf16[64,256]{1,0:T(8,128)(2,1)S(1)} collective-permute-done((bf16[64,256]{1,0:T(8,128)(2,1)S(1)}, bf16[64,256]{1,0:T(8,128)(2,1)S(1)}, u32[]{:S(2)}, u32[]{:S(2)}) %collective-permute-start.11) | collective-permute-done | bytes 32800 | tf_op jit(solution)/shard_map/ppermute | solution.py:454
  31.7 2.6 %collective-permute-done.12.refs_3_ = bf16[64,256]{1,0:T(8,128)(2,1)S(1)} collective-permute-done((bf16[64,256]{1,0:T(8,128)(2,1)S(1)}, bf16[64,256]{1,0:T(8,128)(2,1)S(1)}, u32[]{:S(2)}, u32[]{:S(2)}) %collective-permute-start.12) | collective-permute-done | bytes 32800 | tf_op jit(solution)/shard_map/ppermute | solution.py:454
  34.3 0.8 %assemble.1 = (bf16[256,256]{1,0:T(8,128)(2,1)S(1)}, bf16[256,256]{1,0:T(8,128)(2,1)}, bf16[256,256]{1,0:T(8,128)(2,1)}, bf16[256,256]{1,0:T(8,128)(2,1)}) custom-call(bf16[64,256]{1,0:T(8,128)(2,1)S(1)} %functions_more.1.refs_0_, bf16[64,256]{1,0:T(8,128)(2,1)S(1)} %collective-permute-done.10.refs_1_, bf16[64,256]{1,0:T(8,128)(2,1)S(1)} %collective-permute-done.11.refs_2_, ...), custom_call_target="tpu_custom_call" | custom-call | tf_op jit(solution)/shard_map/assemble/pallas_call | solution.py:373
  35.1 1.0 %collective-permute-start.13 = (bf16[256,256]{1,0:T(8,128)(2,1)}, bf16[256,256]{1,0:T(8,128)(2,1)}, u32[]{:S(2)}, u32[]{:S(2)}) collective-permute-start(bf16[256,256]{1,0:T(8,128)(2,1)} %get-tuple-element.52), channel_id=1, source_target_pairs={{0,24},{8,16},{16,8},{24,0},{1,25},{9,17},{17,9},{25,1},{2,26},{10... | collective-permute-start | bytes 393224 | tf_op jit(solution)/shard_map/ppermute | solution.py:454
  36.1 1.0 %collective-permute-start.14 = (bf16[256,256]{1,0:T(8,128)(2,1)}, bf16[256,256]{1,0:T(8,128)(2,1)S(1)}, u32[]{:S(2)}, u32[]{:S(2)}) collective-permute-start(bf16[256,256]{1,0:T(8,128)(2,1)} %get-tuple-element.53), channel_id=1, source_target_pairs={{0,8},{8,0},{16,24},{24,16},{1,9},{9,1},{17,25},{25,17},{2,10},{10... | collective-permute-start | bytes 393224 | tf_op jit(solution)/shard_map/ppermute | solution.py:454
  37.1 1.5 %collective-permute-start.15 = (bf16[256,256]{1,0:T(8,128)(2,1)}, bf16[256,256]{1,0:T(8,128)(2,1)S(1)}, u32[]{:S(2)}, u32[]{:S(2)}) collective-permute-start(bf16[256,256]{1,0:T(8,128)(2,1)} %get-tuple-element.54), channel_id=1, source_target_pairs={{0,16},{8,24},{16,0},{24,8},{1,17},{9,25},{17,1},{25,9},{2,18},{10... | collective-permute-start | bytes 393224 | tf_op jit(solution)/shard_map/ppermute | solution.py:454
  38.8 0.8 %diagonal.1.total_ref = f32[1024,256]{1,0:T(8,128)S(1)} custom-call(s32[16]{0:T(128)S(1)} %copy-done.1, bf16[1024,256]{1,0:T(8,128)(2,1)S(1)} %copy-done, f32[1024,1]{1,0:T(8,128)S(1)} %copy.10.row_ref, f32[1,256]{1,0:T(1,128)S(1)} %bitcast.3), custom_call_target="tpu_custom_call" | custom-call | tf_op jit(solution)/shard_map/diagonal/pallas_call | solution.py:395
  39.9 1.7 %collective-permute-done.13.grid_ref = bf16[256,256]{1,0:T(8,128)(2,1)} collective-permute-done((bf16[256,256]{1,0:T(8,128)(2,1)}, bf16[256,256]{1,0:T(8,128)(2,1)}, u32[]{:S(2)}, u32[]{:S(2)}) %collective-permute-start.13) | collective-permute-done | bytes 131104 | tf_op jit(solution)/shard_map/ppermute | solution.py:454
  41.7 1.2 %backward_more.4.total_ref = f32[1024,256]{1,0:T(8,128)S(1)} custom-call(f32[1024,256]{1,0:T(8,128)S(1)} %backward_more.3.total_ref, bf16[1024,1024]{1,0:T(8,128)(2,1)S(1)} %get-tuple-element.30.rolled_ref, bf16[256,256]{1,0:T(8,128)(2,1)} %collective-permute-done.13.grid_ref), custom_call_target="tpu_custom_call" | custom-call | flops 134217728 | bytes 3145728 | tf_op jit(solution)/shard_map/backward_more/pallas_call | solution.py:412
  43.2 1.2 %backward_end.1 = f32[1024,256]{1,0:T(8,128)} custom-call(f32[1024,256]{1,0:T(8,128)S(1)} %backward_more.5.total_ref, bf16[1024,1024]{1,0:T(8,128)(2,1)S(1)} %get-tuple-element.30.rolled_ref, bf16[256,256]{1,0:T(8,128)(2,1)S(1)} %collective-permute-done.15.grid_ref), custom_call_target="tpu_custom_call" | custom-call | flops 134217728 | bytes 4194304 | tf_op jit(solution)/shard_map/backward_end/pallas_call | solution.py:441
  (36 shorter events, 4.7 us)
Async XLA Ops:
  2.3 10.6 %collective-permute-start = (bf16[256,256]{1,0:T(8,128)(2,1)S(1)}, bf16[256,256]{1,0:T(8,128)(2,1)S(1)}, u32[]{:S(2)}, u32[]{:S(2)}) collective-permute-start(bf16[256,256]{1,0:T(8,128)(2,1)S(1)} %get-tuple-element.33), channel_id=1, source_target_pairs={{0,24},{8,16},{16,8},{24,0},{1,25},{9,17},{17,9},{25,1},{2,26},{10... | collective-permute-start | bytes 393224 | tf_op jit(solution)/shard_map/ppermute | solution.py:454
  6.7 6.2 %collective-permute-start.4 = (bf16[128,256]{1,0:T(8,128)(2,1)S(1)}, bf16[128,256]{1,0:T(8,128)(2,1)S(1)}, u32[]{:S(2)}, u32[]{:S(2)}) collective-permute-start(bf16[128,256]{1,0:T(8,128)(2,1)S(1)} %get-tuple-element.39), channel_id=1, source_target_pairs={{0,16},{8,24},{16,0},{24,8},{1,17},{9,25},{17,1},{25,9},{2,18},{10... | collective-permute-start | bytes 196616 | tf_op jit(solution)/shard_map/ppermute | solution.py:454
  7.6 5.3 %collective-permute-start.3 = (bf16[128,256]{1,0:T(8,128)(2,1)S(1)}, bf16[128,256]{1,0:T(8,128)(2,1)S(1)}, u32[]{:S(2)}, u32[]{:S(2)}) collective-permute-start(bf16[128,256]{1,0:T(8,128)(2,1)S(1)} %get-tuple-element.38), channel_id=1, source_target_pairs={{0,8},{8,0},{16,24},{24,16},{1,9},{9,1},{17,25},{25,17},{2,10},{10... | collective-permute-start | bytes 196616 | tf_op jit(solution)/shard_map/ppermute | solution.py:454
  7.8 9.2 %collective-permute-start.2 = (bf16[128,256]{1,0:T(8,128)(2,1)S(1)}, bf16[128,256]{1,0:T(8,128)(2,1)S(1)}, u32[]{:S(2)}, u32[]{:S(2)}) collective-permute-start(bf16[128,256]{1,0:T(8,128)(2,1)S(1)} %get-tuple-element.35), channel_id=1, source_target_pairs={{0,16},{8,24},{16,0},{24,8},{1,17},{9,25},{17,1},{25,9},{2,18},{10... | collective-permute-start | bytes 196616 | tf_op jit(solution)/shard_map/ppermute | solution.py:454
  9.7 7.3 %collective-permute-start.1 = (bf16[128,256]{1,0:T(8,128)(2,1)S(1)}, bf16[128,256]{1,0:T(8,128)(2,1)S(1)}, u32[]{:S(2)}, u32[]{:S(2)}) collective-permute-start(bf16[128,256]{1,0:T(8,128)(2,1)S(1)} %get-tuple-element.34), channel_id=1, source_target_pairs={{0,8},{8,0},{16,24},{24,16},{1,9},{9,1},{17,25},{25,17},{2,10},{10... | collective-permute-start | bytes 196616 | tf_op jit(solution)/shard_map/ppermute | solution.py:454
  13.0 5.2 %collective-permute-start.5 = (bf16[64,256]{1,0:T(8,128)(2,1)S(1)}, bf16[64,256]{1,0:T(8,128)(2,1)S(1)}, u32[]{:S(2)}, u32[]{:S(2)}) collective-permute-start(bf16[64,256]{1,0:T(8,128)(2,1)S(1)} %get-tuple-element.40), channel_id=1, source_target_pairs={{0,4},{1,5},{2,6},{3,7},{4,0},{5,1},{6,2},{7,3},{8,12},{9,13},{10,... | collective-permute-start | bytes 98312 | tf_op jit(solution)/shard_map/ppermute | solution.py:454
  15.6 5.7 %collective-permute-start.6 = (bf16[64,256]{1,0:T(8,128)(2,1)S(1)}, bf16[64,256]{1,0:T(8,128)(2,1)S(1)}, u32[]{:S(2)}, u32[]{:S(2)}) collective-permute-start(bf16[64,256]{1,0:T(8,128)(2,1)S(1)} %get-tuple-element.42), channel_id=1, source_target_pairs={{0,6},{1,7},{2,4},{3,5},{4,2},{5,3},{6,0},{7,1},{8,14},{9,15},{10,... | collective-permute-start | bytes 98312 | tf_op jit(solution)/shard_map/ppermute | solution.py:454
  17.0 4.6 %collective-permute-start.7 = (bf16[64,256]{1,0:T(8,128)(2,1)S(1)}, bf16[64,256]{1,0:T(8,128)(2,1)S(1)}, u32[]{:S(2)}, u32[]{:S(2)}) collective-permute-start(bf16[64,256]{1,0:T(8,128)(2,1)S(1)} %get-tuple-element.43), channel_id=1, source_target_pairs={{0,2},{1,3},{2,0},{3,1},{4,6},{5,7},{6,4},{7,5},{8,10},{9,11},{10,... | collective-permute-start | bytes 98312 | tf_op jit(solution)/shard_map/ppermute | solution.py:454
  22.0 1.6 %collective-permute-start.8 = (f32[32,2048]{1,0:T(8,128)S(1)}, f32[32,2048]{1,0:T(8,128)S(1)}, u32[]{:S(2)}, u32[]{:S(2)}) collective-permute-start(f32[32,2048]{1,0:T(8,128)S(1)} %get-tuple-element.45), channel_id=1, source_target_pairs={{0,1},{1,0},{2,3},{3,2},{4,5},{5,4},{6,7},{7,6},{8,9},{9,8},{10,11... | collective-permute-start | bytes 786440 | tf_op jit(solution)/shard_map/ppermute | solution.py:454
  23.6 1.4 %collective-permute-start.9 = (bf16[32,2048]{1,0:T(8,128)(2,1)S(1)}, bf16[32,2048]{1,0:T(8,128)(2,1)S(1)}, u32[]{:S(2)}, u32[]{:S(2)}) collective-permute-start(bf16[32,2048]{1,0:T(8,128)(2,1)S(1)} %act.1.mine_ref), channel_id=1, source_target_pairs={{0,1},{1,0},{2,3},{3,2},{4,5},{5,4},{6,7},{7,6},{8,9},{9,8},{10,11... | collective-permute-start | bytes 393224 | tf_op jit(solution)/shard_map/ppermute | solution.py:454
  26.1 12.5 %copy-start.3 = (f32[1024]{0:T(1024)S(1)}, f32[1024]{0:T(1024)}, u32[]{:S(2)}) copy-start(f32[1024]{0:T(1024)} %param.10) | copy-start | bytes 12292
  26.1 12.7 %copy-start = (bf16[1024,256]{1,0:T(8,128)(2,1)S(1)}, bf16[1024,256]{1,0:T(8,128)(2,1)}, u32[]{:S(2)}) copy-start(bf16[1024,256]{1,0:T(8,128)(2,1)} %coeff_hbm.1) | copy-start | bytes 1572868
  26.1 12.7 %copy-start.1 = (s32[16]{0:T(128)S(1)}, s32[16]{0:T(128)}, u32[]{:S(2)}) copy-start(s32[16]{0:T(128)} %pad_hbm.1) | copy-start | bytes 196
  26.2 12.7 %copy-start.2 = (f32[256]{0:T(256)S(1)}, f32[256]{0:T(256)}, u32[]{:S(2)}) copy-start(f32[256]{0:T(256)} %param.11) | copy-start | bytes 3076
  26.2 4.9 %collective-permute-start.10 = (bf16[64,256]{1,0:T(8,128)(2,1)S(1)}, bf16[64,256]{1,0:T(8,128)(2,1)S(1)}, u32[]{:S(2)}, u32[]{:S(2)}) collective-permute-start(bf16[64,256]{1,0:T(8,128)(2,1)S(1)} %get-tuple-element.48), channel_id=1, source_target_pairs={{0,2},{1,3},{2,0},{3,1},{4,6},{5,7},{6,4},{7,5},{8,10},{9,11},{10,... | collective-permute-start | bytes 98312 | tf_op jit(solution)/shard_map/ppermute | solution.py:454
  26.2 5.4 %collective-permute-start.11 = (bf16[64,256]{1,0:T(8,128)(2,1)S(1)}, bf16[64,256]{1,0:T(8,128)(2,1)S(1)}, u32[]{:S(2)}, u32[]{:S(2)}) collective-permute-start(bf16[64,256]{1,0:T(8,128)(2,1)S(1)} %get-tuple-element.49), channel_id=1, source_target_pairs={{0,4},{1,5},{2,6},{3,7},{4,0},{5,1},{6,2},{7,3},{8,12},{9,13},{10,... | collective-permute-start | bytes 98312 | tf_op jit(solution)/shard_map/ppermute | solution.py:454
  28.6 5.7 %collective-permute-start.12 = (bf16[64,256]{1,0:T(8,128)(2,1)S(1)}, bf16[64,256]{1,0:T(8,128)(2,1)S(1)}, u32[]{:S(2)}, u32[]{:S(2)}) collective-permute-start(bf16[64,256]{1,0:T(8,128)(2,1)S(1)} %get-tuple-element.50), channel_id=1, source_target_pairs={{0,6},{1,7},{2,4},{3,5},{4,2},{5,3},{6,0},{7,1},{8,14},{9,15},{10,... | collective-permute-start | bytes 98312 | tf_op jit(solution)/shard_map/ppermute | solution.py:454
  35.1 6.6 %collective-permute-start.13 = (bf16[256,256]{1,0:T(8,128)(2,1)}, bf16[256,256]{1,0:T(8,128)(2,1)}, u32[]{:S(2)}, u32[]{:S(2)}) collective-permute-start(bf16[256,256]{1,0:T(8,128)(2,1)} %get-tuple-element.52), channel_id=1, source_target_pairs={{0,24},{8,16},{16,8},{24,0},{1,25},{9,17},{17,9},{25,1},{2,26},{10... | collective-permute-start | bytes 393224 | tf_op jit(solution)/shard_map/ppermute | solution.py:454
  36.1 6.7 %collective-permute-start.14 = (bf16[256,256]{1,0:T(8,128)(2,1)}, bf16[256,256]{1,0:T(8,128)(2,1)S(1)}, u32[]{:S(2)}, u32[]{:S(2)}) collective-permute-start(bf16[256,256]{1,0:T(8,128)(2,1)} %get-tuple-element.53), channel_id=1, source_target_pairs={{0,8},{8,0},{16,24},{24,16},{1,9},{9,1},{17,25},{25,17},{2,10},{10... | collective-permute-start | bytes 393224 | tf_op jit(solution)/shard_map/ppermute | solution.py:454
  37.1 6.1 %collective-permute-start.15 = (bf16[256,256]{1,0:T(8,128)(2,1)}, bf16[256,256]{1,0:T(8,128)(2,1)S(1)}, u32[]{:S(2)}, u32[]{:S(2)}) collective-permute-start(bf16[256,256]{1,0:T(8,128)(2,1)} %get-tuple-element.54), channel_id=1, source_target_pairs={{0,16},{8,24},{16,0},{24,8},{1,17},{9,25},{17,1},{25,9},{2,18},{10... | collective-permute-start | bytes 393224 | tf_op jit(solution)/shard_map/ppermute | solution.py:454

commit v5 on v3

--- a/solution.py
+++ b/solution.py
@@ -451,8 +451,7 @@
 
 
 def exchange(value, step, size, axis):
-    moved = lax.ppermute(value, axis, [(i, i ^ step) for i in range(size)])
-    return pltpu.with_memory_space_constraint(moved, pltpu.VMEM)
+    return lax.ppermute(value, axis, [(i, i ^ step) for i in range(size)])
 
 
 def body(
@@ -505,7 +504,7 @@
     *out, both = first_functions(leave, acted, other, basis, more)
     blocks = {j: exchange(out[i], 2 * j, narrow, "narrow") for i, j in enumerate(leave)}
     grid = assemble([functions(both, where[0])] + [blocks[j] for j in range(1, chips)])
-    steps = [wide - 1] + order
+    steps = order[:1] + [wide - 1] + order[1:]
     grids = {k: exchange(grid, k, wide, "wide") for k in steps}
     total = diagonal(block_pad, coeff, groupb_row_energy, groupa_energy)
     total = backward_more(wide, 0, total, rolled, grid)

time: 43.7 us -> 43.9 us (level)
  transfers between devices with their start and end apart: 16 -> 16, of which waited for: 7 -> 9; matrix products, arithmetic and copies ran while one was open for 1% -> 1% of each run, Pallas kernels for 15% -> 15%
where the time goes in v5:
time: 43.9 us; the launch traced here: 43.7 us
  starting transfers between devices  20.7 us (47%)
  Pallas kernels  11.3 us (26%)
  waiting for transfers between devices  11.1 us (25%)
    ppermute x16, starting transfers between devices, exchange(): return lax.ppermute(value, axis, [(i, i ^ step) for i in range(size)])  20.7 us
    ppermute x16, waiting for transfers between devices, exchange(): return lax.ppermute(value, axis, [(i, i ^ step) for i in range(size)])  11.1 us
    pallas_call x1, Pallas kernels, first(): call(functools.partial(first_kernel, wide, chips), 'forward_first', (arra...  2.33 us
    pallas_call x3, Pallas kernels, backward_more(): call(functools.partial(more_kernel, wide, k), 'backward_more', array(tota...  1.8 us
    pallas_call x1, Pallas kernels, last(): call(functools.partial(last_kernel, wide), 'forward_own', (array((own, co...  1.66 us
    pallas_call x1, Pallas kernels, backward_end(): call(functools.partial(end_kernel, wide, k), 'backward_end', array(total....  1.23 us
    pallas_call x1, Pallas kernels, first_functions(): call(functools.partial(first_functions_kernel, leave), 'functions_first',...  1.07 us
  transfers between devices with their start and end apart: 16, of which 9 were waited for; matrix products, arithmetic and copies ran while one was open for 1% of the time, Pallas kernels for 15%

profile of v5, /device:TPU:0, one launch (start us, length us, event | category | flops | bytes accessed | tf_op | source)
XLA Modules:
  0.0 43.7 jit_solution(2505315851022695981)
XLA Ops:
  0.0 2.3 %forward_first.1 = (bf16[256,256]{1,0:T(8,128)(2,1)S(1)}, bf16[256,1024]{1,0:T(8,128)(2,1)S(1)}, bf16[1024,1024]{1,0:T(8,128)(2,1)S(1)}, bf16[2,256,2048]{2,1,0:T(8,128)(2,1)S(1)}, f32[32,2048]{1,0:T(8,128)S(1)}) custom-call(s32[16]{0:T(128)} %level_hbm.1, s32[16]{0:T(128)} %pad_hbm.1, s32[16]{0:T(128)} %shift_hbm.1, bf16[1024,256]{1,0:T(8,128)(2,1)} %coeff_hbm.1, ...), custom_call_target="tpu_custom_call" | custom-call | flops 134217728 | bytes 4194304 | tf_op jit(solution)/shard_map/forward_first/pallas_call | solution.py:149
  2.3 4.0 %collective-permute-start = (bf16[256,256]{1,0:T(8,128)(2,1)S(1)}, bf16[256,256]{1,0:T(8,128)(2,1)S(1)}, u32[]{:S(2)}, u32[]{:S(2)}) collective-permute-start(bf16[256,256]{1,0:T(8,128)(2,1)S(1)} %get-tuple-element.29), channel_id=1, source_target_pairs={{0,24},{8,16},{16,8},{24,0},{1,25},{9,17},{17,9},{25,1},{2,26},{10... | collective-permute-start | bytes 393224 | tf_op jit(solution)/shard_map/ppermute | solution.py:454
  6.7 0.6 %collective-permute-start.4 = (bf16[128,256]{1,0:T(8,128)(2,1)S(1)}, bf16[128,256]{1,0:T(8,128)(2,1)S(1)}, u32[]{:S(2)}, u32[]{:S(2)}) collective-permute-start(bf16[128,256]{1,0:T(8,128)(2,1)S(1)} %get-tuple-element.35), channel_id=1, source_target_pairs={{0,16},{8,24},{16,0},{24,8},{1,17},{9,25},{17,1},{25,9},{2,18},{10... | collective-permute-start | bytes 196616 | tf_op jit(solution)/shard_map/ppermute | solution.py:454
  7.8 2.0 %collective-permute-start.2 = (bf16[128,256]{1,0:T(8,128)(2,1)S(1)}, bf16[128,256]{1,0:T(8,128)(2,1)S(1)}, u32[]{:S(2)}, u32[]{:S(2)}) collective-permute-start(bf16[128,256]{1,0:T(8,128)(2,1)S(1)} %get-tuple-element.31), channel_id=1, source_target_pairs={{0,16},{8,24},{16,0},{24,8},{1,17},{9,25},{17,1},{25,9},{2,18},{10... | collective-permute-start | bytes 196616 | tf_op jit(solution)/shard_map/ppermute | solution.py:454
  9.7 1.5 %collective-permute-start.1 = (bf16[128,256]{1,0:T(8,128)(2,1)S(1)}, bf16[128,256]{1,0:T(8,128)(2,1)S(1)}, u32[]{:S(2)}, u32[]{:S(2)}) collective-permute-start(bf16[128,256]{1,0:T(8,128)(2,1)S(1)} %get-tuple-element.30), channel_id=1, source_target_pairs={{0,8},{8,0},{16,24},{24,16},{1,9},{9,1},{17,25},{25,17},{2,10},{10... | collective-permute-start | bytes 196616 | tf_op jit(solution)/shard_map/ppermute | solution.py:454
  11.2 1.7 %forward_own.1 = (f32[256,256]{1,0:T(8,128)S(1)}, bf16[2,256,2048]{2,1,0:T(8,128)(2,1)S(1)}) custom-call(bf16[256,1024]{1,0:T(8,128)(2,1)S(1)} %get-tuple-element.27.turned_ref, bf16[1024,1024]{1,0:T(8,128)(2,1)S(1)} %get-tuple-element.26.rolled_ref, bf16[2048,2048]{1,0:T(8,128)(2,1)} %basis_hbm.3), custom_call_target="tpu_custom_call" | custom-call | tf_op jit(solution)/shard_map/forward_own/pallas_call | solution.py:206
  13.0 2.7 %collective-permute-start.5 = (bf16[64,256]{1,0:T(8,128)(2,1)S(1)}, bf16[64,256]{1,0:T(8,128)(2,1)S(1)}, u32[]{:S(2)}, u32[]{:S(2)}) collective-permute-start(bf16[64,256]{1,0:T(8,128)(2,1)S(1)} %get-tuple-element.36), channel_id=1, source_target_pairs={{0,4},{1,5},{2,6},{3,7},{4,0},{5,1},{6,2},{7,3},{8,12},{9,13},{10,... | collective-permute-start | bytes 98312 | tf_op jit(solution)/shard_map/ppermute | solution.py:454
  15.6 1.4 %collective-permute-start.6 = (bf16[64,256]{1,0:T(8,128)(2,1)S(1)}, bf16[64,256]{1,0:T(8,128)(2,1)S(1)}, u32[]{:S(2)}, u32[]{:S(2)}) collective-permute-start(bf16[64,256]{1,0:T(8,128)(2,1)S(1)} %get-tuple-element.38), channel_id=1, source_target_pairs={{0,6},{1,7},{2,4},{3,5},{4,2},{5,3},{6,0},{7,1},{8,14},{9,15},{10,... | collective-permute-start | bytes 98312 | tf_op jit(solution)/shard_map/ppermute | solution.py:454
  18.5 2.9 %collective-permute-done.6.x_ref = bf16[64,256]{1,0:T(8,128)(2,1)S(1)} collective-permute-done((bf16[64,256]{1,0:T(8,128)(2,1)S(1)}, bf16[64,256]{1,0:T(8,128)(2,1)S(1)}, u32[]{:S(2)}, u32[]{:S(2)}) %collective-permute-start.6) | collective-permute-done | bytes 32800 | tf_op jit(solution)/shard_map/ppermute | solution.py:454
  22.1 1.5 %collective-permute-done.8.other_ref = f32[32,2048]{1,0:T(8,128)S(1)} collective-permute-done((f32[32,2048]{1,0:T(8,128)S(1)}, f32[32,2048]{1,0:T(8,128)S(1)}, u32[]{:S(2)}, u32[]{:S(2)}) %collective-permute-start.8) | collective-permute-done | bytes 262176 | tf_op jit(solution)/shard_map/ppermute | solution.py:454
  23.8 1.2 %collective-permute-done.9.other_ref = bf16[32,2048]{1,0:T(8,128)(2,1)S(1)} collective-permute-done((bf16[32,2048]{1,0:T(8,128)(2,1)S(1)}, bf16[32,2048]{1,0:T(8,128)(2,1)S(1)}, u32[]{:S(2)}, u32[]{:S(2)}) %collective-permute-start.9) | collective-permute-done | bytes 131104 | tf_op jit(solution)/shard_map/ppermute | solution.py:454
  25.0 1.1 %functions_first.1 = (bf16[64,256]{1,0:T(8,128)(2,1)S(1)}, bf16[64,256]{1,0:T(8,128)(2,1)S(1)}, bf16[64,256]{1,0:T(8,128)(2,1)S(1)}, bf16[64,2048]{1,0:T(8,128)(2,1)S(1)}) custom-call(bf16[32,2048]{1,0:T(8,128)(2,1)S(1)} %act.1.mine_ref, bf16[32,2048]{1,0:T(8,128)(2,1)S(1)} %collective-permute-done.9.other_ref, ...), custom_call_target="tpu_custom_call" | custom-call | tf_op jit(solution)/shard_map/functions_first/pallas_call | solution.py:332
  26.2 2.4 %collective-permute-start.11 = (bf16[64,256]{1,0:T(8,128)(2,1)S(1)}, bf16[64,256]{1,0:T(8,128)(2,1)S(1)}, u32[]{:S(2)}, u32[]{:S(2)}) collective-permute-start(bf16[64,256]{1,0:T(8,128)(2,1)S(1)} %get-tuple-element.45), channel_id=1, source_target_pairs={{0,4},{1,5},{2,6},{3,7},{4,0},{5,1},{6,2},{7,3},{8,12},{9,13},{10,... | collective-permute-start | bytes 98312 | tf_op jit(solution)/shard_map/ppermute | solution.py:454
  28.6 2.0 %collective-permute-start.12 = (bf16[64,256]{1,0:T(8,128)(2,1)S(1)}, bf16[64,256]{1,0:T(8,128)(2,1)S(1)}, u32[]{:S(2)}, u32[]{:S(2)}) collective-permute-start(bf16[64,256]{1,0:T(8,128)(2,1)S(1)} %get-tuple-element.46), channel_id=1, source_target_pairs={{0,6},{1,7},{2,4},{3,5},{4,2},{5,3},{6,0},{7,1},{8,14},{9,15},{10,... | collective-permute-start | bytes 98312 | tf_op jit(solution)/shard_map/ppermute | solution.py:454
  31.1 0.6 %collective-permute-done.11.refs_2_ = bf16[64,256]{1,0:T(8,128)(2,1)S(1)} collective-permute-done((bf16[64,256]{1,0:T(8,128)(2,1)S(1)}, bf16[64,256]{1,0:T(8,128)(2,1)S(1)}, u32[]{:S(2)}, u32[]{:S(2)}) %collective-permute-start.11) | collective-permute-done | bytes 32800 | tf_op jit(solution)/shard_map/ppermute | solution.py:454
  31.7 2.6 %collective-permute-done.12.refs_3_ = bf16[64,256]{1,0:T(8,128)(2,1)S(1)} collective-permute-done((bf16[64,256]{1,0:T(8,128)(2,1)S(1)}, bf16[64,256]{1,0:T(8,128)(2,1)S(1)}, u32[]{:S(2)}, u32[]{:S(2)}) %collective-permute-start.12) | collective-permute-done | bytes 32800 | tf_op jit(solution)/shard_map/ppermute | solution.py:454
  34.3 0.6 %collective-permute-start.13 = (bf16[256,256]{1,0:T(8,128)(2,1)S(1)}, bf16[256,256]{1,0:T(8,128)(2,1)}, u32[]{:S(2)}, u32[]{:S(2)}) collective-permute-start(bf16[256,256]{1,0:T(8,128)(2,1)S(1)} %assemble.1.grid_ref), channel_id=1, source_target_pairs={{0,8},{8,0},{16,24},{24,16},{1,9},{9,1},{17,25},{25,17},{2,10},{10... | collective-permute-start | bytes 393224 | tf_op jit(solution)/shard_map/ppermute | solution.py:454
  34.9 1.5 %collective-permute-start.14 = (bf16[256,256]{1,0:T(8,128)(2,1)S(1)}, bf16[256,256]{1,0:T(8,128)(2,1)S(1)}, u32[]{:S(2)}, u32[]{:S(2)}) collective-permute-start(bf16[256,256]{1,0:T(8,128)(2,1)S(1)} %assemble.1.grid_ref), channel_id=1, source_target_pairs={{0,24},{8,16},{16,8},{24,0},{1,25},{9,17},{17,9},{25,1},{2,26},{10... | collective-permute-start | bytes 393224 | tf_op jit(solution)/shard_map/ppermute | solution.py:454
  36.4 1.5 %collective-permute-start.15 = (bf16[256,256]{1,0:T(8,128)(2,1)S(1)}, bf16[256,256]{1,0:T(8,128)(2,1)S(1)}, u32[]{:S(2)}, u32[]{:S(2)}) collective-permute-start(bf16[256,256]{1,0:T(8,128)(2,1)S(1)} %assemble.1.grid_ref), channel_id=1, source_target_pairs={{0,16},{8,24},{16,0},{24,8},{1,17},{9,25},{17,1},{25,9},{2,18},{10... | collective-permute-start | bytes 393224 | tf_op jit(solution)/shard_map/ppermute | solution.py:454
  38.2 0.8 %diagonal.1.total_ref = f32[1024,256]{1,0:T(8,128)S(1)} custom-call(s32[16]{0:T(128)S(1)} %copy-done.1, bf16[1024,256]{1,0:T(8,128)(2,1)S(1)} %copy-done, f32[1024,1]{1,0:T(8,128)S(1)} %copy.10.row_ref, f32[1,256]{1,0:T(1,128)S(1)} %bitcast.3), custom_call_target="tpu_custom_call" | custom-call | tf_op jit(solution)/shard_map/diagonal/pallas_call | solution.py:395
  39.2 0.6 %collective-permute-done.13.grid_ref = bf16[256,256]{1,0:T(8,128)(2,1)} collective-permute-done((bf16[256,256]{1,0:T(8,128)(2,1)S(1)}, bf16[256,256]{1,0:T(8,128)(2,1)}, u32[]{:S(2)}, u32[]{:S(2)}) %collective-permute-start.13) | collective-permute-done | bytes 131104 | tf_op jit(solution)/shard_map/ppermute | solution.py:454
  39.8 1.2 %backward_more.4.total_ref = f32[1024,256]{1,0:T(8,128)S(1)} custom-call(f32[1024,256]{1,0:T(8,128)S(1)} %backward_more.3.total_ref, bf16[1024,1024]{1,0:T(8,128)(2,1)S(1)} %get-tuple-element.26.rolled_ref, bf16[256,256]{1,0:T(8,128)(2,1)} %collective-permute-done.13.grid_ref), custom_call_target="tpu_custom_call" | custom-call | flops 134217728 | bytes 3145728 | tf_op jit(solution)/shard_map/backward_more/pallas_call | solution.py:412
  41.5 1.0 %collective-permute-done.15.grid_ref = bf16[256,256]{1,0:T(8,128)(2,1)S(1)} collective-permute-done((bf16[256,256]{1,0:T(8,128)(2,1)S(1)}, bf16[256,256]{1,0:T(8,128)(2,1)S(1)}, u32[]{:S(2)}, u32[]{:S(2)}) %collective-permute-start.15) | collective-permute-done | bytes 131104 | tf_op jit(solution)/shard_map/ppermute | solution.py:454
  42.5 1.2 %backward_end.1 = f32[1024,256]{1,0:T(8,128)} custom-call(f32[1024,256]{1,0:T(8,128)S(1)} %backward_more.5.total_ref, bf16[1024,1024]{1,0:T(8,128)(2,1)S(1)} %get-tuple-element.26.rolled_ref, bf16[256,256]{1,0:T(8,128)(2,1)S(1)} %collective-permute-done.15.grid_ref), custom_call_target="tpu_custom_call" | custom-call | flops 134217728 | bytes 4194304 | tf_op jit(solution)/shard_map/backward_end/pallas_call | solution.py:441
  (36 shorter events, 4.9 us)
Async XLA Ops:
  2.3 10.6 %collective-permute-start = (bf16[256,256]{1,0:T(8,128)(2,1)S(1)}, bf16[256,256]{1,0:T(8,128)(2,1)S(1)}, u32[]{:S(2)}, u32[]{:S(2)}) collective-permute-start(bf16[256,256]{1,0:T(8,128)(2,1)S(1)} %get-tuple-element.29), channel_id=1, source_target_pairs={{0,24},{8,16},{16,8},{24,0},{1,25},{9,17},{17,9},{25,1},{2,26},{10... | collective-permute-start | bytes 393224 | tf_op jit(solution)/shard_map/ppermute | solution.py:454
  6.7 6.2 %collective-permute-start.4 = (bf16[128,256]{1,0:T(8,128)(2,1)S(1)}, bf16[128,256]{1,0:T(8,128)(2,1)S(1)}, u32[]{:S(2)}, u32[]{:S(2)}) collective-permute-start(bf16[128,256]{1,0:T(8,128)(2,1)S(1)} %get-tuple-element.35), channel_id=1, source_target_pairs={{0,16},{8,24},{16,0},{24,8},{1,17},{9,25},{17,1},{25,9},{2,18},{10... | collective-permute-start | bytes 196616 | tf_op jit(solution)/shard_map/ppermute | solution.py:454
  7.6 5.3 %collective-permute-start.3 = (bf16[128,256]{1,0:T(8,128)(2,1)S(1)}, bf16[128,256]{1,0:T(8,128)(2,1)S(1)}, u32[]{:S(2)}, u32[]{:S(2)}) collective-permute-start(bf16[128,256]{1,0:T(8,128)(2,1)S(1)} %get-tuple-element.34), channel_id=1, source_target_pairs={{0,8},{8,0},{16,24},{24,16},{1,9},{9,1},{17,25},{25,17},{2,10},{10... | collective-permute-start | bytes 196616 | tf_op jit(solution)/shard_map/ppermute | solution.py:454
  7.8 9.2 %collective-permute-start.2 = (bf16[128,256]{1,0:T(8,128)(2,1)S(1)}, bf16[128,256]{1,0:T(8,128)(2,1)S(1)}, u32[]{:S(2)}, u32[]{:S(2)}) collective-permute-start(bf16[128,256]{1,0:T(8,128)(2,1)S(1)} %get-tuple-element.31), channel_id=1, source_target_pairs={{0,16},{8,24},{16,0},{24,8},{1,17},{9,25},{17,1},{25,9},{2,18},{10... | collective-permute-start | bytes 196616 | tf_op jit(solution)/shard_map/ppermute | solution.py:454
  9.7 7.3 %collective-permute-start.1 = (bf16[128,256]{1,0:T(8,128)(2,1)S(1)}, bf16[128,256]{1,0:T(8,128)(2,1)S(1)}, u32[]{:S(2)}, u32[]{:S(2)}) collective-permute-start(bf16[128,256]{1,0:T(8,128)(2,1)S(1)} %get-tuple-element.30), channel_id=1, source_target_pairs={{0,8},{8,0},{16,24},{24,16},{1,9},{9,1},{17,25},{25,17},{2,10},{10... | collective-permute-start | bytes 196616 | tf_op jit(solution)/shard_map/ppermute | solution.py:454
  13.0 5.2 %collective-permute-start.5 = (bf16[64,256]{1,0:T(8,128)(2,1)S(1)}, bf16[64,256]{1,0:T(8,128)(2,1)S(1)}, u32[]{:S(2)}, u32[]{:S(2)}) collective-permute-start(bf16[64,256]{1,0:T(8,128)(2,1)S(1)} %get-tuple-element.36), channel_id=1, source_target_pairs={{0,4},{1,5},{2,6},{3,7},{4,0},{5,1},{6,2},{7,3},{8,12},{9,13},{10,... | collective-permute-start | bytes 98312 | tf_op jit(solution)/shard_map/ppermute | solution.py:454
  15.6 5.7 %collective-permute-start.6 = (bf16[64,256]{1,0:T(8,128)(2,1)S(1)}, bf16[64,256]{1,0:T(8,128)(2,1)S(1)}, u32[]{:S(2)}, u32[]{:S(2)}) collective-permute-start(bf16[64,256]{1,0:T(8,128)(2,1)S(1)} %get-tuple-element.38), channel_id=1, source_target_pairs={{0,6},{1,7},{2,4},{3,5},{4,2},{5,3},{6,0},{7,1},{8,14},{9,15},{10,... | collective-permute-start | bytes 98312 | tf_op jit(solution)/shard_map/ppermute | solution.py:454
  17.0 4.6 %collective-permute-start.7 = (bf16[64,256]{1,0:T(8,128)(2,1)S(1)}, bf16[64,256]{1,0:T(8,128)(2,1)S(1)}, u32[]{:S(2)}, u32[]{:S(2)}) collective-permute-start(bf16[64,256]{1,0:T(8,128)(2,1)S(1)} %get-tuple-element.39), channel_id=1, source_target_pairs={{0,2},{1,3},{2,0},{3,1},{4,6},{5,7},{6,4},{7,5},{8,10},{9,11},{10,... | collective-permute-start | bytes 98312 | tf_op jit(solution)/shard_map/ppermute | solution.py:454
  22.0 1.6 %collective-permute-start.8 = (f32[32,2048]{1,0:T(8,128)S(1)}, f32[32,2048]{1,0:T(8,128)S(1)}, u32[]{:S(2)}, u32[]{:S(2)}) collective-permute-start(f32[32,2048]{1,0:T(8,128)S(1)} %get-tuple-element.41), channel_id=1, source_target_pairs={{0,1},{1,0},{2,3},{3,2},{4,5},{5,4},{6,7},{7,6},{8,9},{9,8},{10,11... | collective-permute-start | bytes 786440 | tf_op jit(solution)/shard_map/ppermute | solution.py:454
  23.6 1.4 %collective-permute-start.9 = (bf16[32,2048]{1,0:T(8,128)(2,1)S(1)}, bf16[32,2048]{1,0:T(8,128)(2,1)S(1)}, u32[]{:S(2)}, u32[]{:S(2)}) collective-permute-start(bf16[32,2048]{1,0:T(8,128)(2,1)S(1)} %act.1.mine_ref), channel_id=1, source_target_pairs={{0,1},{1,0},{2,3},{3,2},{4,5},{5,4},{6,7},{7,6},{8,9},{9,8},{10,11... | collective-permute-start | bytes 393224 | tf_op jit(solution)/shard_map/ppermute | solution.py:454
  26.1 11.8 %copy-start.3 = (f32[1024]{0:T(1024)S(1)}, f32[1024]{0:T(1024)}, u32[]{:S(2)}) copy-start(f32[1024]{0:T(1024)} %param.10) | copy-start | bytes 12292
  26.1 12.0 %copy-start = (bf16[1024,256]{1,0:T(8,128)(2,1)S(1)}, bf16[1024,256]{1,0:T(8,128)(2,1)}, u32[]{:S(2)}) copy-start(bf16[1024,256]{1,0:T(8,128)(2,1)} %coeff_hbm.1) | copy-start | bytes 1572868
  26.1 12.0 %copy-start.1 = (s32[16]{0:T(128)S(1)}, s32[16]{0:T(128)}, u32[]{:S(2)}) copy-start(s32[16]{0:T(128)} %pad_hbm.1) | copy-start | bytes 196
  26.2 12.0 %copy-start.2 = (f32[256]{0:T(256)S(1)}, f32[256]{0:T(256)}, u32[]{:S(2)}) copy-start(f32[256]{0:T(256)} %param.11) | copy-start | bytes 3076
  26.2 4.9 %collective-permute-start.10 = (bf16[64,256]{1,0:T(8,128)(2,1)S(1)}, bf16[64,256]{1,0:T(8,128)(2,1)S(1)}, u32[]{:S(2)}, u32[]{:S(2)}) collective-permute-start(bf16[64,256]{1,0:T(8,128)(2,1)S(1)} %get-tuple-element.44), channel_id=1, source_target_pairs={{0,2},{1,3},{2,0},{3,1},{4,6},{5,7},{6,4},{7,5},{8,10},{9,11},{10,... | collective-permute-start | bytes 98312 | tf_op jit(solution)/shard_map/ppermute | solution.py:454
  26.2 5.4 %collective-permute-start.11 = (bf16[64,256]{1,0:T(8,128)(2,1)S(1)}, bf16[64,256]{1,0:T(8,128)(2,1)S(1)}, u32[]{:S(2)}, u32[]{:S(2)}) collective-permute-start(bf16[64,256]{1,0:T(8,128)(2,1)S(1)} %get-tuple-element.45), channel_id=1, source_target_pairs={{0,4},{1,5},{2,6},{3,7},{4,0},{5,1},{6,2},{7,3},{8,12},{9,13},{10,... | collective-permute-start | bytes 98312 | tf_op jit(solution)/shard_map/ppermute | solution.py:454
  28.6 5.7 %collective-permute-start.12 = (bf16[64,256]{1,0:T(8,128)(2,1)S(1)}, bf16[64,256]{1,0:T(8,128)(2,1)S(1)}, u32[]{:S(2)}, u32[]{:S(2)}) collective-permute-start(bf16[64,256]{1,0:T(8,128)(2,1)S(1)} %get-tuple-element.46), channel_id=1, source_target_pairs={{0,6},{1,7},{2,4},{3,5},{4,2},{5,3},{6,0},{7,1},{8,14},{9,15},{10,... | collective-permute-start | bytes 98312 | tf_op jit(solution)/shard_map/ppermute | solution.py:454
  34.3 5.5 %collective-permute-start.13 = (bf16[256,256]{1,0:T(8,128)(2,1)S(1)}, bf16[256,256]{1,0:T(8,128)(2,1)}, u32[]{:S(2)}, u32[]{:S(2)}) collective-permute-start(bf16[256,256]{1,0:T(8,128)(2,1)S(1)} %assemble.1.grid_ref), channel_id=1, source_target_pairs={{0,8},{8,0},{16,24},{24,16},{1,9},{9,1},{17,25},{25,17},{2,10},{10... | collective-permute-start | bytes 393224 | tf_op jit(solution)/shard_map/ppermute | solution.py:454
  34.9 6.2 %collective-permute-start.14 = (bf16[256,256]{1,0:T(8,128)(2,1)S(1)}, bf16[256,256]{1,0:T(8,128)(2,1)S(1)}, u32[]{:S(2)}, u32[]{:S(2)}) collective-permute-start(bf16[256,256]{1,0:T(8,128)(2,1)S(1)} %assemble.1.grid_ref), channel_id=1, source_target_pairs={{0,24},{8,16},{16,8},{24,0},{1,25},{9,17},{17,9},{25,1},{2,26},{10... | collective-permute-start | bytes 393224 | tf_op jit(solution)/shard_map/ppermute | solution.py:454
  36.4 6.1 %collective-permute-start.15 = (bf16[256,256]{1,0:T(8,128)(2,1)S(1)}, bf16[256,256]{1,0:T(8,128)(2,1)S(1)}, u32[]{:S(2)}, u32[]{:S(2)}) collective-permute-start(bf16[256,256]{1,0:T(8,128)(2,1)S(1)} %assemble.1.grid_ref), channel_id=1, source_target_pairs={{0,16},{8,24},{16,0},{24,8},{1,17},{9,25},{17,1},{25,9},{2,18},{10... | collective-permute-start | bytes 393224 | tf_op jit(solution)/shard_map/ppermute | solution.py:454

commit v6 on v5

--- a/solution.py
+++ b/solution.py
@@ -357,20 +357,20 @@
     )(both, basis)
 
 
-def assemble_kernel(*refs):
+def assemble_kernel(visits, *refs):
     parts, out_ref = refs[:-1], refs[-1]
     chip = lax.axis_index("narrow") // 2
     rows = parts[0].shape[0]
-    for j, part in enumerate(parts):
+    for j, part in zip(visits, parts):
         start = pl.multiple_of((chip ^ j) * rows, rows)
         out_ref[pl.ds(start, rows), :] = part[...]
 
 
-def assemble(parts):
+def assemble(visits, parts):
     rows, columns = parts[0].shape
     chips = len(parts)
     return call(
-        assemble_kernel,
+        functools.partial(assemble_kernel, visits),
         "assemble",
         array((rows * chips, columns), BF16),
         [VMEM] * chips,
@@ -500,11 +500,11 @@
     mine, theirs = last_points(total, xs[visits[-1]], where[visits[-1]])
     acted = act(mine, exchange(theirs, 1, narrow, "narrow"), pot)
     other = exchange(acted, 1, narrow, "narrow")
-    leave = list(reversed(range(1, chips)))
+    leave = visits
     *out, both = first_functions(leave, acted, other, basis, more)
     blocks = {j: exchange(out[i], 2 * j, narrow, "narrow") for i, j in enumerate(leave)}
-    grid = assemble([functions(both, where[0])] + [blocks[j] for j in range(1, chips)])
-    steps = order[:1] + [wide - 1] + order[1:]
+    grid = assemble([0] + leave, [functions(both, where[0])] + [blocks[j] for j in leave])
+    steps = [wide - 1] + order
     grids = {k: exchange(grid, k, wide, "wide") for k in steps}
     total = diagonal(block_pad, coeff, groupb_row_energy, groupa_energy)
     total = backward_more(wide, 0, total, rolled, grid)

time: 43.9 us -> 42.6 us (0.970)
  starting transfers between devices: 20.7 us -> 19.8 us
    ppermute x16, starting transfers between devices: 20.7 us -> 19.8 us  [exchange(): return lax.ppermute(value, axis, [(i, i ^ step) for i in range(size)])]
  transfers between devices with their start and end apart: 16 -> 16, of which waited for: 9 -> 7; matrix products, arithmetic and copies ran while one was open for 1% -> 1% of each run, Pallas kernels for 15% -> 15%
where the time goes in v6:
time: 42.6 us; the launch traced here: 42.5 us
  starting transfers between devices  19.8 us (46%)
  Pallas kernels  11.3 us (27%)
  waiting for transfers between devices  10.8 us (25%)
    ppermute x16, starting transfers between devices, exchange(): return lax.ppermute(value, axis, [(i, i ^ step) for i in range(size)])  19.8 us
    ppermute x16, waiting for transfers between devices, exchange(): return lax.ppermute(value, axis, [(i, i ^ step) for i in range(size)])  10.8 us
    pallas_call x1, Pallas kernels, first(): call(functools.partial(first_kernel, wide, chips), 'forward_first', (arra...  2.33 us
    pallas_call x3, Pallas kernels, backward_more(): call(functools.partial(more_kernel, wide, k), 'backward_more', array(tota...  1.79 us
    pallas_call x1, Pallas kernels, last(): call(functools.partial(last_kernel, wide), 'forward_own', (array((own, co...  1.66 us
    pallas_call x1, Pallas kernels, backward_end(): call(functools.partial(end_kernel, wide, k), 'backward_end', array(total....  1.23 us
    pallas_call x1, Pallas kernels, first_functions(): call(functools.partial(first_functions_kernel, leave), 'functions_first',...  1.07 us
  transfers between devices with their start and end apart: 16, of which 7 were waited for; matrix products, arithmetic and copies ran while one was open for 1% of the time, Pallas kernels for 15%

profile of v6, /device:TPU:0, one launch (start us, length us, event | category | flops | bytes accessed | tf_op | source)
XLA Modules:
  0.0 42.5 jit_solution(17455712456758925279)
XLA Ops:
  0.0 2.3 %forward_first.1 = (bf16[256,256]{1,0:T(8,128)(2,1)S(1)}, bf16[256,1024]{1,0:T(8,128)(2,1)S(1)}, bf16[1024,1024]{1,0:T(8,128)(2,1)S(1)}, bf16[2,256,2048]{2,1,0:T(8,128)(2,1)S(1)}, f32[32,2048]{1,0:T(8,128)S(1)}) custom-call(s32[16]{0:T(128)} %level_hbm.1, s32[16]{0:T(128)} %pad_hbm.1, s32[16]{0:T(128)} %shift_hbm.1, bf16[1024,256]{1,0:T(8,128)(2,1)} %coeff_hbm.1, ...), custom_call_target="tpu_custom_call" | custom-call | flops 134217728 | bytes 4194304 | tf_op jit(solution)/shard_map/forward_first/pallas_call | solution.py:149
  2.3 4.0 %collective-permute-start = (bf16[256,256]{1,0:T(8,128)(2,1)S(1)}, bf16[256,256]{1,0:T(8,128)(2,1)S(1)}, u32[]{:S(2)}, u32[]{:S(2)}) collective-permute-start(bf16[256,256]{1,0:T(8,128)(2,1)S(1)} %get-tuple-element.29), channel_id=1, source_target_pairs={{0,24},{8,16},{16,8},{24,0},{1,25},{9,17},{17,9},{25,1},{2,26},{10... | collective-permute-start | bytes 393224 | tf_op jit(solution)/shard_map/ppermute | solution.py:454
  6.7 0.6 %collective-permute-start.4 = (bf16[128,256]{1,0:T(8,128)(2,1)S(1)}, bf16[128,256]{1,0:T(8,128)(2,1)S(1)}, u32[]{:S(2)}, u32[]{:S(2)}) collective-permute-start(bf16[128,256]{1,0:T(8,128)(2,1)S(1)} %get-tuple-element.35), channel_id=1, source_target_pairs={{0,16},{8,24},{16,0},{24,8},{1,17},{9,25},{17,1},{25,9},{2,18},{10... | collective-permute-start | bytes 196616 | tf_op jit(solution)/shard_map/ppermute | solution.py:454
  7.8 2.0 %collective-permute-start.2 = (bf16[128,256]{1,0:T(8,128)(2,1)S(1)}, bf16[128,256]{1,0:T(8,128)(2,1)S(1)}, u32[]{:S(2)}, u32[]{:S(2)}) collective-permute-start(bf16[128,256]{1,0:T(8,128)(2,1)S(1)} %get-tuple-element.31), channel_id=1, source_target_pairs={{0,16},{8,24},{16,0},{24,8},{1,17},{9,25},{17,1},{25,9},{2,18},{10... | collective-permute-start | bytes 196616 | tf_op jit(solution)/shard_map/ppermute | solution.py:454
  9.7 1.5 %collective-permute-start.1 = (bf16[128,256]{1,0:T(8,128)(2,1)S(1)}, bf16[128,256]{1,0:T(8,128)(2,1)S(1)}, u32[]{:S(2)}, u32[]{:S(2)}) collective-permute-start(bf16[128,256]{1,0:T(8,128)(2,1)S(1)} %get-tuple-element.30), channel_id=1, source_target_pairs={{0,8},{8,0},{16,24},{24,16},{1,9},{9,1},{17,25},{25,17},{2,10},{10... | collective-permute-start | bytes 196616 | tf_op jit(solution)/shard_map/ppermute | solution.py:454
  11.2 1.7 %forward_own.1 = (f32[256,256]{1,0:T(8,128)S(1)}, bf16[2,256,2048]{2,1,0:T(8,128)(2,1)S(1)}) custom-call(bf16[256,1024]{1,0:T(8,128)(2,1)S(1)} %get-tuple-element.27.turned_ref, bf16[1024,1024]{1,0:T(8,128)(2,1)S(1)} %get-tuple-element.26.rolled_ref, bf16[2048,2048]{1,0:T(8,128)(2,1)} %basis_hbm.3), custom_call_target="tpu_custom_call" | custom-call | tf_op jit(solution)/shard_map/forward_own/pallas_call | solution.py:206
  13.0 2.7 %collective-permute-start.5 = (bf16[64,256]{1,0:T(8,128)(2,1)S(1)}, bf16[64,256]{1,0:T(8,128)(2,1)S(1)}, u32[]{:S(2)}, u32[]{:S(2)}) collective-permute-start(bf16[64,256]{1,0:T(8,128)(2,1)S(1)} %get-tuple-element.36), channel_id=1, source_target_pairs={{0,4},{1,5},{2,6},{3,7},{4,0},{5,1},{6,2},{7,3},{8,12},{9,13},{10,... | collective-permute-start | bytes 98312 | tf_op jit(solution)/shard_map/ppermute | solution.py:454
  15.6 1.4 %collective-permute-start.6 = (bf16[64,256]{1,0:T(8,128)(2,1)S(1)}, bf16[64,256]{1,0:T(8,128)(2,1)S(1)}, u32[]{:S(2)}, u32[]{:S(2)}) collective-permute-start(bf16[64,256]{1,0:T(8,128)(2,1)S(1)} %get-tuple-element.38), channel_id=1, source_target_pairs={{0,6},{1,7},{2,4},{3,5},{4,2},{5,3},{6,0},{7,1},{8,14},{9,15},{10,... | collective-permute-start | bytes 98312 | tf_op jit(solution)/shard_map/ppermute | solution.py:454
  18.5 2.9 %collective-permute-done.6.x_ref = bf16[64,256]{1,0:T(8,128)(2,1)S(1)} collective-permute-done((bf16[64,256]{1,0:T(8,128)(2,1)S(1)}, bf16[64,256]{1,0:T(8,128)(2,1)S(1)}, u32[]{:S(2)}, u32[]{:S(2)}) %collective-permute-start.6) | collective-permute-done | bytes 32800 | tf_op jit(solution)/shard_map/ppermute | solution.py:454
  22.1 1.5 %collective-permute-done.8.other_ref = f32[32,2048]{1,0:T(8,128)S(1)} collective-permute-done((f32[32,2048]{1,0:T(8,128)S(1)}, f32[32,2048]{1,0:T(8,128)S(1)}, u32[]{:S(2)}, u32[]{:S(2)}) %collective-permute-start.8) | collective-permute-done | bytes 262176 | tf_op jit(solution)/shard_map/ppermute | solution.py:454
  23.8 1.2 %collective-permute-done.9.other_ref = bf16[32,2048]{1,0:T(8,128)(2,1)S(1)} collective-permute-done((bf16[32,2048]{1,0:T(8,128)(2,1)S(1)}, bf16[32,2048]{1,0:T(8,128)(2,1)S(1)}, u32[]{:S(2)}, u32[]{:S(2)}) %collective-permute-start.9) | collective-permute-done | bytes 131104 | tf_op jit(solution)/shard_map/ppermute | solution.py:454
  25.0 1.1 %functions_first.1 = (bf16[64,256]{1,0:T(8,128)(2,1)S(1)}, bf16[64,256]{1,0:T(8,128)(2,1)S(1)}, bf16[64,256]{1,0:T(8,128)(2,1)S(1)}, bf16[64,2048]{1,0:T(8,128)(2,1)S(1)}) custom-call(bf16[32,2048]{1,0:T(8,128)(2,1)S(1)} %act.1.mine_ref, bf16[32,2048]{1,0:T(8,128)(2,1)S(1)} %collective-permute-done.9.other_ref, ...), custom_call_target="tpu_custom_call" | custom-call | tf_op jit(solution)/shard_map/functions_first/pallas_call | solution.py:332
  26.2 1.1 %collective-permute-start.10 = (bf16[64,256]{1,0:T(8,128)(2,1)S(1)}, bf16[64,256]{1,0:T(8,128)(2,1)S(1)}, u32[]{:S(2)}, u32[]{:S(2)}) collective-permute-start(bf16[64,256]{1,0:T(8,128)(2,1)S(1)} %get-tuple-element.44), channel_id=1, source_target_pairs={{0,4},{1,5},{2,6},{3,7},{4,0},{5,1},{6,2},{7,3},{8,12},{9,13},{10,... | collective-permute-start | bytes 98312 | tf_op jit(solution)/shard_map/ppermute | solution.py:454
  27.3 1.1 %collective-permute-start.11 = (bf16[64,256]{1,0:T(8,128)(2,1)S(1)}, bf16[64,256]{1,0:T(8,128)(2,1)S(1)}, u32[]{:S(2)}, u32[]{:S(2)}) collective-permute-start(bf16[64,256]{1,0:T(8,128)(2,1)S(1)} %get-tuple-element.45), channel_id=1, source_target_pairs={{0,6},{1,7},{2,4},{3,5},{4,2},{5,3},{6,0},{7,1},{8,14},{9,15},{10,... | collective-permute-start | bytes 98312 | tf_op jit(solution)/shard_map/ppermute | solution.py:454
  28.4 1.4 %collective-permute-start.12 = (bf16[64,256]{1,0:T(8,128)(2,1)S(1)}, bf16[64,256]{1,0:T(8,128)(2,1)S(1)}, u32[]{:S(2)}, u32[]{:S(2)}) collective-permute-start(bf16[64,256]{1,0:T(8,128)(2,1)S(1)} %get-tuple-element.46), channel_id=1, source_target_pairs={{0,2},{1,3},{2,0},{3,1},{4,6},{5,7},{6,4},{7,5},{8,10},{9,11},{10,... | collective-permute-start | bytes 98312 | tf_op jit(solution)/shard_map/ppermute | solution.py:454
  30.2 1.1 %collective-permute-done.10.refs_1_ = bf16[64,256]{1,0:T(8,128)(2,1)S(1)} collective-permute-done((bf16[64,256]{1,0:T(8,128)(2,1)S(1)}, bf16[64,256]{1,0:T(8,128)(2,1)S(1)}, u32[]{:S(2)}, u32[]{:S(2)}) %collective-permute-start.10) | collective-permute-done | bytes 32800 | tf_op jit(solution)/shard_map/ppermute | solution.py:454
  31.3 1.7 %collective-permute-done.11.refs_2_ = bf16[64,256]{1,0:T(8,128)(2,1)S(1)} collective-permute-done((bf16[64,256]{1,0:T(8,128)(2,1)S(1)}, bf16[64,256]{1,0:T(8,128)(2,1)S(1)}, u32[]{:S(2)}, u32[]{:S(2)}) %collective-permute-start.11) | collective-permute-done | bytes 32800 | tf_op jit(solution)/shard_map/ppermute | solution.py:454
  33.0 1.1 %collective-permute-start.13 = (bf16[256,256]{1,0:T(8,128)(2,1)S(1)}, bf16[256,256]{1,0:T(8,128)(2,1)}, u32[]{:S(2)}, u32[]{:S(2)}) collective-permute-start(bf16[256,256]{1,0:T(8,128)(2,1)S(1)} %assemble.1.grid_ref), channel_id=1, source_target_pairs={{0,24},{8,16},{16,8},{24,0},{1,25},{9,17},{17,9},{25,1},{2,26},{10... | collective-permute-start | bytes 393224 | tf_op jit(solution)/shard_map/ppermute | solution.py:454
  34.1 1.0 %collective-permute-start.14 = (bf16[256,256]{1,0:T(8,128)(2,1)S(1)}, bf16[256,256]{1,0:T(8,128)(2,1)S(1)}, u32[]{:S(2)}, u32[]{:S(2)}) collective-permute-start(bf16[256,256]{1,0:T(8,128)(2,1)S(1)} %assemble.1.grid_ref), channel_id=1, source_target_pairs={{0,8},{8,0},{16,24},{24,16},{1,9},{9,1},{17,25},{25,17},{2,10},{10... | collective-permute-start | bytes 393224 | tf_op jit(solution)/shard_map/ppermute | solution.py:454
  35.1 1.5 %collective-permute-start.15 = (bf16[256,256]{1,0:T(8,128)(2,1)S(1)}, bf16[256,256]{1,0:T(8,128)(2,1)S(1)}, u32[]{:S(2)}, u32[]{:S(2)}) collective-permute-start(bf16[256,256]{1,0:T(8,128)(2,1)S(1)} %assemble.1.grid_ref), channel_id=1, source_target_pairs={{0,16},{8,24},{16,0},{24,8},{1,17},{9,25},{17,1},{25,9},{2,18},{10... | collective-permute-start | bytes 393224 | tf_op jit(solution)/shard_map/ppermute | solution.py:454
  36.8 0.8 %diagonal.1.total_ref = f32[1024,256]{1,0:T(8,128)S(1)} custom-call(s32[16]{0:T(128)S(1)} %copy-done.1, bf16[1024,256]{1,0:T(8,128)(2,1)S(1)} %copy-done, f32[1024,1]{1,0:T(8,128)S(1)} %copy.10.row_ref, f32[1,256]{1,0:T(1,128)S(1)} %bitcast.3), custom_call_target="tpu_custom_call" | custom-call | tf_op jit(solution)/shard_map/diagonal/pallas_call | solution.py:395
  37.9 1.8 %collective-permute-done.13.grid_ref = bf16[256,256]{1,0:T(8,128)(2,1)} collective-permute-done((bf16[256,256]{1,0:T(8,128)(2,1)S(1)}, bf16[256,256]{1,0:T(8,128)(2,1)}, u32[]{:S(2)}, u32[]{:S(2)}) %collective-permute-start.13) | collective-permute-done | bytes 131104 | tf_op jit(solution)/shard_map/ppermute | solution.py:454
  39.7 1.2 %backward_more.4.total_ref = f32[1024,256]{1,0:T(8,128)S(1)} custom-call(f32[1024,256]{1,0:T(8,128)S(1)} %backward_more.3.total_ref, bf16[1024,1024]{1,0:T(8,128)(2,1)S(1)} %get-tuple-element.26.rolled_ref, bf16[256,256]{1,0:T(8,128)(2,1)} %collective-permute-done.13.grid_ref), custom_call_target="tpu_custom_call" | custom-call | flops 134217728 | bytes 3145728 | tf_op jit(solution)/shard_map/backward_more/pallas_call | solution.py:412
  41.3 1.2 %backward_end.1 = f32[1024,256]{1,0:T(8,128)} custom-call(f32[1024,256]{1,0:T(8,128)S(1)} %backward_more.5.total_ref, bf16[1024,1024]{1,0:T(8,128)(2,1)S(1)} %get-tuple-element.26.rolled_ref, bf16[256,256]{1,0:T(8,128)(2,1)S(1)} %collective-permute-done.15.grid_ref), custom_call_target="tpu_custom_call" | custom-call | flops 134217728 | bytes 4194304 | tf_op jit(solution)/shard_map/backward_end/pallas_call | solution.py:441
  (36 shorter events, 4.7 us)
Async XLA Ops:
  2.3 10.6 %collective-permute-start = (bf16[256,256]{1,0:T(8,128)(2,1)S(1)}, bf16[256,256]{1,0:T(8,128)(2,1)S(1)}, u32[]{:S(2)}, u32[]{:S(2)}) collective-permute-start(bf16[256,256]{1,0:T(8,128)(2,1)S(1)} %get-tuple-element.29), channel_id=1, source_target_pairs={{0,24},{8,16},{16,8},{24,0},{1,25},{9,17},{17,9},{25,1},{2,26},{10... | collective-permute-start | bytes 393224 | tf_op jit(solution)/shard_map/ppermute | solution.py:454
  6.7 6.2 %collective-permute-start.4 = (bf16[128,256]{1,0:T(8,128)(2,1)S(1)}, bf16[128,256]{1,0:T(8,128)(2,1)S(1)}, u32[]{:S(2)}, u32[]{:S(2)}) collective-permute-start(bf16[128,256]{1,0:T(8,128)(2,1)S(1)} %get-tuple-element.35), channel_id=1, source_target_pairs={{0,16},{8,24},{16,0},{24,8},{1,17},{9,25},{17,1},{25,9},{2,18},{10... | collective-permute-start | bytes 196616 | tf_op jit(solution)/shard_map/ppermute | solution.py:454
  7.6 5.3 %collective-permute-start.3 = (bf16[128,256]{1,0:T(8,128)(2,1)S(1)}, bf16[128,256]{1,0:T(8,128)(2,1)S(1)}, u32[]{:S(2)}, u32[]{:S(2)}) collective-permute-start(bf16[128,256]{1,0:T(8,128)(2,1)S(1)} %get-tuple-element.34), channel_id=1, source_target_pairs={{0,8},{8,0},{16,24},{24,16},{1,9},{9,1},{17,25},{25,17},{2,10},{10... | collective-permute-start | bytes 196616 | tf_op jit(solution)/shard_map/ppermute | solution.py:454
  7.8 9.2 %collective-permute-start.2 = (bf16[128,256]{1,0:T(8,128)(2,1)S(1)}, bf16[128,256]{1,0:T(8,128)(2,1)S(1)}, u32[]{:S(2)}, u32[]{:S(2)}) collective-permute-start(bf16[128,256]{1,0:T(8,128)(2,1)S(1)} %get-tuple-element.31), channel_id=1, source_target_pairs={{0,16},{8,24},{16,0},{24,8},{1,17},{9,25},{17,1},{25,9},{2,18},{10... | collective-permute-start | bytes 196616 | tf_op jit(solution)/shard_map/ppermute | solution.py:454
  9.7 7.3 %collective-permute-start.1 = (bf16[128,256]{1,0:T(8,128)(2,1)S(1)}, bf16[128,256]{1,0:T(8,128)(2,1)S(1)}, u32[]{:S(2)}, u32[]{:S(2)}) collective-permute-start(bf16[128,256]{1,0:T(8,128)(2,1)S(1)} %get-tuple-element.30), channel_id=1, source_target_pairs={{0,8},{8,0},{16,24},{24,16},{1,9},{9,1},{17,25},{25,17},{2,10},{10... | collective-permute-start | bytes 196616 | tf_op jit(solution)/shard_map/ppermute | solution.py:454
  13.0 5.2 %collective-permute-start.5 = (bf16[64,256]{1,0:T(8,128)(2,1)S(1)}, bf16[64,256]{1,0:T(8,128)(2,1)S(1)}, u32[]{:S(2)}, u32[]{:S(2)}) collective-permute-start(bf16[64,256]{1,0:T(8,128)(2,1)S(1)} %get-tuple-element.36), channel_id=1, source_target_pairs={{0,4},{1,5},{2,6},{3,7},{4,0},{5,1},{6,2},{7,3},{8,12},{9,13},{10,... | collective-permute-start | bytes 98312 | tf_op jit(solution)/shard_map/ppermute | solution.py:454
  15.6 5.7 %collective-permute-start.6 = (bf16[64,256]{1,0:T(8,128)(2,1)S(1)}, bf16[64,256]{1,0:T(8,128)(2,1)S(1)}, u32[]{:S(2)}, u32[]{:S(2)}) collective-permute-start(bf16[64,256]{1,0:T(8,128)(2,1)S(1)} %get-tuple-element.38), channel_id=1, source_target_pairs={{0,6},{1,7},{2,4},{3,5},{4,2},{5,3},{6,0},{7,1},{8,14},{9,15},{10,... | collective-permute-start | bytes 98312 | tf_op jit(solution)/shard_map/ppermute | solution.py:454
  17.0 4.6 %collective-permute-start.7 = (bf16[64,256]{1,0:T(8,128)(2,1)S(1)}, bf16[64,256]{1,0:T(8,128)(2,1)S(1)}, u32[]{:S(2)}, u32[]{:S(2)}) collective-permute-start(bf16[64,256]{1,0:T(8,128)(2,1)S(1)} %get-tuple-element.39), channel_id=1, source_target_pairs={{0,2},{1,3},{2,0},{3,1},{4,6},{5,7},{6,4},{7,5},{8,10},{9,11},{10,... | collective-permute-start | bytes 98312 | tf_op jit(solution)/shard_map/ppermute | solution.py:454
  22.0 1.6 %collective-permute-start.8 = (f32[32,2048]{1,0:T(8,128)S(1)}, f32[32,2048]{1,0:T(8,128)S(1)}, u32[]{:S(2)}, u32[]{:S(2)}) collective-permute-start(f32[32,2048]{1,0:T(8,128)S(1)} %get-tuple-element.41), channel_id=1, source_target_pairs={{0,1},{1,0},{2,3},{3,2},{4,5},{5,4},{6,7},{7,6},{8,9},{9,8},{10,11... | collective-permute-start | bytes 786440 | tf_op jit(solution)/shard_map/ppermute | solution.py:454
  23.6 1.4 %collective-permute-start.9 = (bf16[32,2048]{1,0:T(8,128)(2,1)S(1)}, bf16[32,2048]{1,0:T(8,128)(2,1)S(1)}, u32[]{:S(2)}, u32[]{:S(2)}) collective-permute-start(bf16[32,2048]{1,0:T(8,128)(2,1)S(1)} %act.1.mine_ref), channel_id=1, source_target_pairs={{0,1},{1,0},{2,3},{3,2},{4,5},{5,4},{6,7},{7,6},{8,9},{9,8},{10,11... | collective-permute-start | bytes 393224 | tf_op jit(solution)/shard_map/ppermute | solution.py:454
  26.1 10.4 %copy-start.3 = (f32[1024]{0:T(1024)S(1)}, f32[1024]{0:T(1024)}, u32[]{:S(2)}) copy-start(f32[1024]{0:T(1024)} %param.10) | copy-start | bytes 12292
  26.1 10.7 %copy-start = (bf16[1024,256]{1,0:T(8,128)(2,1)S(1)}, bf16[1024,256]{1,0:T(8,128)(2,1)}, u32[]{:S(2)}) copy-start(bf16[1024,256]{1,0:T(8,128)(2,1)} %coeff_hbm.1) | copy-start | bytes 1572868
  26.1 10.7 %copy-start.1 = (s32[16]{0:T(128)S(1)}, s32[16]{0:T(128)}, u32[]{:S(2)}) copy-start(s32[16]{0:T(128)} %pad_hbm.1) | copy-start | bytes 196
  26.2 10.7 %copy-start.2 = (f32[256]{0:T(256)S(1)}, f32[256]{0:T(256)}, u32[]{:S(2)}) copy-start(f32[256]{0:T(256)} %param.11) | copy-start | bytes 3076
  26.2 5.1 %collective-permute-start.10 = (bf16[64,256]{1,0:T(8,128)(2,1)S(1)}, bf16[64,256]{1,0:T(8,128)(2,1)S(1)}, u32[]{:S(2)}, u32[]{:S(2)}) collective-permute-start(bf16[64,256]{1,0:T(8,128)(2,1)S(1)} %get-tuple-element.44), channel_id=1, source_target_pairs={{0,4},{1,5},{2,6},{3,7},{4,0},{5,1},{6,2},{7,3},{8,12},{9,13},{10,... | collective-permute-start | bytes 98312 | tf_op jit(solution)/shard_map/ppermute | solution.py:454
  27.3 5.7 %collective-permute-start.11 = (bf16[64,256]{1,0:T(8,128)(2,1)S(1)}, bf16[64,256]{1,0:T(8,128)(2,1)S(1)}, u32[]{:S(2)}, u32[]{:S(2)}) collective-permute-start(bf16[64,256]{1,0:T(8,128)(2,1)S(1)} %get-tuple-element.45), channel_id=1, source_target_pairs={{0,6},{1,7},{2,4},{3,5},{4,2},{5,3},{6,0},{7,1},{8,14},{9,15},{10,... | collective-permute-start | bytes 98312 | tf_op jit(solution)/shard_map/ppermute | solution.py:454
  28.4 4.6 %collective-permute-start.12 = (bf16[64,256]{1,0:T(8,128)(2,1)S(1)}, bf16[64,256]{1,0:T(8,128)(2,1)S(1)}, u32[]{:S(2)}, u32[]{:S(2)}) collective-permute-start(bf16[64,256]{1,0:T(8,128)(2,1)S(1)} %get-tuple-element.46), channel_id=1, source_target_pairs={{0,2},{1,3},{2,0},{3,1},{4,6},{5,7},{6,4},{7,5},{8,10},{9,11},{10,... | collective-permute-start | bytes 98312 | tf_op jit(solution)/shard_map/ppermute | solution.py:454
  33.0 6.7 %collective-permute-start.13 = (bf16[256,256]{1,0:T(8,128)(2,1)S(1)}, bf16[256,256]{1,0:T(8,128)(2,1)}, u32[]{:S(2)}, u32[]{:S(2)}) collective-permute-start(bf16[256,256]{1,0:T(8,128)(2,1)S(1)} %assemble.1.grid_ref), channel_id=1, source_target_pairs={{0,24},{8,16},{16,8},{24,0},{1,25},{9,17},{17,9},{25,1},{2,26},{10... | collective-permute-start | bytes 393224 | tf_op jit(solution)/shard_map/ppermute | solution.py:454
  34.1 6.8 %collective-permute-start.14 = (bf16[256,256]{1,0:T(8,128)(2,1)S(1)}, bf16[256,256]{1,0:T(8,128)(2,1)S(1)}, u32[]{:S(2)}, u32[]{:S(2)}) collective-permute-start(bf16[256,256]{1,0:T(8,128)(2,1)S(1)} %assemble.1.grid_ref), channel_id=1, source_target_pairs={{0,8},{8,0},{16,24},{24,16},{1,9},{9,1},{17,25},{25,17},{2,10},{10... | collective-permute-start | bytes 393224 | tf_op jit(solution)/shard_map/ppermute | solution.py:454
  35.1 6.2 %collective-permute-start.15 = (bf16[256,256]{1,0:T(8,128)(2,1)S(1)}, bf16[256,256]{1,0:T(8,128)(2,1)S(1)}, u32[]{:S(2)}, u32[]{:S(2)}) collective-permute-start(bf16[256,256]{1,0:T(8,128)(2,1)S(1)} %assemble.1.grid_ref), channel_id=1, source_target_pairs={{0,16},{8,24},{16,0},{24,8},{1,17},{9,25},{17,1},{25,9},{2,18},{10... | collective-permute-start | bytes 393224 | tf_op jit(solution)/shard_map/ppermute | solution.py:454

commit v7 on v6

--- a/solution.py
+++ b/solution.py
@@ -420,6 +420,28 @@
     )(total, rolled, grid)
 
 
+def pair_kernel(wide, k, other, total_ref, rolled_ref, grid_hbm, other_ref, out_ref, grid_ref, sem):
+    start_pieces(grid_hbm, grid_ref, 32, sem)
+    own = rolled_ref.shape[1] // wide
+    me = lax.axis_index("wide")
+    start = pl.multiple_of((me ^ other) * own, own)
+    out_ref[...] = total_ref[...] + dot(rolled_ref[:, pl.ds(start, own)], other_ref[...])
+    wait_all(grid_hbm, grid_ref, sem)
+    start = pl.multiple_of((me ^ k) * own, own)
+    out_ref[...] += dot(rolled_ref[:, pl.ds(start, own)], grid_ref[...])
+
+
+def backward_pair(wide, k, other, total, rolled, grid, other_grid):
+    return call(
+        functools.partial(pair_kernel, wide, k, other),
+        "backward_pair",
+        array(total.shape, F32),
+        [VMEM, VMEM, HBM, VMEM],
+        VMEM,
+        [pltpu.VMEM(grid.shape, grid.dtype), pltpu.SemaphoreType.DMA],
+    )(total, rolled, in_hbm(grid), other_grid)
+
+
 def end_kernel(wide, k, total_ref, rolled_ref, grid_ref, out_hbm, out_ref, sems):
     own = rolled_ref.shape[1] // wide
     start = pl.multiple_of((lax.axis_index("wide") ^ k) * own, own)
@@ -508,7 +530,9 @@
     grids = {k: exchange(grid, k, wide, "wide") for k in steps}
     total = diagonal(block_pad, coeff, groupb_row_energy, groupa_energy)
     total = backward_more(wide, 0, total, rolled, grid)
-    for k in steps[:-1]:
+    k, other = steps[:2]
+    total = backward_pair(wide, k, other, total, rolled, grids[k], grids[other])
+    for k in steps[2:-1]:
         total = backward_more(wide, k, total, rolled, grids[k])
     return backward_end(wide, steps[-1], total, rolled, grids[steps[-1]])
 

time: 42.6 us -> 42.9 us (level)
    pallas_call x3 -> x1, Pallas kernels: 1.79 us -> 0.3 us  [backward_more(): call(functools.partial(more_kernel, wide, k), 'backward_more', array(tota...]
    pallas_call x0 -> x1, Pallas kernels: none -> 1.49 us  [backward_pair(): call(functools.partial(pair_kernel, wide, k, other), 'backward_pair', arr...]
  transfers between devices with their start and end apart: 16 -> 16, of which waited for: 7 -> 8; matrix products, arithmetic and copies ran while one was open for 1% -> 1% of each run, Pallas kernels for 15% -> 15%
where the time goes in v7:
time: 42.9 us; the launch traced here: 42.7 us
  starting transfers between devices  19.8 us (46%)
  Pallas kernels  11.3 us (26%)
  waiting for transfers between devices  11.1 us (26%)
    ppermute x16, starting transfers between devices, exchange(): return lax.ppermute(value, axis, [(i, i ^ step) for i in range(size)])  19.8 us
    ppermute x16, waiting for transfers between devices, exchange(): return lax.ppermute(value, axis, [(i, i ^ step) for i in range(size)])  11.1 us
    pallas_call x1, Pallas kernels, first(): call(functools.partial(first_kernel, wide, chips), 'forward_first', (arra...  2.33 us
    pallas_call x1, Pallas kernels, last(): call(functools.partial(last_kernel, wide), 'forward_own', (array((own, co...  1.66 us
    pallas_call x1, Pallas kernels, backward_pair(): call(functools.partial(pair_kernel, wide, k, other), 'backward_pair', arr...  1.49 us
    pallas_call x1, Pallas kernels, backward_end(): call(functools.partial(end_kernel, wide, k), 'backward_end', array(total....  1.24 us
    pallas_call x1, Pallas kernels, first_functions(): call(functools.partial(first_functions_kernel, leave), 'functions_first',...  1.07 us
  transfers between devices with their start and end apart: 16, of which 8 were waited for; matrix products, arithmetic and copies ran while one was open for 1% of the time, Pallas kernels for 15%

profile of v7, /device:TPU:0, one launch (start us, length us, event | category | flops | bytes accessed | tf_op | source)
XLA Modules:
  0.0 42.7 jit_solution(390462639464305966)
XLA Ops:
  0.0 2.3 %forward_first.1 = (bf16[256,256]{1,0:T(8,128)(2,1)S(1)}, bf16[256,1024]{1,0:T(8,128)(2,1)S(1)}, bf16[1024,1024]{1,0:T(8,128)(2,1)S(1)}, bf16[2,256,2048]{2,1,0:T(8,128)(2,1)S(1)}, f32[32,2048]{1,0:T(8,128)S(1)}) custom-call(s32[16]{0:T(128)} %level_hbm.1, s32[16]{0:T(128)} %pad_hbm.1, s32[16]{0:T(128)} %shift_hbm.1, bf16[1024,256]{1,0:T(8,128)(2,1)} %coeff_hbm.1, ...), custom_call_target="tpu_custom_call" | custom-call | flops 134217728 | bytes 4194304 | tf_op jit(solution)/shard_map/forward_first/pallas_call | solution.py:149
  2.3 4.0 %collective-permute-start = (bf16[256,256]{1,0:T(8,128)(2,1)S(1)}, bf16[256,256]{1,0:T(8,128)(2,1)S(1)}, u32[]{:S(2)}, u32[]{:S(2)}) collective-permute-start(bf16[256,256]{1,0:T(8,128)(2,1)S(1)} %get-tuple-element.29), channel_id=1, source_target_pairs={{0,24},{8,16},{16,8},{24,0},{1,25},{9,17},{17,9},{25,1},{2,26},{10... | collective-permute-start | bytes 393224 | tf_op jit(solution)/shard_map/ppermute | solution.py:476
  6.7 0.6 %collective-permute-start.4 = (bf16[128,256]{1,0:T(8,128)(2,1)S(1)}, bf16[128,256]{1,0:T(8,128)(2,1)S(1)}, u32[]{:S(2)}, u32[]{:S(2)}) collective-permute-start(bf16[128,256]{1,0:T(8,128)(2,1)S(1)} %get-tuple-element.35), channel_id=1, source_target_pairs={{0,16},{8,24},{16,0},{24,8},{1,17},{9,25},{17,1},{25,9},{2,18},{10... | collective-permute-start | bytes 196616 | tf_op jit(solution)/shard_map/ppermute | solution.py:476
  7.8 2.0 %collective-permute-start.2 = (bf16[128,256]{1,0:T(8,128)(2,1)S(1)}, bf16[128,256]{1,0:T(8,128)(2,1)S(1)}, u32[]{:S(2)}, u32[]{:S(2)}) collective-permute-start(bf16[128,256]{1,0:T(8,128)(2,1)S(1)} %get-tuple-element.31), channel_id=1, source_target_pairs={{0,16},{8,24},{16,0},{24,8},{1,17},{9,25},{17,1},{25,9},{2,18},{10... | collective-permute-start | bytes 196616 | tf_op jit(solution)/shard_map/ppermute | solution.py:476
  9.7 1.5 %collective-permute-start.1 = (bf16[128,256]{1,0:T(8,128)(2,1)S(1)}, bf16[128,256]{1,0:T(8,128)(2,1)S(1)}, u32[]{:S(2)}, u32[]{:S(2)}) collective-permute-start(bf16[128,256]{1,0:T(8,128)(2,1)S(1)} %get-tuple-element.30), channel_id=1, source_target_pairs={{0,8},{8,0},{16,24},{24,16},{1,9},{9,1},{17,25},{25,17},{2,10},{10... | collective-permute-start | bytes 196616 | tf_op jit(solution)/shard_map/ppermute | solution.py:476
  11.2 1.7 %forward_own.1 = (f32[256,256]{1,0:T(8,128)S(1)}, bf16[2,256,2048]{2,1,0:T(8,128)(2,1)S(1)}) custom-call(bf16[256,1024]{1,0:T(8,128)(2,1)S(1)} %get-tuple-element.27.turned_ref, bf16[1024,1024]{1,0:T(8,128)(2,1)S(1)} %get-tuple-element.26.rolled_ref, bf16[2048,2048]{1,0:T(8,128)(2,1)} %basis_hbm.3), custom_call_target="tpu_custom_call" | custom-call | tf_op jit(solution)/shard_map/forward_own/pallas_call | solution.py:206
  13.0 2.7 %collective-permute-start.5 = (bf16[64,256]{1,0:T(8,128)(2,1)S(1)}, bf16[64,256]{1,0:T(8,128)(2,1)S(1)}, u32[]{:S(2)}, u32[]{:S(2)}) collective-permute-start(bf16[64,256]{1,0:T(8,128)(2,1)S(1)} %get-tuple-element.36), channel_id=1, source_target_pairs={{0,4},{1,5},{2,6},{3,7},{4,0},{5,1},{6,2},{7,3},{8,12},{9,13},{10,... | collective-permute-start | bytes 98312 | tf_op jit(solution)/shard_map/ppermute | solution.py:476
  15.6 1.4 %collective-permute-start.6 = (bf16[64,256]{1,0:T(8,128)(2,1)S(1)}, bf16[64,256]{1,0:T(8,128)(2,1)S(1)}, u32[]{:S(2)}, u32[]{:S(2)}) collective-permute-start(bf16[64,256]{1,0:T(8,128)(2,1)S(1)} %get-tuple-element.38), channel_id=1, source_target_pairs={{0,6},{1,7},{2,4},{3,5},{4,2},{5,3},{6,0},{7,1},{8,14},{9,15},{10,... | collective-permute-start | bytes 98312 | tf_op jit(solution)/shard_map/ppermute | solution.py:476
  18.5 2.9 %collective-permute-done.6.x_ref = bf16[64,256]{1,0:T(8,128)(2,1)S(1)} collective-permute-done((bf16[64,256]{1,0:T(8,128)(2,1)S(1)}, bf16[64,256]{1,0:T(8,128)(2,1)S(1)}, u32[]{:S(2)}, u32[]{:S(2)}) %collective-permute-start.6) | collective-permute-done | bytes 32800 | tf_op jit(solution)/shard_map/ppermute | solution.py:476
  22.1 1.5 %collective-permute-done.8.other_ref = f32[32,2048]{1,0:T(8,128)S(1)} collective-permute-done((f32[32,2048]{1,0:T(8,128)S(1)}, f32[32,2048]{1,0:T(8,128)S(1)}, u32[]{:S(2)}, u32[]{:S(2)}) %collective-permute-start.8) | collective-permute-done | bytes 262176 | tf_op jit(solution)/shard_map/ppermute | solution.py:476
  23.8 1.2 %collective-permute-done.9.other_ref = bf16[32,2048]{1,0:T(8,128)(2,1)S(1)} collective-permute-done((bf16[32,2048]{1,0:T(8,128)(2,1)S(1)}, bf16[32,2048]{1,0:T(8,128)(2,1)S(1)}, u32[]{:S(2)}, u32[]{:S(2)}) %collective-permute-start.9) | collective-permute-done | bytes 131104 | tf_op jit(solution)/shard_map/ppermute | solution.py:476
  25.0 1.1 %functions_first.1 = (bf16[64,256]{1,0:T(8,128)(2,1)S(1)}, bf16[64,256]{1,0:T(8,128)(2,1)S(1)}, bf16[64,256]{1,0:T(8,128)(2,1)S(1)}, bf16[64,2048]{1,0:T(8,128)(2,1)S(1)}) custom-call(bf16[32,2048]{1,0:T(8,128)(2,1)S(1)} %act.1.mine_ref, bf16[32,2048]{1,0:T(8,128)(2,1)S(1)} %collective-permute-done.9.other_ref, ...), custom_call_target="tpu_custom_call" | custom-call | tf_op jit(solution)/shard_map/functions_first/pallas_call | solution.py:332
  26.2 1.1 %collective-permute-start.10 = (bf16[64,256]{1,0:T(8,128)(2,1)S(1)}, bf16[64,256]{1,0:T(8,128)(2,1)S(1)}, u32[]{:S(2)}, u32[]{:S(2)}) collective-permute-start(bf16[64,256]{1,0:T(8,128)(2,1)S(1)} %get-tuple-element.44), channel_id=1, source_target_pairs={{0,4},{1,5},{2,6},{3,7},{4,0},{5,1},{6,2},{7,3},{8,12},{9,13},{10,... | collective-permute-start | bytes 98312 | tf_op jit(solution)/shard_map/ppermute | solution.py:476
  27.3 1.1 %collective-permute-start.11 = (bf16[64,256]{1,0:T(8,128)(2,1)S(1)}, bf16[64,256]{1,0:T(8,128)(2,1)S(1)}, u32[]{:S(2)}, u32[]{:S(2)}) collective-permute-start(bf16[64,256]{1,0:T(8,128)(2,1)S(1)} %get-tuple-element.45), channel_id=1, source_target_pairs={{0,6},{1,7},{2,4},{3,5},{4,2},{5,3},{6,0},{7,1},{8,14},{9,15},{10,... | collective-permute-start | bytes 98312 | tf_op jit(solution)/shard_map/ppermute | solution.py:476
  28.4 1.4 %collective-permute-start.12 = (bf16[64,256]{1,0:T(8,128)(2,1)S(1)}, bf16[64,256]{1,0:T(8,128)(2,1)S(1)}, u32[]{:S(2)}, u32[]{:S(2)}) collective-permute-start(bf16[64,256]{1,0:T(8,128)(2,1)S(1)} %get-tuple-element.46), channel_id=1, source_target_pairs={{0,2},{1,3},{2,0},{3,1},{4,6},{5,7},{6,4},{7,5},{8,10},{9,11},{10,... | collective-permute-start | bytes 98312 | tf_op jit(solution)/shard_map/ppermute | solution.py:476
  30.2 1.1 %collective-permute-done.10.refs_1_ = bf16[64,256]{1,0:T(8,128)(2,1)S(1)} collective-permute-done((bf16[64,256]{1,0:T(8,128)(2,1)S(1)}, bf16[64,256]{1,0:T(8,128)(2,1)S(1)}, u32[]{:S(2)}, u32[]{:S(2)}) %collective-permute-start.10) | collective-permute-done | bytes 32800 | tf_op jit(solution)/shard_map/ppermute | solution.py:476
  31.3 1.7 %collective-permute-done.11.refs_2_ = bf16[64,256]{1,0:T(8,128)(2,1)S(1)} collective-permute-done((bf16[64,256]{1,0:T(8,128)(2,1)S(1)}, bf16[64,256]{1,0:T(8,128)(2,1)S(1)}, u32[]{:S(2)}, u32[]{:S(2)}) %collective-permute-start.11) | collective-permute-done | bytes 32800 | tf_op jit(solution)/shard_map/ppermute | solution.py:476
  33.0 1.1 %collective-permute-start.13 = (bf16[256,256]{1,0:T(8,128)(2,1)S(1)}, bf16[256,256]{1,0:T(8,128)(2,1)}, u32[]{:S(2)}, u32[]{:S(2)}) collective-permute-start(bf16[256,256]{1,0:T(8,128)(2,1)S(1)} %assemble.1.grid_ref), channel_id=1, source_target_pairs={{0,24},{8,16},{16,8},{24,0},{1,25},{9,17},{17,9},{25,1},{2,26},{10... | collective-permute-start | bytes 393224 | tf_op jit(solution)/shard_map/ppermute | solution.py:476
  34.1 1.0 %collective-permute-start.14 = (bf16[256,256]{1,0:T(8,128)(2,1)S(1)}, bf16[256,256]{1,0:T(8,128)(2,1)S(1)}, u32[]{:S(2)}, u32[]{:S(2)}) collective-permute-start(bf16[256,256]{1,0:T(8,128)(2,1)S(1)} %assemble.1.grid_ref), channel_id=1, source_target_pairs={{0,8},{8,0},{16,24},{24,16},{1,9},{9,1},{17,25},{25,17},{2,10},{10... | collective-permute-start | bytes 393224 | tf_op jit(solution)/shard_map/ppermute | solution.py:476
  35.1 1.5 %collective-permute-start.15 = (bf16[256,256]{1,0:T(8,128)(2,1)S(1)}, bf16[256,256]{1,0:T(8,128)(2,1)S(1)}, u32[]{:S(2)}, u32[]{:S(2)}) collective-permute-start(bf16[256,256]{1,0:T(8,128)(2,1)S(1)} %assemble.1.grid_ref), channel_id=1, source_target_pairs={{0,16},{8,24},{16,0},{24,8},{1,17},{9,25},{17,1},{25,9},{2,18},{10... | collective-permute-start | bytes 393224 | tf_op jit(solution)/shard_map/ppermute | solution.py:476
  36.8 0.8 %diagonal.1.total_ref = f32[1024,256]{1,0:T(8,128)S(1)} custom-call(s32[16]{0:T(128)S(1)} %copy-done.1, bf16[1024,256]{1,0:T(8,128)(2,1)S(1)} %copy-done, f32[1024,1]{1,0:T(8,128)S(1)} %copy.10.row_ref, f32[1,256]{1,0:T(1,128)S(1)} %bitcast.3), custom_call_target="tpu_custom_call" | custom-call | tf_op jit(solution)/shard_map/diagonal/pallas_call | solution.py:395
  37.9 1.8 %collective-permute-done.13.grid_hbm = bf16[256,256]{1,0:T(8,128)(2,1)} collective-permute-done((bf16[256,256]{1,0:T(8,128)(2,1)S(1)}, bf16[256,256]{1,0:T(8,128)(2,1)}, u32[]{:S(2)}, u32[]{:S(2)}) %collective-permute-start.13) | collective-permute-done | bytes 131104 | tf_op jit(solution)/shard_map/ppermute | solution.py:476
  40.0 1.5 %backward_pair.1.total_ref = f32[1024,256]{1,0:T(8,128)S(1)} custom-call(f32[1024,256]{1,0:T(8,128)S(1)} %backward_more.1.total_ref, bf16[1024,1024]{1,0:T(8,128)(2,1)S(1)} %get-tuple-element.26.rolled_ref, bf16[256,256]{1,0:T(8,128)(2,1)} %collective-permute-done.13.grid_hbm, bf16[256,256]{1,0:T(8,128)(2,1)S(1)} %collective-permute-done.14.other_ref), custom_call_target="tpu_custom_call" | custom-call | tf_op jit(solution)/shard_map/backward_pair/pallas_call | solution.py:435
  41.5 1.2 %backward_end.1 = f32[1024,256]{1,0:T(8,128)} custom-call(f32[1024,256]{1,0:T(8,128)S(1)} %backward_pair.1.total_ref, bf16[1024,1024]{1,0:T(8,128)(2,1)S(1)} %get-tuple-element.26.rolled_ref, bf16[256,256]{1,0:T(8,128)(2,1)S(1)} %collective-permute-done.15.grid_ref), custom_call_target="tpu_custom_call" | custom-call | flops 134217728 | bytes 4194304 | tf_op jit(solution)/shard_map/backward_end/pallas_call | solution.py:463
  (35 shorter events, 4.6 us)
Async XLA Ops:
  2.3 10.6 %collective-permute-start = (bf16[256,256]{1,0:T(8,128)(2,1)S(1)}, bf16[256,256]{1,0:T(8,128)(2,1)S(1)}, u32[]{:S(2)}, u32[]{:S(2)}) collective-permute-start(bf16[256,256]{1,0:T(8,128)(2,1)S(1)} %get-tuple-element.29), channel_id=1, source_target_pairs={{0,24},{8,16},{16,8},{24,0},{1,25},{9,17},{17,9},{25,1},{2,26},{10... | collective-permute-start | bytes 393224 | tf_op jit(solution)/shard_map/ppermute | solution.py:476
  6.7 6.2 %collective-permute-start.4 = (bf16[128,256]{1,0:T(8,128)(2,1)S(1)}, bf16[128,256]{1,0:T(8,128)(2,1)S(1)}, u32[]{:S(2)}, u32[]{:S(2)}) collective-permute-start(bf16[128,256]{1,0:T(8,128)(2,1)S(1)} %get-tuple-element.35), channel_id=1, source_target_pairs={{0,16},{8,24},{16,0},{24,8},{1,17},{9,25},{17,1},{25,9},{2,18},{10... | collective-permute-start | bytes 196616 | tf_op jit(solution)/shard_map/ppermute | solution.py:476
  7.6 5.3 %collective-permute-start.3 = (bf16[128,256]{1,0:T(8,128)(2,1)S(1)}, bf16[128,256]{1,0:T(8,128)(2,1)S(1)}, u32[]{:S(2)}, u32[]{:S(2)}) collective-permute-start(bf16[128,256]{1,0:T(8,128)(2,1)S(1)} %get-tuple-element.34), channel_id=1, source_target_pairs={{0,8},{8,0},{16,24},{24,16},{1,9},{9,1},{17,25},{25,17},{2,10},{10... | collective-permute-start | bytes 196616 | tf_op jit(solution)/shard_map/ppermute | solution.py:476
  7.8 9.2 %collective-permute-start.2 = (bf16[128,256]{1,0:T(8,128)(2,1)S(1)}, bf16[128,256]{1,0:T(8,128)(2,1)S(1)}, u32[]{:S(2)}, u32[]{:S(2)}) collective-permute-start(bf16[128,256]{1,0:T(8,128)(2,1)S(1)} %get-tuple-element.31), channel_id=1, source_target_pairs={{0,16},{8,24},{16,0},{24,8},{1,17},{9,25},{17,1},{25,9},{2,18},{10... | collective-permute-start | bytes 196616 | tf_op jit(solution)/shard_map/ppermute | solution.py:476
  9.7 7.3 %collective-permute-start.1 = (bf16[128,256]{1,0:T(8,128)(2,1)S(1)}, bf16[128,256]{1,0:T(8,128)(2,1)S(1)}, u32[]{:S(2)}, u32[]{:S(2)}) collective-permute-start(bf16[128,256]{1,0:T(8,128)(2,1)S(1)} %get-tuple-element.30), channel_id=1, source_target_pairs={{0,8},{8,0},{16,24},{24,16},{1,9},{9,1},{17,25},{25,17},{2,10},{10... | collective-permute-start | bytes 196616 | tf_op jit(solution)/shard_map/ppermute | solution.py:476
  13.0 5.2 %collective-permute-start.5 = (bf16[64,256]{1,0:T(8,128)(2,1)S(1)}, bf16[64,256]{1,0:T(8,128)(2,1)S(1)}, u32[]{:S(2)}, u32[]{:S(2)}) collective-permute-start(bf16[64,256]{1,0:T(8,128)(2,1)S(1)} %get-tuple-element.36), channel_id=1, source_target_pairs={{0,4},{1,5},{2,6},{3,7},{4,0},{5,1},{6,2},{7,3},{8,12},{9,13},{10,... | collective-permute-start | bytes 98312 | tf_op jit(solution)/shard_map/ppermute | solution.py:476
  15.6 5.7 %collective-permute-start.6 = (bf16[64,256]{1,0:T(8,128)(2,1)S(1)}, bf16[64,256]{1,0:T(8,128)(2,1)S(1)}, u32[]{:S(2)}, u32[]{:S(2)}) collective-permute-start(bf16[64,256]{1,0:T(8,128)(2,1)S(1)} %get-tuple-element.38), channel_id=1, source_target_pairs={{0,6},{1,7},{2,4},{3,5},{4,2},{5,3},{6,0},{7,1},{8,14},{9,15},{10,... | collective-permute-start | bytes 98312 | tf_op jit(solution)/shard_map/ppermute | solution.py:476
  17.0 4.6 %collective-permute-start.7 = (bf16[64,256]{1,0:T(8,128)(2,1)S(1)}, bf16[64,256]{1,0:T(8,128)(2,1)S(1)}, u32[]{:S(2)}, u32[]{:S(2)}) collective-permute-start(bf16[64,256]{1,0:T(8,128)(2,1)S(1)} %get-tuple-element.39), channel_id=1, source_target_pairs={{0,2},{1,3},{2,0},{3,1},{4,6},{5,7},{6,4},{7,5},{8,10},{9,11},{10,... | collective-permute-start | bytes 98312 | tf_op jit(solution)/shard_map/ppermute | solution.py:476
  22.0 1.6 %collective-permute-start.8 = (f32[32,2048]{1,0:T(8,128)S(1)}, f32[32,2048]{1,0:T(8,128)S(1)}, u32[]{:S(2)}, u32[]{:S(2)}) collective-permute-start(f32[32,2048]{1,0:T(8,128)S(1)} %get-tuple-element.41), channel_id=1, source_target_pairs={{0,1},{1,0},{2,3},{3,2},{4,5},{5,4},{6,7},{7,6},{8,9},{9,8},{10,11... | collective-permute-start | bytes 786440 | tf_op jit(solution)/shard_map/ppermute | solution.py:476
  23.6 1.4 %collective-permute-start.9 = (bf16[32,2048]{1,0:T(8,128)(2,1)S(1)}, bf16[32,2048]{1,0:T(8,128)(2,1)S(1)}, u32[]{:S(2)}, u32[]{:S(2)}) collective-permute-start(bf16[32,2048]{1,0:T(8,128)(2,1)S(1)} %act.1.mine_ref), channel_id=1, source_target_pairs={{0,1},{1,0},{2,3},{3,2},{4,5},{5,4},{6,7},{7,6},{8,9},{9,8},{10,11... | collective-permute-start | bytes 393224 | tf_op jit(solution)/shard_map/ppermute | solution.py:476
  26.1 10.4 %copy-start.3 = (f32[1024]{0:T(1024)S(1)}, f32[1024]{0:T(1024)}, u32[]{:S(2)}) copy-start(f32[1024]{0:T(1024)} %param.10) | copy-start | bytes 12292
  26.1 10.7 %copy-start = (bf16[1024,256]{1,0:T(8,128)(2,1)S(1)}, bf16[1024,256]{1,0:T(8,128)(2,1)}, u32[]{:S(2)}) copy-start(bf16[1024,256]{1,0:T(8,128)(2,1)} %coeff_hbm.1) | copy-start | bytes 1572868
  26.1 10.7 %copy-start.1 = (s32[16]{0:T(128)S(1)}, s32[16]{0:T(128)}, u32[]{:S(2)}) copy-start(s32[16]{0:T(128)} %pad_hbm.1) | copy-start | bytes 196
  26.2 10.7 %copy-start.2 = (f32[256]{0:T(256)S(1)}, f32[256]{0:T(256)}, u32[]{:S(2)}) copy-start(f32[256]{0:T(256)} %param.11) | copy-start | bytes 3076
  26.2 5.1 %collective-permute-start.10 = (bf16[64,256]{1,0:T(8,128)(2,1)S(1)}, bf16[64,256]{1,0:T(8,128)(2,1)S(1)}, u32[]{:S(2)}, u32[]{:S(2)}) collective-permute-start(bf16[64,256]{1,0:T(8,128)(2,1)S(1)} %get-tuple-element.44), channel_id=1, source_target_pairs={{0,4},{1,5},{2,6},{3,7},{4,0},{5,1},{6,2},{7,3},{8,12},{9,13},{10,... | collective-permute-start | bytes 98312 | tf_op jit(solution)/shard_map/ppermute | solution.py:476
  27.3 5.7 %collective-permute-start.11 = (bf16[64,256]{1,0:T(8,128)(2,1)S(1)}, bf16[64,256]{1,0:T(8,128)(2,1)S(1)}, u32[]{:S(2)}, u32[]{:S(2)}) collective-permute-start(bf16[64,256]{1,0:T(8,128)(2,1)S(1)} %get-tuple-element.45), channel_id=1, source_target_pairs={{0,6},{1,7},{2,4},{3,5},{4,2},{5,3},{6,0},{7,1},{8,14},{9,15},{10,... | collective-permute-start | bytes 98312 | tf_op jit(solution)/shard_map/ppermute | solution.py:476
  28.4 4.6 %collective-permute-start.12 = (bf16[64,256]{1,0:T(8,128)(2,1)S(1)}, bf16[64,256]{1,0:T(8,128)(2,1)S(1)}, u32[]{:S(2)}, u32[]{:S(2)}) collective-permute-start(bf16[64,256]{1,0:T(8,128)(2,1)S(1)} %get-tuple-element.46), channel_id=1, source_target_pairs={{0,2},{1,3},{2,0},{3,1},{4,6},{5,7},{6,4},{7,5},{8,10},{9,11},{10,... | collective-permute-start | bytes 98312 | tf_op jit(solution)/shard_map/ppermute | solution.py:476
  33.0 6.7 %collective-permute-start.13 = (bf16[256,256]{1,0:T(8,128)(2,1)S(1)}, bf16[256,256]{1,0:T(8,128)(2,1)}, u32[]{:S(2)}, u32[]{:S(2)}) collective-permute-start(bf16[256,256]{1,0:T(8,128)(2,1)S(1)} %assemble.1.grid_ref), channel_id=1, source_target_pairs={{0,24},{8,16},{16,8},{24,0},{1,25},{9,17},{17,9},{25,1},{2,26},{10... | collective-permute-start | bytes 393224 | tf_op jit(solution)/shard_map/ppermute | solution.py:476
  34.1 5.9 %collective-permute-start.14 = (bf16[256,256]{1,0:T(8,128)(2,1)S(1)}, bf16[256,256]{1,0:T(8,128)(2,1)S(1)}, u32[]{:S(2)}, u32[]{:S(2)}) collective-permute-start(bf16[256,256]{1,0:T(8,128)(2,1)S(1)} %assemble.1.grid_ref), channel_id=1, source_target_pairs={{0,8},{8,0},{16,24},{24,16},{1,9},{9,1},{17,25},{25,17},{2,10},{10... | collective-permute-start | bytes 393224 | tf_op jit(solution)/shard_map/ppermute | solution.py:476
  35.1 6.4 %collective-permute-start.15 = (bf16[256,256]{1,0:T(8,128)(2,1)S(1)}, bf16[256,256]{1,0:T(8,128)(2,1)S(1)}, u32[]{:S(2)}, u32[]{:S(2)}) collective-permute-start(bf16[256,256]{1,0:T(8,128)(2,1)S(1)} %assemble.1.grid_ref), channel_id=1, source_target_pairs={{0,16},{8,24},{16,0},{24,8},{1,17},{9,25},{17,1},{25,9},{2,18},{10... | collective-permute-start | bytes 393224 | tf_op jit(solution)/shard_map/ppermute | solution.py:476

commit v8 on v6

--- a/solution.py
+++ b/solution.py
@@ -425,15 +425,14 @@
     start = pl.multiple_of((lax.axis_index("wide") ^ k) * own, own)
     steps = sems.shape[0]
     rows = rolled_ref.shape[0] // steps
-    copies = []
     for i in range(steps):
         span = pl.ds(i * rows, rows)
         part = dot(rolled_ref[span, pl.ds(start, own)], grid_ref[...])
         out_ref[span, :] = total_ref[span, :] + part
-        copies.append(pltpu.make_async_copy(out_ref.at[span, :], out_hbm.at[span, :], sems.at[i]))
-        copies[-1].start()
-    for copy in copies:
-        copy.wait()
+        start_pieces(out_ref.at[span], out_hbm.at[span], rows // 4, sems.at[i])
+    for i in range(steps):
+        span = pl.ds(i * rows, rows)
+        wait_all(out_ref.at[span], out_hbm.at[span], sems.at[i])
 
 
 def backward_end(wide, k, total, rolled, grid):
@@ -444,7 +443,7 @@
         array(total.shape, F32),
         [VMEM] * 3,
         HBM,
-        [pltpu.VMEM(total.shape, F32), pltpu.SemaphoreType.DMA((8,))],
+        [pltpu.VMEM(total.shape, F32), pltpu.SemaphoreType.DMA((4,))],
         flops=2 * rows * columns * rolled.shape[1] // wide,
         moved=4 * MIB,
     )(total, rolled, grid)

time: 42.6 us -> 42.6 us (level)
  no operation moved by 1% of the time
where the time goes in v8:
time: 42.6 us; the launch traced here: 42.5 us
  starting transfers between devices  19.8 us (46%)
  Pallas kernels  11.3 us (27%)
  waiting for transfers between devices  10.8 us (25%)
    ppermute x16, starting transfers between devices, exchange(): return lax.ppermute(value, axis, [(i, i ^ step) for i in range(size)])  19.8 us
    ppermute x16, waiting for transfers between devices, exchange(): return lax.ppermute(value, axis, [(i, i ^ step) for i in range(size)])  10.8 us
    pallas_call x1, Pallas kernels, first(): call(functools.partial(first_kernel, wide, chips), 'forward_first', (arra...  2.33 us
    pallas_call x3, Pallas kernels, backward_more(): call(functools.partial(more_kernel, wide, k), 'backward_more', array(tota...  1.79 us
    pallas_call x1, Pallas kernels, last(): call(functools.partial(last_kernel, wide), 'forward_own', (array((own, co...  1.66 us
    pallas_call x1, Pallas kernels, backward_end(): call(functools.partial(end_kernel, wide, k), 'backward_end', array(total....  1.22 us
    pallas_call x1, Pallas kernels, first_functions(): call(functools.partial(first_functions_kernel, leave), 'functions_first',...  1.07 us
  transfers between devices with their start and end apart: 16, of which 7 were waited for; matrix products, arithmetic and copies ran while one was open for 1% of the time, Pallas kernels for 15%

profile of v8, /device:TPU:0, one launch (start us, length us, event | category | flops | bytes accessed | tf_op | source)
XLA Modules:
  0.0 42.5 jit_solution(2500152070429869052)
XLA Ops:
  0.0 2.3 %forward_first.1 = (bf16[256,256]{1,0:T(8,128)(2,1)S(1)}, bf16[256,1024]{1,0:T(8,128)(2,1)S(1)}, bf16[1024,1024]{1,0:T(8,128)(2,1)S(1)}, bf16[2,256,2048]{2,1,0:T(8,128)(2,1)S(1)}, f32[32,2048]{1,0:T(8,128)S(1)}) custom-call(s32[16]{0:T(128)} %level_hbm.1, s32[16]{0:T(128)} %pad_hbm.1, s32[16]{0:T(128)} %shift_hbm.1, bf16[1024,256]{1,0:T(8,128)(2,1)} %coeff_hbm.1, ...), custom_call_target="tpu_custom_call" | custom-call | flops 134217728 | bytes 4194304 | tf_op jit(solution)/shard_map/forward_first/pallas_call | solution.py:149
  2.3 4.0 %collective-permute-start = (bf16[256,256]{1,0:T(8,128)(2,1)S(1)}, bf16[256,256]{1,0:T(8,128)(2,1)S(1)}, u32[]{:S(2)}, u32[]{:S(2)}) collective-permute-start(bf16[256,256]{1,0:T(8,128)(2,1)S(1)} %get-tuple-element.29), channel_id=1, source_target_pairs={{0,24},{8,16},{16,8},{24,0},{1,25},{9,17},{17,9},{25,1},{2,26},{10... | collective-permute-start | bytes 393224 | tf_op jit(solution)/shard_map/ppermute | solution.py:453
  6.7 0.6 %collective-permute-start.4 = (bf16[128,256]{1,0:T(8,128)(2,1)S(1)}, bf16[128,256]{1,0:T(8,128)(2,1)S(1)}, u32[]{:S(2)}, u32[]{:S(2)}) collective-permute-start(bf16[128,256]{1,0:T(8,128)(2,1)S(1)} %get-tuple-element.35), channel_id=1, source_target_pairs={{0,16},{8,24},{16,0},{24,8},{1,17},{9,25},{17,1},{25,9},{2,18},{10... | collective-permute-start | bytes 196616 | tf_op jit(solution)/shard_map/ppermute | solution.py:453
  7.8 2.0 %collective-permute-start.2 = (bf16[128,256]{1,0:T(8,128)(2,1)S(1)}, bf16[128,256]{1,0:T(8,128)(2,1)S(1)}, u32[]{:S(2)}, u32[]{:S(2)}) collective-permute-start(bf16[128,256]{1,0:T(8,128)(2,1)S(1)} %get-tuple-element.31), channel_id=1, source_target_pairs={{0,16},{8,24},{16,0},{24,8},{1,17},{9,25},{17,1},{25,9},{2,18},{10... | collective-permute-start | bytes 196616 | tf_op jit(solution)/shard_map/ppermute | solution.py:453
  9.7 1.5 %collective-permute-start.1 = (bf16[128,256]{1,0:T(8,128)(2,1)S(1)}, bf16[128,256]{1,0:T(8,128)(2,1)S(1)}, u32[]{:S(2)}, u32[]{:S(2)}) collective-permute-start(bf16[128,256]{1,0:T(8,128)(2,1)S(1)} %get-tuple-element.30), channel_id=1, source_target_pairs={{0,8},{8,0},{16,24},{24,16},{1,9},{9,1},{17,25},{25,17},{2,10},{10... | collective-permute-start | bytes 196616 | tf_op jit(solution)/shard_map/ppermute | solution.py:453
  11.2 1.7 %forward_own.1 = (f32[256,256]{1,0:T(8,128)S(1)}, bf16[2,256,2048]{2,1,0:T(8,128)(2,1)S(1)}) custom-call(bf16[256,1024]{1,0:T(8,128)(2,1)S(1)} %get-tuple-element.27.turned_ref, bf16[1024,1024]{1,0:T(8,128)(2,1)S(1)} %get-tuple-element.26.rolled_ref, bf16[2048,2048]{1,0:T(8,128)(2,1)} %basis_hbm.3), custom_call_target="tpu_custom_call" | custom-call | tf_op jit(solution)/shard_map/forward_own/pallas_call | solution.py:206
  13.0 2.7 %collective-permute-start.5 = (bf16[64,256]{1,0:T(8,128)(2,1)S(1)}, bf16[64,256]{1,0:T(8,128)(2,1)S(1)}, u32[]{:S(2)}, u32[]{:S(2)}) collective-permute-start(bf16[64,256]{1,0:T(8,128)(2,1)S(1)} %get-tuple-element.36), channel_id=1, source_target_pairs={{0,4},{1,5},{2,6},{3,7},{4,0},{5,1},{6,2},{7,3},{8,12},{9,13},{10,... | collective-permute-start | bytes 98312 | tf_op jit(solution)/shard_map/ppermute | solution.py:453
  15.6 1.4 %collective-permute-start.6 = (bf16[64,256]{1,0:T(8,128)(2,1)S(1)}, bf16[64,256]{1,0:T(8,128)(2,1)S(1)}, u32[]{:S(2)}, u32[]{:S(2)}) collective-permute-start(bf16[64,256]{1,0:T(8,128)(2,1)S(1)} %get-tuple-element.38), channel_id=1, source_target_pairs={{0,6},{1,7},{2,4},{3,5},{4,2},{5,3},{6,0},{7,1},{8,14},{9,15},{10,... | collective-permute-start | bytes 98312 | tf_op jit(solution)/shard_map/ppermute | solution.py:453
  18.5 2.9 %collective-permute-done.6.x_ref = bf16[64,256]{1,0:T(8,128)(2,1)S(1)} collective-permute-done((bf16[64,256]{1,0:T(8,128)(2,1)S(1)}, bf16[64,256]{1,0:T(8,128)(2,1)S(1)}, u32[]{:S(2)}, u32[]{:S(2)}) %collective-permute-start.6) | collective-permute-done | bytes 32800 | tf_op jit(solution)/shard_map/ppermute | solution.py:453
  22.1 1.5 %collective-permute-done.8.other_ref = f32[32,2048]{1,0:T(8,128)S(1)} collective-permute-done((f32[32,2048]{1,0:T(8,128)S(1)}, f32[32,2048]{1,0:T(8,128)S(1)}, u32[]{:S(2)}, u32[]{:S(2)}) %collective-permute-start.8) | collective-permute-done | bytes 262176 | tf_op jit(solution)/shard_map/ppermute | solution.py:453
  23.8 1.2 %collective-permute-done.9.other_ref = bf16[32,2048]{1,0:T(8,128)(2,1)S(1)} collective-permute-done((bf16[32,2048]{1,0:T(8,128)(2,1)S(1)}, bf16[32,2048]{1,0:T(8,128)(2,1)S(1)}, u32[]{:S(2)}, u32[]{:S(2)}) %collective-permute-start.9) | collective-permute-done | bytes 131104 | tf_op jit(solution)/shard_map/ppermute | solution.py:453
  25.0 1.1 %functions_first.1 = (bf16[64,256]{1,0:T(8,128)(2,1)S(1)}, bf16[64,256]{1,0:T(8,128)(2,1)S(1)}, bf16[64,256]{1,0:T(8,128)(2,1)S(1)}, bf16[64,2048]{1,0:T(8,128)(2,1)S(1)}) custom-call(bf16[32,2048]{1,0:T(8,128)(2,1)S(1)} %act.1.mine_ref, bf16[32,2048]{1,0:T(8,128)(2,1)S(1)} %collective-permute-done.9.other_ref, ...), custom_call_target="tpu_custom_call" | custom-call | tf_op jit(solution)/shard_map/functions_first/pallas_call | solution.py:332
  26.2 1.1 %collective-permute-start.10 = (bf16[64,256]{1,0:T(8,128)(2,1)S(1)}, bf16[64,256]{1,0:T(8,128)(2,1)S(1)}, u32[]{:S(2)}, u32[]{:S(2)}) collective-permute-start(bf16[64,256]{1,0:T(8,128)(2,1)S(1)} %get-tuple-element.44), channel_id=1, source_target_pairs={{0,4},{1,5},{2,6},{3,7},{4,0},{5,1},{6,2},{7,3},{8,12},{9,13},{10,... | collective-permute-start | bytes 98312 | tf_op jit(solution)/shard_map/ppermute | solution.py:453
  27.3 1.1 %collective-permute-start.11 = (bf16[64,256]{1,0:T(8,128)(2,1)S(1)}, bf16[64,256]{1,0:T(8,128)(2,1)S(1)}, u32[]{:S(2)}, u32[]{:S(2)}) collective-permute-start(bf16[64,256]{1,0:T(8,128)(2,1)S(1)} %get-tuple-element.45), channel_id=1, source_target_pairs={{0,6},{1,7},{2,4},{3,5},{4,2},{5,3},{6,0},{7,1},{8,14},{9,15},{10,... | collective-permute-start | bytes 98312 | tf_op jit(solution)/shard_map/ppermute | solution.py:453
  28.4 1.4 %collective-permute-start.12 = (bf16[64,256]{1,0:T(8,128)(2,1)S(1)}, bf16[64,256]{1,0:T(8,128)(2,1)S(1)}, u32[]{:S(2)}, u32[]{:S(2)}) collective-permute-start(bf16[64,256]{1,0:T(8,128)(2,1)S(1)} %get-tuple-element.46), channel_id=1, source_target_pairs={{0,2},{1,3},{2,0},{3,1},{4,6},{5,7},{6,4},{7,5},{8,10},{9,11},{10,... | collective-permute-start | bytes 98312 | tf_op jit(solution)/shard_map/ppermute | solution.py:453
  30.2 1.1 %collective-permute-done.10.refs_1_ = bf16[64,256]{1,0:T(8,128)(2,1)S(1)} collective-permute-done((bf16[64,256]{1,0:T(8,128)(2,1)S(1)}, bf16[64,256]{1,0:T(8,128)(2,1)S(1)}, u32[]{:S(2)}, u32[]{:S(2)}) %collective-permute-start.10) | collective-permute-done | bytes 32800 | tf_op jit(solution)/shard_map/ppermute | solution.py:453
  31.3 1.7 %collective-permute-done.11.refs_2_ = bf16[64,256]{1,0:T(8,128)(2,1)S(1)} collective-permute-done((bf16[64,256]{1,0:T(8,128)(2,1)S(1)}, bf16[64,256]{1,0:T(8,128)(2,1)S(1)}, u32[]{:S(2)}, u32[]{:S(2)}) %collective-permute-start.11) | collective-permute-done | bytes 32800 | tf_op jit(solution)/shard_map/ppermute | solution.py:453
  33.0 1.1 %collective-permute-start.13 = (bf16[256,256]{1,0:T(8,128)(2,1)S(1)}, bf16[256,256]{1,0:T(8,128)(2,1)}, u32[]{:S(2)}, u32[]{:S(2)}) collective-permute-start(bf16[256,256]{1,0:T(8,128)(2,1)S(1)} %assemble.1.grid_ref), channel_id=1, source_target_pairs={{0,24},{8,16},{16,8},{24,0},{1,25},{9,17},{17,9},{25,1},{2,26},{10... | collective-permute-start | bytes 393224 | tf_op jit(solution)/shard_map/ppermute | solution.py:453
  34.1 1.0 %collective-permute-start.14 = (bf16[256,256]{1,0:T(8,128)(2,1)S(1)}, bf16[256,256]{1,0:T(8,128)(2,1)S(1)}, u32[]{:S(2)}, u32[]{:S(2)}) collective-permute-start(bf16[256,256]{1,0:T(8,128)(2,1)S(1)} %assemble.1.grid_ref), channel_id=1, source_target_pairs={{0,8},{8,0},{16,24},{24,16},{1,9},{9,1},{17,25},{25,17},{2,10},{10... | collective-permute-start | bytes 393224 | tf_op jit(solution)/shard_map/ppermute | solution.py:453
  35.1 1.5 %collective-permute-start.15 = (bf16[256,256]{1,0:T(8,128)(2,1)S(1)}, bf16[256,256]{1,0:T(8,128)(2,1)S(1)}, u32[]{:S(2)}, u32[]{:S(2)}) collective-permute-start(bf16[256,256]{1,0:T(8,128)(2,1)S(1)} %assemble.1.grid_ref), channel_id=1, source_target_pairs={{0,16},{8,24},{16,0},{24,8},{1,17},{9,25},{17,1},{25,9},{2,18},{10... | collective-permute-start | bytes 393224 | tf_op jit(solution)/shard_map/ppermute | solution.py:453
  36.8 0.8 %diagonal.1.total_ref = f32[1024,256]{1,0:T(8,128)S(1)} custom-call(s32[16]{0:T(128)S(1)} %copy-done.1, bf16[1024,256]{1,0:T(8,128)(2,1)S(1)} %copy-done, f32[1024,1]{1,0:T(8,128)S(1)} %copy.10.row_ref, f32[1,256]{1,0:T(1,128)S(1)} %bitcast.3), custom_call_target="tpu_custom_call" | custom-call | tf_op jit(solution)/shard_map/diagonal/pallas_call | solution.py:395
  37.9 1.8 %collective-permute-done.13.grid_ref = bf16[256,256]{1,0:T(8,128)(2,1)} collective-permute-done((bf16[256,256]{1,0:T(8,128)(2,1)S(1)}, bf16[256,256]{1,0:T(8,128)(2,1)}, u32[]{:S(2)}, u32[]{:S(2)}) %collective-permute-start.13) | collective-permute-done | bytes 131104 | tf_op jit(solution)/shard_map/ppermute | solution.py:453
  39.7 1.2 %backward_more.4.total_ref = f32[1024,256]{1,0:T(8,128)S(1)} custom-call(f32[1024,256]{1,0:T(8,128)S(1)} %backward_more.3.total_ref, bf16[1024,1024]{1,0:T(8,128)(2,1)S(1)} %get-tuple-element.26.rolled_ref, bf16[256,256]{1,0:T(8,128)(2,1)} %collective-permute-done.13.grid_ref), custom_call_target="tpu_custom_call" | custom-call | flops 134217728 | bytes 3145728 | tf_op jit(solution)/shard_map/backward_more/pallas_call | solution.py:412
  41.3 1.2 %backward_end.1 = f32[1024,256]{1,0:T(8,128)} custom-call(f32[1024,256]{1,0:T(8,128)S(1)} %backward_more.5.total_ref, bf16[1024,1024]{1,0:T(8,128)(2,1)S(1)} %get-tuple-element.26.rolled_ref, bf16[256,256]{1,0:T(8,128)(2,1)S(1)} %collective-permute-done.15.grid_ref), custom_call_target="tpu_custom_call" | custom-call | flops 134217728 | bytes 4194304 | tf_op jit(solution)/shard_map/backward_end/pallas_call | solution.py:440
  (36 shorter events, 4.7 us)
Async XLA Ops:
  2.3 10.6 %collective-permute-start = (bf16[256,256]{1,0:T(8,128)(2,1)S(1)}, bf16[256,256]{1,0:T(8,128)(2,1)S(1)}, u32[]{:S(2)}, u32[]{:S(2)}) collective-permute-start(bf16[256,256]{1,0:T(8,128)(2,1)S(1)} %get-tuple-element.29), channel_id=1, source_target_pairs={{0,24},{8,16},{16,8},{24,0},{1,25},{9,17},{17,9},{25,1},{2,26},{10... | collective-permute-start | bytes 393224 | tf_op jit(solution)/shard_map/ppermute | solution.py:453
  6.7 6.2 %collective-permute-start.4 = (bf16[128,256]{1,0:T(8,128)(2,1)S(1)}, bf16[128,256]{1,0:T(8,128)(2,1)S(1)}, u32[]{:S(2)}, u32[]{:S(2)}) collective-permute-start(bf16[128,256]{1,0:T(8,128)(2,1)S(1)} %get-tuple-element.35), channel_id=1, source_target_pairs={{0,16},{8,24},{16,0},{24,8},{1,17},{9,25},{17,1},{25,9},{2,18},{10... | collective-permute-start | bytes 196616 | tf_op jit(solution)/shard_map/ppermute | solution.py:453
  7.6 5.3 %collective-permute-start.3 = (bf16[128,256]{1,0:T(8,128)(2,1)S(1)}, bf16[128,256]{1,0:T(8,128)(2,1)S(1)}, u32[]{:S(2)}, u32[]{:S(2)}) collective-permute-start(bf16[128,256]{1,0:T(8,128)(2,1)S(1)} %get-tuple-element.34), channel_id=1, source_target_pairs={{0,8},{8,0},{16,24},{24,16},{1,9},{9,1},{17,25},{25,17},{2,10},{10... | collective-permute-start | bytes 196616 | tf_op jit(solution)/shard_map/ppermute | solution.py:453
  7.8 9.2 %collective-permute-start.2 = (bf16[128,256]{1,0:T(8,128)(2,1)S(1)}, bf16[128,256]{1,0:T(8,128)(2,1)S(1)}, u32[]{:S(2)}, u32[]{:S(2)}) collective-permute-start(bf16[128,256]{1,0:T(8,128)(2,1)S(1)} %get-tuple-element.31), channel_id=1, source_target_pairs={{0,16},{8,24},{16,0},{24,8},{1,17},{9,25},{17,1},{25,9},{2,18},{10... | collective-permute-start | bytes 196616 | tf_op jit(solution)/shard_map/ppermute | solution.py:453
  9.7 7.3 %collective-permute-start.1 = (bf16[128,256]{1,0:T(8,128)(2,1)S(1)}, bf16[128,256]{1,0:T(8,128)(2,1)S(1)}, u32[]{:S(2)}, u32[]{:S(2)}) collective-permute-start(bf16[128,256]{1,0:T(8,128)(2,1)S(1)} %get-tuple-element.30), channel_id=1, source_target_pairs={{0,8},{8,0},{16,24},{24,16},{1,9},{9,1},{17,25},{25,17},{2,10},{10... | collective-permute-start | bytes 196616 | tf_op jit(solution)/shard_map/ppermute | solution.py:453
  13.0 5.2 %collective-permute-start.5 = (bf16[64,256]{1,0:T(8,128)(2,1)S(1)}, bf16[64,256]{1,0:T(8,128)(2,1)S(1)}, u32[]{:S(2)}, u32[]{:S(2)}) collective-permute-start(bf16[64,256]{1,0:T(8,128)(2,1)S(1)} %get-tuple-element.36), channel_id=1, source_target_pairs={{0,4},{1,5},{2,6},{3,7},{4,0},{5,1},{6,2},{7,3},{8,12},{9,13},{10,... | collective-permute-start | bytes 98312 | tf_op jit(solution)/shard_map/ppermute | solution.py:453
  15.6 5.7 %collective-permute-start.6 = (bf16[64,256]{1,0:T(8,128)(2,1)S(1)}, bf16[64,256]{1,0:T(8,128)(2,1)S(1)}, u32[]{:S(2)}, u32[]{:S(2)}) collective-permute-start(bf16[64,256]{1,0:T(8,128)(2,1)S(1)} %get-tuple-element.38), channel_id=1, source_target_pairs={{0,6},{1,7},{2,4},{3,5},{4,2},{5,3},{6,0},{7,1},{8,14},{9,15},{10,... | collective-permute-start | bytes 98312 | tf_op jit(solution)/shard_map/ppermute | solution.py:453
  17.0 4.6 %collective-permute-start.7 = (bf16[64,256]{1,0:T(8,128)(2,1)S(1)}, bf16[64,256]{1,0:T(8,128)(2,1)S(1)}, u32[]{:S(2)}, u32[]{:S(2)}) collective-permute-start(bf16[64,256]{1,0:T(8,128)(2,1)S(1)} %get-tuple-element.39), channel_id=1, source_target_pairs={{0,2},{1,3},{2,0},{3,1},{4,6},{5,7},{6,4},{7,5},{8,10},{9,11},{10,... | collective-permute-start | bytes 98312 | tf_op jit(solution)/shard_map/ppermute | solution.py:453
  22.0 1.6 %collective-permute-start.8 = (f32[32,2048]{1,0:T(8,128)S(1)}, f32[32,2048]{1,0:T(8,128)S(1)}, u32[]{:S(2)}, u32[]{:S(2)}) collective-permute-start(f32[32,2048]{1,0:T(8,128)S(1)} %get-tuple-element.41), channel_id=1, source_target_pairs={{0,1},{1,0},{2,3},{3,2},{4,5},{5,4},{6,7},{7,6},{8,9},{9,8},{10,11... | collective-permute-start | bytes 786440 | tf_op jit(solution)/shard_map/ppermute | solution.py:453
  23.6 1.4 %collective-permute-start.9 = (bf16[32,2048]{1,0:T(8,128)(2,1)S(1)}, bf16[32,2048]{1,0:T(8,128)(2,1)S(1)}, u32[]{:S(2)}, u32[]{:S(2)}) collective-permute-start(bf16[32,2048]{1,0:T(8,128)(2,1)S(1)} %act.1.mine_ref), channel_id=1, source_target_pairs={{0,1},{1,0},{2,3},{3,2},{4,5},{5,4},{6,7},{7,6},{8,9},{9,8},{10,11... | collective-permute-start | bytes 393224 | tf_op jit(solution)/shard_map/ppermute | solution.py:453
  26.1 10.4 %copy-start.3 = (f32[1024]{0:T(1024)S(1)}, f32[1024]{0:T(1024)}, u32[]{:S(2)}) copy-start(f32[1024]{0:T(1024)} %param.10) | copy-start | bytes 12292
  26.1 10.7 %copy-start = (bf16[1024,256]{1,0:T(8,128)(2,1)S(1)}, bf16[1024,256]{1,0:T(8,128)(2,1)}, u32[]{:S(2)}) copy-start(bf16[1024,256]{1,0:T(8,128)(2,1)} %coeff_hbm.1) | copy-start | bytes 1572868
  26.1 10.7 %copy-start.1 = (s32[16]{0:T(128)S(1)}, s32[16]{0:T(128)}, u32[]{:S(2)}) copy-start(s32[16]{0:T(128)} %pad_hbm.1) | copy-start | bytes 196
  26.2 10.7 %copy-start.2 = (f32[256]{0:T(256)S(1)}, f32[256]{0:T(256)}, u32[]{:S(2)}) copy-start(f32[256]{0:T(256)} %param.11) | copy-start | bytes 3076
  26.2 5.1 %collective-permute-start.10 = (bf16[64,256]{1,0:T(8,128)(2,1)S(1)}, bf16[64,256]{1,0:T(8,128)(2,1)S(1)}, u32[]{:S(2)}, u32[]{:S(2)}) collective-permute-start(bf16[64,256]{1,0:T(8,128)(2,1)S(1)} %get-tuple-element.44), channel_id=1, source_target_pairs={{0,4},{1,5},{2,6},{3,7},{4,0},{5,1},{6,2},{7,3},{8,12},{9,13},{10,... | collective-permute-start | bytes 98312 | tf_op jit(solution)/shard_map/ppermute | solution.py:453
  27.3 5.7 %collective-permute-start.11 = (bf16[64,256]{1,0:T(8,128)(2,1)S(1)}, bf16[64,256]{1,0:T(8,128)(2,1)S(1)}, u32[]{:S(2)}, u32[]{:S(2)}) collective-permute-start(bf16[64,256]{1,0:T(8,128)(2,1)S(1)} %get-tuple-element.45), channel_id=1, source_target_pairs={{0,6},{1,7},{2,4},{3,5},{4,2},{5,3},{6,0},{7,1},{8,14},{9,15},{10,... | collective-permute-start | bytes 98312 | tf_op jit(solution)/shard_map/ppermute | solution.py:453
  28.4 4.6 %collective-permute-start.12 = (bf16[64,256]{1,0:T(8,128)(2,1)S(1)}, bf16[64,256]{1,0:T(8,128)(2,1)S(1)}, u32[]{:S(2)}, u32[]{:S(2)}) collective-permute-start(bf16[64,256]{1,0:T(8,128)(2,1)S(1)} %get-tuple-element.46), channel_id=1, source_target_pairs={{0,2},{1,3},{2,0},{3,1},{4,6},{5,7},{6,4},{7,5},{8,10},{9,11},{10,... | collective-permute-start | bytes 98312 | tf_op jit(solution)/shard_map/ppermute | solution.py:453
  33.0 6.7 %collective-permute-start.13 = (bf16[256,256]{1,0:T(8,128)(2,1)S(1)}, bf16[256,256]{1,0:T(8,128)(2,1)}, u32[]{:S(2)}, u32[]{:S(2)}) collective-permute-start(bf16[256,256]{1,0:T(8,128)(2,1)S(1)} %assemble.1.grid_ref), channel_id=1, source_target_pairs={{0,24},{8,16},{16,8},{24,0},{1,25},{9,17},{17,9},{25,1},{2,26},{10... | collective-permute-start | bytes 393224 | tf_op jit(solution)/shard_map/ppermute | solution.py:453
  34.1 6.8 %collective-permute-start.14 = (bf16[256,256]{1,0:T(8,128)(2,1)S(1)}, bf16[256,256]{1,0:T(8,128)(2,1)S(1)}, u32[]{:S(2)}, u32[]{:S(2)}) collective-permute-start(bf16[256,256]{1,0:T(8,128)(2,1)S(1)} %assemble.1.grid_ref), channel_id=1, source_target_pairs={{0,8},{8,0},{16,24},{24,16},{1,9},{9,1},{17,25},{25,17},{2,10},{10... | collective-permute-start | bytes 393224 | tf_op jit(solution)/shard_map/ppermute | solution.py:453
  35.1 6.2 %collective-permute-start.15 = (bf16[256,256]{1,0:T(8,128)(2,1)S(1)}, bf16[256,256]{1,0:T(8,128)(2,1)S(1)}, u32[]{:S(2)}, u32[]{:S(2)}) collective-permute-start(bf16[256,256]{1,0:T(8,128)(2,1)S(1)} %assemble.1.grid_ref), channel_id=1, source_target_pairs={{0,16},{8,24},{16,0},{24,8},{1,17},{9,25},{17,1},{25,9},{2,18},{10... | collective-permute-start | bytes 393224 | tf_op jit(solution)/shard_map/ppermute | solution.py:453
